TPU v7x, 32 devices: a whole 2x2x4 slice. The times are simulated.
32 devices in a mesh: rep: 2 (over y), dp: 4 (over z), tp: 4 (over x, core).
Axes of the slice: x: 2, y: 2, z: 4, core: 2. Of those that a mesh axis runs over, the one named last changes fastest.
Arguments:
- hidden: bfloat16 [4, 512, 8192], P(None, ('rep', 'dp'), 'tp'), parts along dimension 1, may hold values from -6 to 6
- queries: bfloat16 [4, 512, 8192], P(None, ('rep', 'dp'), 'tp'), parts along dimension 1, may hold values from -8 to 8
- projection: bfloat16 [8192, 2048], P('tp'), may hold values from -0.0625 to 0.0625
- cached_key_rows: bfloat16 [512, 8, 128, 128], P(('rep', 'dp'), 'tp'), parts along dimension 0, may hold values from -8 to 8
- cached_value_rows: bfloat16 [512, 8, 128, 128], P(('rep', 'dp'), 'tp'), parts along dimension 0, may hold values from -6 to 6
- adapter_shrink_weight: bfloat16 [128, 16, 8192], P('dp', None, 'tp'), may hold values from -0.0625 to 0.0625
- adapter_expand_weight: bfloat16 [128, 16, 2048], P('dp', None, 'tp'), may hold values from -1.5 to 1.5
- requests: int32 [512], P(('rep', 'dp')), parts along dimension 0, may hold values from 0 to 127, as said below
- adapter_store_row: int32 [256], P('rep'), parts along dimension 0, may hold values from 0 to 127, as said below
- lengths: int32 [512], P(('rep', 'dp')), parts along dimension 0, may hold values from 2 to 128, as said below
Outputs:
- attended: bfloat16 [4, 512, 8192], P(None, ('rep', 'dp'), 'tp'), parts along dimension 1
- new_key_value: bfloat16 [4, 512, 2048], P(None, ('rep', 'dp'), 'tp'), parts along dimension 1
There are 2 independent parts, one for each index of `rep`. A program takes and returns all parts, laid end to end along the dimension named above; an argument that names none is the same for every part. Nothing has to cross between parts.
Inputs may be any that keep to these rules, and one draw needn't show every extreme that they name: `requests`: in the block of 64 sequences of each dp index, at most 16 sequences use adapters whose store rows lie in any one dp index's block of 32 rows, and in every draw one such block serves exactly 16 sequences of every dp index. `adapter_store_row`: A permutation: every store row holds exactly one adapter. `lengths`: some sequence uses all 128 positions in every draw.
All inputs are finite; a program needn't handle non-finite values.
Results may differ from a plain program's by a relative error of at most 0.006.
Values may be sent and summed in bfloat16 or wider, within the bound.
No kernel may reach another device: no remote copies, remote signals or barrier semaphores. Data moves between devices by JAX's collectives and lax.ppermute only.
A program may use at most 128 MiB of HBM per device.

v0:
```python
import math

import jax
import jax.numpy as jnp
from jax import lax
from jax.sharding import PartitionSpec as P

adapter_scale = 0.5


def attend(query_heads, cached_key_rows, cached_value_rows, fresh_keys, fresh_values, lengths):
    step_count = query_heads.shape[0]
    scaling = 1.0 / math.sqrt(query_heads.shape[-1])
    past = (
        jnp.einsum(
            "sbhgd,bhpd->sbhgp", query_heads, cached_key_rows, preferred_element_type=jnp.float32
        )
        * scaling
    )
    fresh = (
        jnp.einsum("sbhgd,tbhd->sbhgt", query_heads, fresh_keys, preferred_element_type=jnp.float32)
        * scaling
    )
    live = jnp.arange(cached_key_rows.shape[2], dtype=jnp.int32)[None, :] < lengths[:, None]
    past = jnp.where(live[None, :, None, None, :], past, -jnp.inf)
    causal = jnp.arange(step_count)[None, :] <= jnp.arange(step_count)[:, None]
    fresh = jnp.where(causal[:, None, None, None, :], fresh, -jnp.inf)
    highest = jnp.maximum(jnp.max(past, axis=-1), jnp.max(fresh, axis=-1))[..., None]
    past_exp = jnp.exp(past - highest)
    fresh_exp = jnp.exp(fresh - highest)
    total = jnp.sum(past_exp, axis=-1, keepdims=True) + jnp.sum(fresh_exp, axis=-1, keepdims=True)
    past_weights = (past_exp / total).astype(jnp.bfloat16)
    fresh_weights = (fresh_exp / total).astype(jnp.bfloat16)
    mixed = jnp.einsum(
        "sbhgp,bhpd->sbhgd", past_weights, cached_value_rows, preferred_element_type=jnp.float32
    )
    mixed = mixed + jnp.einsum(
        "sbhgt,tbhd->sbhgd", fresh_weights, fresh_values, preferred_element_type=jnp.float32
    )
    return mixed.astype(jnp.bfloat16)


def body(
    hidden,
    queries,
    projection,
    cached_key_rows,
    cached_value_rows,
    adapter_shrink_weight,
    adapter_expand_weight,
    requests,
    adapter_store_row,
    lengths,
):
    step_count, seq_count, feature_count = hidden.shape
    groups = lax.axis_size("dp")
    capacity = seq_count // 4
    stored_entries = adapter_shrink_weight.shape[0]
    rank_total = adapter_shrink_weight.shape[1]
    local_heads = cached_key_rows.shape[1]
    head_size = cached_key_rows.shape[3]
    column_total = adapter_expand_weight.shape[2]
    partial_value = jnp.dot(
        hidden.reshape(step_count * seq_count, feature_count),
        projection,
        preferred_element_type=jnp.float32,
    )
    base = lax.psum_scatter(partial_value, "tp", scatter_dimension=1, tiled=True).reshape(
        step_count, seq_count, column_total
    )
    matches = requests[:, None] == jnp.arange(adapter_store_row.shape[0], dtype=jnp.int32)[None, :]
    store_rows = jnp.sum(jnp.where(matches, adapter_store_row[None, :], 0), axis=1)
    owners = store_rows // stored_entries
    slots = store_rows % stored_entries
    positions = jnp.arange(seq_count, dtype=jnp.int32)
    earlier = (owners[:, None] == owners[None, :]) & (positions[None, :] < positions[:, None])
    buckets = owners * capacity + jnp.sum(earlier, axis=1)
    placed = buckets[None, :] == jnp.arange(groups * capacity, dtype=jnp.int32)[:, None]
    placed_bf = placed.astype(jnp.bfloat16)
    bucket_slots = jnp.sum(jnp.where(placed, slots[None, :], 0), axis=1).reshape(groups, capacity)
    selected_entries = (
        lax.all_to_all(bucket_slots, "dp", split_axis=0, concat_axis=0, tiled=True)[..., None]
        == jnp.arange(stored_entries, dtype=jnp.int32)[None, None, :]
    ).astype(jnp.bfloat16)
    shrink_factor_rows = jnp.einsum(
        "wsj,jqb->wsqb", selected_entries, adapter_shrink_weight, preferred_element_type=jnp.float32
    ).astype(jnp.bfloat16)
    expand_factor_rows = jnp.einsum(
        "ymu,usx->ymsx", selected_entries, adapter_expand_weight, preferred_element_type=jnp.float32
    ).astype(jnp.bfloat16)
    got_down, got_up = (
        lax.all_to_all(shrink_factor_rows, "dp", split_axis=0, concat_axis=0, tiled=True),
        lax.all_to_all(expand_factor_rows, "dp", split_axis=0, concat_axis=0, tiled=True),
    )
    seq_down = jnp.einsum(
        "bq,brd->qrd",
        placed_bf,
        got_down.reshape(groups * capacity, rank_total, feature_count),
        preferred_element_type=jnp.float32,
    ).astype(jnp.bfloat16)
    sequence_expand = jnp.einsum(
        "bq,brk->qrk",
        placed_bf,
        got_up.reshape(groups * capacity, rank_total, column_total),
        preferred_element_type=jnp.float32,
    ).astype(jnp.bfloat16)
    shrunken_input = jnp.einsum(
        "sqd,qrd->sqr", hidden, seq_down, preferred_element_type=jnp.float32
    )
    summed_output = lax.psum(shrunken_input, "tp").astype(jnp.bfloat16)
    adapter_update = (
        adapter_scale
        * jnp.einsum(
            "cmx,mxp->cmp", summed_output, sequence_expand, preferred_element_type=jnp.float32
        )
    ).astype(jnp.bfloat16)
    key_value = (base + adapter_update.astype(jnp.float32)).astype(jnp.bfloat16)
    paired = key_value.reshape(step_count, seq_count, local_heads, 2, head_size)
    query_heads = queries.reshape(step_count, seq_count, local_heads, -1, head_size)
    mixed = attend(
        query_heads,
        cached_key_rows,
        cached_value_rows,
        paired[:, :, :, 0],
        paired[:, :, :, 1],
        lengths,
    )
    return (mixed.reshape(step_count, seq_count, -1), key_value)


def solution(mesh):
    placed = (
        P(None, ("rep", "dp"), "tp"),
        P(None, ("rep", "dp"), "tp"),
        P("tp", None),
        P(("rep", "dp"), "tp", None, None),
        P(("rep", "dp"), "tp", None, None),
        P("dp", None, "tp"),
        P("dp", None, "tp"),
        P(("rep", "dp")),
        P("rep"),
        P(("rep", "dp")),
    )
    return jax.shard_map(
        body,
        mesh=mesh,
        in_specs=placed,
        out_specs=(P(None, ("rep", "dp"), "tp"), P(None, ("rep", "dp"), "tp")),
        check_vma=False,
    )
```

profile of v0, /device:TPU:0, one launch (start us, length us, event | category | flops | bytes accessed | tf_op | source)
XLA Modules:
  0.0 201.2 jit_solution(11699068000879091762)
XLA Ops:
  7.2 0.0 copy-start
  7.2 0.9 select_reduce_fusion.1
  8.1 0.2 convert_reduce_fusion
  8.3 0.1 select_reduce_fusion
  8.4 0.1 all_to_all.12
  8.5 11.7 %all_to_all.19 = s32[4,1,16]{2,1,0:T(1,128)S(1)} all-to-all(s32[4,1,16]{2,1,0:T(1,128)S(1)} %bitcast.97), channel_id=1, replica_groups=mesh['rep'=2,'dp'=4,'tp'=4] {'dp'}, dimensions={0} | all-to-all | bytes 512 | tf_op jit(solution)/shard_map/all_to_all | solution.py:82
  20.2 2.5 %convolution_convert_fusion.1 = bf16[4,16,16,512]{3,1,2,0:T(8,128)(2,1)} fusion(bf16[32,16,512]{2,1,0:T(8,128)(2,1)} %param.16, s32[4,16]{1,0:T(4,128)S(1)} %bitcast.95), kind=kOutput, calls=%fused_computation.20 | convolution fusion | flops 34080768 | bytes 1573120 | tf_op jit(solution)/shard_map/ymu,usx->ymsx/dot_general | solution.py:88
  22.7 3.5 %all-to-all-start.1 = ((bf16[4,16,16,512]{3,1,2,0:T(8,128)(2,1)}), bf16[4,16,16,512]{3,1,2,0:T(8,128)(2,1)S(1)}, u32[]{:S(2)}, u32[]{:S(2)}) async-start(bf16[4,16,16,512]{3,1,2,0:T(8,128)(2,1)} %convolution_convert_fusion.1), calls=%async_computation.2 | async-start | bytes 2097152 | tf_op jit(solution)/shard_map/all_to_all | solution.py:93
  26.2 6.8 %convolution_convert_fusion = bf16[4,16,16,2048]{3,1,2,0:T(8,128)(2,1)} fusion(bf16[32,16,2048]{2,1,0:T(8,128)(2,1)} %param.15, s32[4,16]{1,0:T(4,128)S(1)} %bitcast.96), kind=kOutput, calls=%fused_computation.9 | convolution fusion | flops 136316928 | bytes 6291712 | tf_op jit(solution)/shard_map/wsj,jqb->wsqb/dot_general | solution.py:85
  33.0 17.8 %all-to-all-done.1 = bf16[4,16,16,512]{3,1,2,0:T(8,128)(2,1)S(1)} async-done(((bf16[4,16,16,512]{3,1,2,0:T(8,128)(2,1)}), bf16[4,16,16,512]{3,1,2,0:T(8,128)(2,1)S(1)}, u32[]{:S(2)}, u32[]{:S(2)}) %all-to-all-start.1) | async-done | bytes 1048608 | tf_op jit(solution)/shard_map/all_to_all | solution.py:93
  50.8 0.0 copy-start.1
  50.8 1.0 copy-done.1
  51.7 4.8 %all-to-all-start.2 = ((bf16[4,16,16,2048]{3,1,2,0:T(8,128)(2,1)}), bf16[4,16,16,2048]{3,1,2,0:T(8,128)(2,1)}, u32[]{:S(2)}, u32[]{:S(2)}) async-start(bf16[4,16,16,2048]{3,1,2,0:T(8,128)(2,1)} %convolution_convert_fusion), calls=%async_computation.3 | async-start | bytes 8388608 | tf_op jit(solution)/shard_map/all_to_all | solution.py:92
  56.6 0.2 reduce-scatter.2.cloned.1.call-start
  56.8 0.0 copy-done
  56.8 7.1 %fusion.60 = f32[256,2048]{1,0:T(8,128)} fusion(bf16[256,2048]{1,0:T(8,128)(2,1)S(1)} %bitcast.89, bf16[2048,2048]{1,0:T(8,128)(2,1)} %param.12), kind=kOutput, calls=%fused_computation.79 | convolution fusion | flops 2147483648 | bytes 11534336 | tf_op jit(solution)/shard_map/dot_general | solution.py:63
  63.9 0.0 copy-start.5
  63.9 0.0 copy-start.6
  64.0 0.0 reduce-scatter.2.cloned.1.call-update
  64.0 1.2 copy-done.5
  65.2 0.2 copy.72
  65.4 0.0 copy-start.3
  65.4 0.0 copy-done.6
  65.4 0.1 iota_compare_fusion.4
  65.5 0.0 copy-start.2
  65.5 5.6 %bitcast_reduce_fusion = (f32[4,64,2,8]{3,0,2,1:T(4,128)}, f32[64,2,128,4,8]{2,4,3,1,0:T(8,128)S(1)}) fusion(pred[64,128]{1,0:T(8,128)(4,1)S(1)} %iota_compare_fusion.4, bf16[4,64,2,8,128]{4,3,2,1,0:T(8,128)(2,1)S(1)} %bitcast.92, bf16[64,2,128,128]{3,2,1,0:T(8,128)(2,1)} %param.13), kind=kOutput, calls=%fused_computation.14 | convolution fusion | flops 135786496 | bytes 7364608 | tf_op jit(solution)/shard_map/sbhgd,bhpd->sbhgp/dot_general | solution.py:15
  71.2 0.0 copy-done.3
  71.2 0.0 copy-done.2
  71.2 0.6 copy.51
  71.7 2.4 %convolution_convert_fusion.2 = bf16[64,16,512]{2,0,1:T(8,128)(2,1)} fusion(bf16[64,16,512]{2,1,0:T(8,128)(2,1)S(1)} %bitcast.91, s32[64]{0:T(128)S(1)} %multiply_add_fusion), kind=kOutput, calls=%fused_computation.21 | convolution fusion | flops 67637248 | bytes 2097408 | tf_op jit(solution)/shard_map/bq,brk->qrk/dot_general | solution.py:101
  74.2 75.1 %all-to-all-done.2 = bf16[4,16,16,2048]{3,1,2,0:T(8,128)(2,1)} async-done(((bf16[4,16,16,2048]{3,1,2,0:T(8,128)(2,1)}), bf16[4,16,16,2048]{3,1,2,0:T(8,128)(2,1)}, u32[]{:S(2)}, u32[]{:S(2)}) %all-to-all-start.2) | async-done | bytes 4194336 | tf_op jit(solution)/shard_map/all_to_all | solution.py:92
  149.3 4.5 %copy.54 = bf16[4,16,16,2048]{3,2,1,0:T(8,128)(2,1)S(1)} copy(bf16[4,16,16,2048]{3,1,2,0:T(8,128)(2,1)} %all-to-all-done.2) | data formatting | bytes 8388608 | tf_op jit(solution)/shard_map/all_to_all | solution.py:92
  153.8 5.8 %fusion.8 = bf16[64,16,2048]{2,0,1:T(8,128)(2,1)S(1)} fusion(bf16[64,16,2048]{2,1,0:T(8,128)(2,1)S(1)} %bitcast.90, s32[64]{0:T(128)S(1)} %multiply_add_fusion), kind=kOutput, calls=%fused_computation.8 | convolution fusion | flops 270536704 | bytes 8388864 | tf_op jit(solution)/shard_map/bq,brd->qrd/dot_general | solution.py:95
  159.5 2.8 %fusion.25 = f32[4,64,16]{2,0,1:T(4,128)S(1)} fusion(bf16[64,16,2048]{2,0,1:T(8,128)(2,1)S(1)} %fusion.8, bf16[4,64,2048]{2,1,0:T(8,128)(2,1)S(1)} %copy-done), kind=kOutput, calls=%fused_computation.31 | convolution fusion | flops 16777216 | bytes 5259264 | tf_op jit(solution)/shard_map/sqd,qrd->sqr/dot_general | solution.py:107
  162.4 11.6 %psum.7 = bf16[4,64,16]{2,0,1:T(4,128)(2,1)S(1)} all-reduce(f32[4,64,16]{2,0,1:T(4,128)S(1)} %fusion.25), channel_id=1, replica_groups=mesh['rep'=2,'dp'=4,'tp'=4] {'tp'}, use_global_device_ids=true, to_apply=%region_5.6 | all-reduce | flops 4096 | bytes 24576 | tf_op jit(solution)/shard_map/psum | solution.py:110
  174.0 0.0 reduce-scatter.2.cloned.1.call-done
  174.0 3.0 %fusion.24 = bf16[4,64,512]{2,0,1:T(4,128)(2,1)} fusion(bf16[64,16,512]{2,0,1:T(8,128)(2,1)} %convolution_convert_fusion.2, f32[4,64,512]{2,1,0:T(8,128)} %bitcast.98, bf16[4,64,16]{2,0,1:T(4,128)(2,1)S(1)} %psum.7), kind=kOutput, calls=%fused_computation.30 | convolution fusion | flops 4849664 | bytes 1843200 | tf_op jit(solution)/shard_map/cmx,mxp->cmp/dot_general | solution.py:113
  177.0 1.1 reshape.131
  178.0 1.7 copy.64
  179.7 0.0 copy-start.4
  179.7 0.4 fusion.58
  180.1 6.0 %fusion.59 = (f32[4,64,2,8]{3,0,2,1:T(4,128)S(1)}, f32[4,64,2,8,4]{3,4,0,2,1:T(4,128)S(1)}) fusion(bf16[4,64,2,8,128]{4,3,2,1,0:T(8,128)(2,1)} %bitcast.93, bf16[4,64,2,1,128]{4,3,2,0,1:T(2,128)(2,1)S(1)} %get-tuple-element.11, pred[4,4]{1,0:T(4,128)(4,1)S(1)} %iota_compare_fusion.5), kind=kOutput, calls=%fused_computation.78 | convolution fusion | flops 4239360 | bytes 1261584 | tf_op jit(solution)/shard_map/sbhgd,tbhd->sbhgt/dot_general | solution.py:21
  186.1 0.0 copy-done.4
  186.2 0.1 max.7
  186.2 1.0 fusion.38
  187.2 1.4 fusion.17
  188.6 0.1 add.50
  188.7 0.0 copy-start.7
  188.7 0.8 fusion.39
  189.5 1.4 copy-done.7
  190.9 1.9 fusion.11
  192.8 0.2 copy.63
  193.0 1.3 reshape.132
  (3 shorter events, 0.0 us)
Async XLA Ops:
  7.2 49.7 %copy-start = (bf16[4,64,2048]{2,1,0:T(8,128)(2,1)S(1)}, bf16[4,64,2048]{2,1,0:T(8,128)(2,1)}, u32[]{:S(2)}) copy-start(bf16[4,64,2048]{2,1,0:T(8,128)(2,1)} %param.10) | copy-start | bytes 3145732
  22.7 28.1 %all-to-all-start.1 = ((bf16[4,16,16,512]{3,1,2,0:T(8,128)(2,1)}), bf16[4,16,16,512]{3,1,2,0:T(8,128)(2,1)S(1)}, u32[]{:S(2)}, u32[]{:S(2)}) async-start(bf16[4,16,16,512]{3,1,2,0:T(8,128)(2,1)} %convolution_convert_fusion.1), calls=%async_computation.2 | async-start | bytes 2097152 | tf_op jit(solution)/shard_map/all_to_all | solution.py:93
  50.8 1.0 copy-start.1
  51.7 97.5 %all-to-all-start.2 = ((bf16[4,16,16,2048]{3,1,2,0:T(8,128)(2,1)}), bf16[4,16,16,2048]{3,1,2,0:T(8,128)(2,1)}, u32[]{:S(2)}, u32[]{:S(2)}) async-start(bf16[4,16,16,2048]{3,1,2,0:T(8,128)(2,1)} %convolution_convert_fusion), calls=%async_computation.3 | async-start | bytes 8388608 | tf_op jit(solution)/shard_map/all_to_all | solution.py:92
  56.6 117.4 %reduce-scatter.2.cloned.1.call-start = ((), (), s32[]{:S(2)}) async-start(), calls=%async_computation.4 | async-start | bytes 2621440 | tf_op jit(solution)/shard_map/reduce_scatter | solution.py:68
  63.9 1.2 copy-start.5
  63.9 1.5 copy-start.6
  65.4 5.8 %copy-start.3 = (bf16[32,8,16,128]{3,2,1,0:T(8,128)(2,1)}, bf16[32,8,16,128]{3,2,1,0:T(8,128)(2,1)S(1)}, u32[]{:S(2)}) copy-start(bf16[32,8,16,128]{3,2,1,0:T(8,128)(2,1)S(1)} %copy.72) | copy-start | bytes 3145732
  65.5 5.6 %copy-start.2 = (bf16[4,16,16,512]{3,1,2,0:T(8,128)(2,1)S(1)}, bf16[4,16,16,512]{3,1,2,0:T(8,128)(2,1)}, u32[]{:S(2)}) copy-start(bf16[4,16,16,512]{3,1,2,0:T(8,128)(2,1)} %copy-done.1) | copy-start | bytes 3145732
  179.7 6.4 %copy-start.4 = (f32[4,64,2,8]{3,0,2,1:T(4,128)S(1)}, f32[4,64,2,8]{3,0,2,1:T(4,128)}, u32[]{:S(2)}) copy-start(f32[4,64,2,8]{3,0,2,1:T(4,128)} %get-tuple-element.14) | copy-start | bytes 49156
  188.7 2.2 %copy-start.7 = (bf16[64,2,128,128]{3,2,1,0:T(8,128)(2,1)S(1)}, bf16[64,2,128,128]{3,2,1,0:T(8,128)(2,1)}, u32[]{:S(2)}) copy-start(bf16[64,2,128,128]{3,2,1,0:T(8,128)(2,1)} %param.14) | copy-start | bytes 12582916
Sparse Core Ops, SparseCore 0:
  64.1 32.6 reduce-scatter.1
where the time goes:
time: 202 us; the launch traced here: 201 us
  waiting for transfers between devices  92.9 us (46%)
  matrix products  44.8 us (22%)
  blocking collectives  23.3 us (12%)
  between operations  14.2 us (7%)
  local copies, waits for them, and re-layouts  13.5 us (7%)
  starting transfers between devices  8.58 us (4%)
  other arithmetic  3.85 us (2%)
    all_to_all x1, waiting for transfers between devices, body(): lax.all_to_all(shrink_factor_rows, 'dp', split_axis=0, concat_axis=0, til...  75.1 us
    all_to_all x1, waiting for transfers between devices, body(): lax.all_to_all(expand_factor_rows, 'dp', split_axis=0, concat_axis=0, til...  17.8 us
    all_to_all x1, blocking collectives, body(): lax.all_to_all(bucket_slots, 'dp', split_axis=0, concat_axis=0, tiled=True)  11.7 us
    psum x1, blocking collectives, body(): summed_output = lax.psum(shrunken_input, 'tp').astype(jnp.bfloat16)  11.6 us
    dot_general x1, matrix products, body(): jnp.dot(hidden.reshape(step_count * seq_count, feature_count), projection...  7.11 us
    dot_general x1, matrix products, body(): jnp.einsum('wsj,jqb->wsqb', selected_entries, adapter_shrink_weight, pref...  6.77 us
    dot_general x1, matrix products, attend(): jnp.einsum('sbhgd,tbhd->sbhgt', query_heads, fresh_keys, preferred_elemen...  6.02 us
    dot_general x1, matrix products, body(): jnp.einsum('bq,brd->qrd', placed_bf, got_down.reshape(groups * capacity,...  5.77 us
  transfers between devices with their start and end apart: 3, of which 2 were waited for; matrix products, arithmetic and copies ran while one was open for 18% of the time, Pallas kernels for 0%

commit v1 on v0

v1 whole, which is shorter than its diff:
```python
import functools
import math

import jax
import jax.numpy as jnp
from jax import lax
from jax.experimental import pallas as pl
from jax.experimental.pallas import tpu as pltpu
from jax.sharding import PartitionSpec as P

adapter_scale = 0.5
F32 = jnp.float32
BF16 = jnp.bfloat16
NT = (((1,), (1,)), ((), ()))
TN = (((0,), (0,)), ((), ()))
MIB = 1024 * 1024


def params(mib=40, **kw):
    return pltpu.CompilerParams(vmem_limit_bytes=mib * MIB, **kw)


def cost(flops, nbytes, transcendentals=0):
    return pl.CostEstimate(
        flops=int(flops), bytes_accessed=int(nbytes), transcendentals=int(transcendentals)
    )


def swap(axis, size, distance):
    pairs = [(i, i ^ distance) for i in range(size)]
    return lambda value: lax.ppermute(value, axis, pairs)


def iota(shape, dim):
    return lax.broadcasted_iota(jnp.int32, shape, dim)


def column(row):
    size = row.shape[1]
    diagonal = iota((size, size), 0) == iota((size, size), 1)
    return jnp.sum(jnp.where(diagonal, row, 0.0), axis=1, keepdims=True)


def route_kernel(groups, cap, entries, requests_ref, store_ref, hidden_ref, *outs):
    blocks, slots, back_ref = outs[:groups], outs[groups : 2 * groups], outs[2 * groups]
    steps, seqs, _ = hidden_ref.shape
    me = lax.axis_index("dp")
    store_col = column(store_ref[...].astype(F32))
    adapters = store_col.shape[0]
    rows = jnp.sum(
        jnp.where(iota((adapters, seqs), 0) == requests_ref[...], store_col, 0.0),
        axis=0,
        keepdims=True,
    ).astype(jnp.int32)
    owner = lax.div(rows, jnp.int32(entries))
    slot_col = column((rows - owner * entries).astype(F32))
    distance = jnp.bitwise_xor(owner, me).astype(F32)
    distance_col = column(distance)
    before = (distance_col == distance) & (iota((seqs, seqs), 0) < iota((seqs, seqs), 1))
    rank = jnp.sum(jnp.where(before, 1.0, 0.0), axis=0, keepdims=True)
    bucket = distance * cap + rank
    bucket_col = column(bucket).astype(jnp.int32)
    bucket = bucket.astype(jnp.int32)
    placed = jnp.where(iota((groups * cap, seqs), 0) == bucket, 1.0, 0.0).astype(BF16)
    back_ref[...] = jnp.where(bucket_col == iota((seqs, groups * cap), 1), 1.0, 0.0).astype(BF16)
    for k in range(groups):
        spot = lax.rem(iota((seqs, steps * cap), 1), jnp.int32(cap)) + k * cap
        slots[k][...] = jnp.sum(
            jnp.where(bucket_col == spot, slot_col, 0.0), axis=0, keepdims=True
        ).astype(jnp.int32)
    for s in range(steps):
        picked = jnp.dot(placed, hidden_ref[s], preferred_element_type=F32).astype(BF16)
        for k in range(groups):
            blocks[k][s * cap : (s + 1) * cap, :] = picked[k * cap : (k + 1) * cap, :]


def route(requests, store, hidden, groups, cap, entries):
    steps, seqs, features = hidden.shape
    rows = steps * cap
    return pl.pallas_call(
        functools.partial(route_kernel, groups, cap, entries),
        out_shape=[jax.ShapeDtypeStruct((rows, features), BF16)] * groups
        + [jax.ShapeDtypeStruct((1, rows), jnp.int32)] * groups
        + [jax.ShapeDtypeStruct((seqs, groups * cap), BF16)],
        compiler_params=params(),
        cost_estimate=cost(
            2 * groups * cap * seqs * steps * features, 4 * steps * seqs * features
        ),
        name="route",
    )(requests[None, :], store[None, :], hidden)


def base_kernel(tp_ref, hidden_ref, projection_ref, out_ref):
    out_ref[0] = jnp.dot(hidden_ref[...], projection_ref[...], preferred_element_type=F32)


def base_part(tp_index, hidden, projection, size, low):
    rows, features = hidden.shape
    width = projection.shape[1] // size
    count = size // 2
    cuts = 2
    piece = width // cuts

    def pick(i, j, tp):
        return (0, jnp.bitwise_xor(tp[0], 2 * i + low) * cuts + j)

    return pl.pallas_call(
        base_kernel,
        grid_spec=pltpu.PrefetchScalarGridSpec(
            num_scalar_prefetch=1,
            grid=(count, cuts),
            in_specs=[
                pl.BlockSpec((rows, features), lambda i, j, tp: (0, 0)),
                pl.BlockSpec((features, piece), pick),
            ],
            out_specs=pl.BlockSpec((1, rows, piece), lambda i, j, tp: (i, 0, j)),
        ),
        out_shape=jax.ShapeDtypeStruct((count, rows, width), F32),
        compiler_params=params(),
        cost_estimate=cost(
            2 * rows * features * width * count,
            2 * features * width * count + 2 * rows * features + 4 * rows * width * count,
        ),
        name="base_sent" if low else "base_kept",
    )(tp_index, hidden, projection)


def past_kernel(lengths_ref, query_ref, key_ref, value_ref, mixed_ref, lse_ref):
    steps, chunk, width = query_ref.shape
    _, heads, positions, size = key_ref.shape
    total_heads = width // size
    share = total_heads // heads
    first = pl.program_id(0) * chunk
    scaling = 1.0 / math.sqrt(size)
    by_seq = []
    for s in range(steps):
        whole = query_ref[s].astype(F32)
        stacked = jnp.stack(
            [whole[:, i * size : (i + 1) * size] for i in range(total_heads)], axis=0
        )
        by_seq.append(jnp.swapaxes(stacked, 0, 1))
    mixed_rows = [[] for _ in range(steps)]
    lse_rows = [[] for _ in range(steps)]
    for i in range(chunk):
        live = iota((steps * share, positions), 1) < lengths_ref[first + i]
        parts = []
        lses = []
        for g in range(heads):
            q = jnp.concatenate(
                [by_seq[s][i, g * share : (g + 1) * share, :] for s in range(steps)], axis=0
            ).astype(BF16)
            scores = (
                lax.dot_general(q, key_ref[i, g], NT, preferred_element_type=F32) * scaling
            )
            scores = jnp.where(live, scores, -jnp.inf)
            top = jnp.max(scores, axis=1, keepdims=True)
            raised = jnp.exp(scores - top)
            total = jnp.sum(raised, axis=1, keepdims=True)
            mixed = jnp.dot(
                raised.astype(BF16), value_ref[i, g], preferred_element_type=F32
            )
            parts.append(mixed / total)
            lses.append(jnp.broadcast_to(top + jnp.log(total), (steps * share, size)))
        for s in range(steps):
            cut = slice(s * share, (s + 1) * share)
            mixed_rows[s].append(jnp.concatenate([p[cut] for p in parts], axis=0))
            lse_rows[s].append(jnp.concatenate([p[cut] for p in lses], axis=0))
    lane = iota((chunk, size), 1)
    for s in range(steps):
        mixed = jnp.swapaxes(jnp.stack(mixed_rows[s], axis=0), 0, 1)
        lse = jnp.swapaxes(jnp.stack(lse_rows[s], axis=0), 0, 1)
        packed = jnp.zeros((chunk, size), F32)
        for i in range(total_heads):
            mixed_ref[s, :, i * size : (i + 1) * size] = mixed[i]
            packed = jnp.where(lane == i, lse[i], packed)
        lse_ref[s] = packed


def past(lengths, queries, keys, values):
    steps, seqs, width = queries.shape
    _, heads, positions, size = keys.shape
    chunk = 8
    cache_spec = pl.BlockSpec((chunk, heads, positions, size), lambda i, n: (i, 0, 0, 0))
    return pl.pallas_call(
        past_kernel,
        grid_spec=pltpu.PrefetchScalarGridSpec(
            num_scalar_prefetch=1,
            grid=(seqs // chunk,),
            in_specs=[
                pl.BlockSpec((steps, chunk, width), lambda i, n: (0, i, 0)),
                cache_spec,
                cache_spec,
            ],
            out_specs=[
                pl.BlockSpec((steps, chunk, width), lambda i, n: (0, i, 0)),
                pl.BlockSpec((steps, chunk, size), lambda i, n: (0, i, 0)),
            ],
        ),
        out_shape=[
            jax.ShapeDtypeStruct((steps, seqs, width), F32),
            jax.ShapeDtypeStruct((steps, seqs, size), F32),
        ],
        compiler_params=params(),
        cost_estimate=cost(
            4 * steps * seqs * width * positions,
            4 * seqs * heads * positions * size + 6 * steps * seqs * width,
            steps * seqs * (width // size) * positions,
        ),
        name="past",
    )(lengths, queries, keys, values)


def slot_mask(entries, rank, slots):
    return lax.div(iota((entries * rank, slots.shape[1]), 0), jnp.int32(rank)) == slots


def shrink_kernel(count, entries, rank, weight_ref, *refs):
    hidden, slots, out_ref = refs[:count], refs[count : 2 * count], refs[2 * count]
    rows = jnp.concatenate([r[...] for r in hidden], axis=0)
    slot = jnp.concatenate([r[...] for r in slots], axis=1)
    every = lax.dot_general(weight_ref[...], rows, NT, preferred_element_type=F32)
    kept = jnp.where(slot_mask(entries, rank, slot), every, 0.0)
    out_ref[...] = jnp.sum(kept.reshape(entries, rank, kept.shape[1]), axis=0)


def shrink(weight, hidden, slots):
    entries, rank, features = weight.shape
    count = len(hidden)
    rows = count * hidden[0].shape[0]
    return pl.pallas_call(
        functools.partial(shrink_kernel, count, entries, rank),
        out_shape=jax.ShapeDtypeStruct((rank, rows), F32),
        compiler_params=params(),
        cost_estimate=cost(
            2 * entries * rank * features * rows, 2 * features * (entries * rank + rows)
        ),
        name="shrink",
    )(weight.reshape(entries * rank, features), *hidden, *slots)


def expand_kernel(groups, size, entries, rank, weight_ref, *refs):
    parts, slots, outs = refs[:size], refs[size : size + groups], refs[size + groups :]
    total = parts[0][...]
    for part in parts[1:]:
        total = total + part[...]
    slot = jnp.concatenate([r[...] for r in slots], axis=1)
    shrunk = total.astype(BF16).astype(F32)
    spread = jnp.broadcast_to(shrunk[None], (entries,) + shrunk.shape).reshape(
        entries * rank, shrunk.shape[1]
    )
    spread = jnp.where(slot_mask(entries, rank, slot), spread, 0.0).astype(BF16)
    delta = adapter_scale * lax.dot_general(
        spread, weight_ref[...], TN, preferred_element_type=F32
    )
    delta = delta.astype(BF16)
    rows = outs[0].shape[0]
    for k in range(groups):
        outs[k][...] = delta[k * rows : (k + 1) * rows]


def expand(weight, parts, slots):
    entries, rank, columns = weight.shape
    groups = len(slots)
    rows = parts[0].shape[1] // groups
    return pl.pallas_call(
        functools.partial(expand_kernel, groups, len(parts), entries, rank),
        out_shape=[jax.ShapeDtypeStruct((rows, columns), BF16)] * groups,
        compiler_params=params(),
        cost_estimate=cost(
            2 * entries * rank * columns * rows * groups, 2 * entries * rank * columns
        ),
        name="expand",
    )(weight.reshape(entries * rank, columns), *parts, *slots)


def finish_kernel(
    groups, cap, heads, back_ref, own_ref, got_ref, query_ref, mixed_ref, lse_ref, *refs
):
    deltas, out_ref, new_ref = refs[:groups], refs[groups], refs[groups + 1]
    steps, seqs, width = query_ref.shape
    columns = new_ref.shape[2]
    size = columns // (2 * heads)
    share = width // (size * heads)
    scaling = 1.0 / math.sqrt(size)
    back = back_ref[...]
    new = []
    for s in range(steps):
        delta = jnp.concatenate([r[s * cap : (s + 1) * cap, :] for r in deltas], axis=0)
        update = jnp.dot(back, delta, preferred_element_type=F32)
        rows = slice(s * seqs, (s + 1) * seqs)
        base = own_ref[rows, :] + got_ref[rows, :].astype(F32)
        new.append((base + update).astype(BF16))
        new_ref[s] = new[s]
    for g in range(heads):
        left = g * 2 * size
        keys = jnp.concatenate([n[:, left : left + size] for n in new], axis=0)
        values = jnp.concatenate([n[:, left + size : left + 2 * size] for n in new], axis=0)
        for s in range(steps):
            fresh = (s + 1) * seqs
            same = lax.rem(iota((seqs, fresh), 1), jnp.int32(seqs)) == iota((seqs, fresh), 0)
            for h in range(share):
                head = g * share + h
                lanes = slice(head * size, (head + 1) * size)
                q = query_ref[s, :, lanes]
                scores = (
                    lax.dot_general(q, keys[:fresh], NT, preferred_element_type=F32) * scaling
                )
                scores = jnp.where(same, scores, -jnp.inf)
                lse = lse_ref[s, :, head : head + 1]
                top = jnp.maximum(jnp.max(scores, axis=1, keepdims=True), lse)
                raised = jnp.exp(scores - top)
                old = jnp.exp(lse - top)
                scale = 1.0 / (jnp.sum(raised, axis=1, keepdims=True) + old)
                weights = (raised * scale).astype(BF16)
                mixed = jnp.dot(weights, values[:fresh], preferred_element_type=F32)
                mixed = mixed + mixed_ref[s, :, lanes] * (old * scale)
                out_ref[s, :, lanes] = mixed.astype(BF16)


def finish(back, own, got, queries, mixed, lse, deltas, cap, heads):
    steps, seqs, width = queries.shape
    columns = own.shape[1]
    return pl.pallas_call(
        functools.partial(finish_kernel, len(deltas), cap, heads),
        out_shape=[
            jax.ShapeDtypeStruct((steps, seqs, width), BF16),
            jax.ShapeDtypeStruct((steps, seqs, columns), BF16),
        ],
        compiler_params=params(),
        cost_estimate=cost(
            4 * steps * seqs * width * steps * seqs,
            8 * steps * seqs * width + 8 * steps * seqs * columns,
            steps * seqs * width * 2,
        ),
        name="finish",
    )(back, own, got, queries, mixed, lse, *deltas)


def body(
    hidden,
    queries,
    projection,
    cached_key_rows,
    cached_value_rows,
    adapter_shrink_weight,
    adapter_expand_weight,
    requests,
    adapter_store_row,
    lengths,
):
    steps, seqs, features = hidden.shape
    groups = lax.axis_size("dp")
    size = lax.axis_size("tp")
    cap = seqs // 4
    entries = adapter_shrink_weight.shape[0]
    heads = cached_key_rows.shape[1]

    routed = route(requests, adapter_store_row, hidden, groups, cap, entries)
    blocks, slots, back = routed[:groups], routed[groups : 2 * groups], routed[2 * groups]
    over_dp = [None] + [swap("dp", groups, k) for k in range(1, groups)]
    over_tp = [None] + [swap("tp", size, k) for k in range(1, size)]
    order = sorted(range(1, groups), key=lambda k: -k)
    got_blocks = {0: blocks[0]}
    got_slots = {0: slots[0]}
    for k in order:
        got_blocks[k] = over_dp[k](blocks[k])
    for k in order:
        got_slots[k] = over_dp[k](slots[k])

    tp_index = lax.axis_index("tp").astype(jnp.int32).reshape(1)
    flat = hidden.reshape(steps * seqs, features)
    sent = base_part(tp_index, flat, projection, size, 1)
    kept = base_part(tp_index, flat, projection, size, 0)
    held = kept + over_tp[1](sent)
    distance = size // 2
    received = None
    while distance > 1:
        half = distance // 2
        received = over_tp[distance](held[half:].astype(BF16))
        if distance > 2:
            held = held[:half] + received.astype(F32)
        distance = half
    own, received = held[0], received[0]

    mixed, lse = past(lengths, queries, cached_key_rows, cached_value_rows)

    hidden_blocks = [got_blocks[k] for k in range(groups)]
    slot_blocks = [got_slots[k] for k in range(groups)]
    shrunk = shrink(adapter_shrink_weight, hidden_blocks, slot_blocks)
    parts = [shrunk] + [over_tp[k](shrunk) for k in range(1, size)]
    deltas = expand(adapter_expand_weight, parts, slot_blocks)
    deltas = [deltas[0]] + [over_dp[k](deltas[k]) for k in range(1, groups)]
    return tuple(finish(back, own, received, queries, mixed, lse, deltas, cap, heads))


def solution(mesh):
    placed = (
        P(None, ("rep", "dp"), "tp"),
        P(None, ("rep", "dp"), "tp"),
        P("tp", None),
        P(("rep", "dp"), "tp", None, None),
        P(("rep", "dp"), "tp", None, None),
        P("dp", None, "tp"),
        P("dp", None, "tp"),
        P(("rep", "dp")),
        P("rep"),
        P(("rep", "dp")),
    )
    return jax.shard_map(
        body,
        mesh=mesh,
        in_specs=placed,
        out_specs=(P(None, ("rep", "dp"), "tp"), P(None, ("rep", "dp"), "tp")),
        check_vma=False,
    )
```

time: 202 us -> 125 us (0.62)
  Pallas kernels: 0 us -> 71.1 us
  waiting for transfers between devices: 92.9 us -> 23.4 us
  matrix products: 44.8 us -> 0 us
  blocking collectives: 23.3 us -> 0 us
  between operations: 14.2 us -> 0.82 us
  starting transfers between devices: 8.58 us -> 20.5 us
  local copies, waits for them, and re-layouts: 13.5 us -> 7.26 us
  other arithmetic: 3.85 us -> 1.43 us
    all_to_all x2 -> x0, waiting for transfers between devices: 92.9 us -> none  [the longest x1 75.1 us: body(): lax.all_to_all(shrink_factor_rows, 'dp', split_axis=0, concat_axis=0, til...]
    pallas_call x0 -> x7, Pallas kernels: none -> 71.1 us  [the longest x1 32.5 us: past(): pl.pallas_call(past_kernel, grid_spec=pltpu.PrefetchScalarGridSpec(num_sc...]
    dot_general x11 -> x0, matrix products: 44.8 us -> none  [the longest x1 7.11 us: body(): jnp.dot(hidden.reshape(step_count * seq_count, feature_count), projection...]
    ppermute x0 -> x14, waiting for transfers between devices: none -> 23.4 us  [swap(): return lambda value: lax.ppermute(value, axis, pairs)]
    ppermute x0 -> x14, starting transfers between devices: none -> 20.5 us  [swap(): return lambda value: lax.ppermute(value, axis, pairs)]
    all_to_all x1 -> x0, blocking collectives: 11.7 us -> none  [body(): lax.all_to_all(bucket_slots, 'dp', split_axis=0, concat_axis=0, tiled=True)]
    psum x1 -> x0, blocking collectives: 11.6 us -> none  [body(): summed_output = lax.psum(shrunken_input, 'tp').astype(jnp.bfloat16)]
    all_to_all x2 -> x0, starting transfers between devices: 8.36 us -> none  [the longest x1 4.84 us: body(): lax.all_to_all(shrink_factor_rows, 'dp', split_axis=0, concat_axis=0, til...]
  transfers between devices with their start and end apart: 3 -> 14, of which waited for: 2 -> 5; matrix products, arithmetic and copies ran while one was open for 18% -> 1% of each run, Pallas kernels for 0% -> 30%
where the time goes in v1:
time: 125 us; the launch traced here: 124 us
  Pallas kernels  71.1 us (57%)
  waiting for transfers between devices  23.4 us (19%)
  starting transfers between devices  20.5 us (16%)
  local copies, waits for them, and re-layouts  7.26 us (6%)
  other arithmetic  1.43 us (1%)
    pallas_call x1, Pallas kernels, past(): pl.pallas_call(past_kernel, grid_spec=pltpu.PrefetchScalarGridSpec(num_sc...  32.5 us
    pallas_call x1, Pallas kernels, finish(): pl.pallas_call(functools.partial(finish_kernel, len(deltas), cap, heads),...  31.7 us
    ppermute x14, waiting for transfers between devices, swap(): return lambda value: lax.ppermute(value, axis, pairs)  23.4 us
    ppermute x14, starting transfers between devices, swap(): return lambda value: lax.ppermute(value, axis, pairs)  20.5 us
    unnamed x28, local copies, waits for them, and re-layouts  7.19 us
    pallas_call x2, Pallas kernels, base_part(): pl.pallas_call(base_kernel, grid_spec=pltpu.PrefetchScalarGridSpec(num_sc...  5.09 us
  transfers between devices with their start and end apart: 14, of which 5 were waited for; matrix products, arithmetic and copies ran while one was open for 1% of the time, Pallas kernels for 30%

profile of v1, /device:TPU:0, one launch (start us, length us, event | category | flops | bytes accessed | tf_op | source)
XLA Modules:
  0.0 124.4 jit_solution(6308590830763412656)
XLA Ops:
  0.6 0.0 copy-start
  0.6 3.4 %copy-done = bf16[2048,2048]{1,0:T(8,128)(2,1)S(1)} copy-done((bf16[2048,2048]{1,0:T(8,128)(2,1)S(1)}, bf16[2048,2048]{1,0:T(8,128)(2,1)}, u32[]{:S(2)}) %copy-start) | copy-done | bytes 8388632
  4.0 0.0 copy-start.2
  4.0 1.2 copy-done.2
  5.2 0.0 copy-start.3
  5.2 0.0 copy-start.11
  5.2 0.0 copy-start.12
  5.2 0.0 copy-start.1
  5.3 2.5 %base_sent.1 = f32[2,256,512]{2,1,0:T(8,128)S(1)} custom-call(s32[1]{0:T(128)} %bitcast.2.tp_ref, bf16[256,2048]{1,0:T(8,128)(2,1)S(1)} %bitcast.9, bf16[2048,2048]{1,0:T(8,128)(2,1)S(1)} %copy-done), custom_call_target="tpu_custom_call" | custom-call | flops 1073741824 | bytes 6291456 | tf_op jit(solution)/shard_map/base_sent/pallas_call | solution.py:107
  7.8 0.5 collective-permute-start
  8.3 0.0 copy-done.3
  8.3 0.0 copy-done.11
  8.3 0.0 copy-done.12
  8.3 0.6 route.1
  9.0 2.7 %collective-permute-start.2 = (bf16[64,2048]{1,0:T(8,128)(2,1)S(1)}, bf16[64,2048]{1,0:T(8,128)(2,1)S(1)}, u32[]{:S(2)}, u32[]{:S(2)}) collective-permute-start(bf16[64,2048]{1,0:T(8,128)(2,1)S(1)} %get-tuple-element.21), channel_id=1, source_target_pairs={{0,4},{4,0},{8,12},{12,8},{1,5},{5,1},{9,13},{13,9},{2,6},{6,2},{1... | collective-permute-start | bytes 786440 | tf_op jit(solution)/shard_map/ppermute | solution.py:31
  11.6 2.6 %collective-permute-start.3 = (bf16[64,2048]{1,0:T(8,128)(2,1)S(1)}, bf16[64,2048]{1,0:T(8,128)(2,1)S(1)}, u32[]{:S(2)}, u32[]{:S(2)}) collective-permute-start(bf16[64,2048]{1,0:T(8,128)(2,1)S(1)} %get-tuple-element.22), channel_id=1, source_target_pairs={{0,8},{4,12},{8,0},{12,4},{1,9},{5,13},{9,1},{13,5},{2,10},{6,14},... | collective-permute-start | bytes 786440 | tf_op jit(solution)/shard_map/ppermute | solution.py:31
  14.2 0.0 collective-permute-start.4
  14.2 0.9 collective-permute-start.5
  15.1 14.0 %collective-permute-done.5.refs_5_ = s32[1,64]{1,0:T(1,128)S(1)} collective-permute-done((s32[1,64]{1,0:T(1,128)S(1)}, s32[1,64]{1,0:T(1,128)S(1)}, u32[]{:S(2)}, u32[]{:S(2)}) %collective-permute-start.5) | collective-permute-done | bytes 288 | tf_op jit(solution)/shard_map/ppermute | solution.py:31
  29.2 3.4 %collective-permute-start.6 = (s32[1,64]{1,0:T(1,128)S(1)}, s32[1,64]{1,0:T(1,128)S(1)}, u32[]{:S(2)}, u32[]{:S(2)}) collective-permute-start(s32[1,64]{1,0:T(1,128)S(1)} %get-tuple-element.26), channel_id=1, source_target_pairs={{0,8},{4,12},{8,0},{12,4},{1,9},{5,13},{9,1},{13,5},{2,10},{6,14},... | collective-permute-start | bytes 776 | tf_op jit(solution)/shard_map/ppermute | solution.py:31
  32.6 5.2 %collective-permute-done.6.refs_6_ = s32[1,64]{1,0:T(1,128)S(1)} collective-permute-done((s32[1,64]{1,0:T(1,128)S(1)}, s32[1,64]{1,0:T(1,128)S(1)}, u32[]{:S(2)}, u32[]{:S(2)}) %collective-permute-start.6) | collective-permute-done | bytes 288 | tf_op jit(solution)/shard_map/ppermute | solution.py:31
  37.8 0.0 copy-start.6
  37.8 0.0 copy-start.13
  37.8 2.5 %collective-permute-start.7 = (s32[1,64]{1,0:T(1,128)S(1)}, s32[1,64]{1,0:T(1,128)S(1)}, u32[]{:S(2)}, u32[]{:S(2)}) collective-permute-start(s32[1,64]{1,0:T(1,128)S(1)} %get-tuple-element.27), channel_id=1, source_target_pairs={{0,12},{4,8},{8,4},{12,0},{1,13},{5,9},{9,5},{13,1},{2,14},{6,10},... | collective-permute-start | bytes 776 | tf_op jit(solution)/shard_map/ppermute | solution.py:31
  40.3 0.0 copy-done.1
  40.3 0.0 copy-start.4
  40.3 0.0 copy-start.5
  40.3 2.5 %base_kept.1 = f32[2,256,512]{2,1,0:T(8,128)S(1)} custom-call(s32[1]{0:T(128)} %bitcast.2.tp_ref, bf16[256,2048]{1,0:T(8,128)(2,1)S(1)} %bitcast.10, bf16[2048,2048]{1,0:T(8,128)(2,1)S(1)} %copy-done.1), custom_call_target="tpu_custom_call" | custom-call | flops 1073741824 | bytes 6291456 | tf_op jit(solution)/shard_map/base_kept/pallas_call | solution.py:107
  42.9 0.0 copy-start.7
  42.9 1.0 copy-done.7
  43.8 0.0 collective-permute-done.7.refs_7_
  43.8 0.0 collective-permute-done.2.refs_1_
  43.8 0.0 collective-permute-done.3.refs_2_
  43.8 0.0 collective-permute-done.4.refs_3_
  43.9 0.0 copy-start.9
  43.9 1.6 %copy-done.9 = bf16[32,16,2048]{2,1,0:T(8,128)(2,1)S(1)} copy-done((bf16[32,16,2048]{2,1,0:T(8,128)(2,1)S(1)}, bf16[32,16,2048]{2,1,0:T(8,128)(2,1)}, u32[]{:S(2)}) %copy-start.9) | copy-done | bytes 2097176
  45.5 0.7 shrink.1.refs_0_
  46.2 0.0 copy-start.8
  46.2 0.0 copy-start.10
  46.2 0.1 collective-permute-start.10
  46.3 1.5 %collective-permute-start.9 = (f32[16,256]{1,0:T(8,128)S(1)}, f32[16,256]{1,0:T(8,128)S(1)}, u32[]{:S(2)}, u32[]{:S(2)}) collective-permute-start(f32[16,256]{1,0:T(8,128)S(1)} %shrink.1.refs_0_), channel_id=1, source_target_pairs={{0,2},{1,3},{2,0},{3,1},{4,6},{5,7},{6,4},{7,5},{8,10},{9,11},{10,... | collective-permute-start | bytes 49160 | tf_op jit(solution)/shard_map/ppermute | solution.py:31
  47.9 0.3 collective-permute-start.8
  48.2 0.0 copy-done.6
  48.2 0.0 copy-done.13
  48.2 0.0 copy-done.4
  48.2 0.0 copy-done.5
  48.2 32.5 %past.1 = (f32[4,64,2048]{2,1,0:T(8,128)S(1)}, f32[4,64,128]{2,1,0:T(8,128)S(1)}) custom-call(s32[64]{0:T(128)S(1)} %copy-done.13, bf16[4,64,2048]{2,1,0:T(8,128)(2,1)S(1)} %copy-done.6, bf16[64,2,128,128]{3,2,1,0:T(8,128)(2,1)S(1)} %copy-done.4, bf16[64,2,128,128]{3,2,1,0:T(8,128)(2,1)S(1)} %copy-done.5), custom_call_target="tpu_custom_call" | custom-call | flops 268435456 | bytes 11534336 | tf_op jit(solution)/shard_map/past/pallas_call | solution.py:184
  80.7 0.0 collective-permute-done
  80.7 0.0 copy-done.8
  80.7 1.4 %add.3 = f32[2,256,512]{2,1,0:T(8,128)S(1)} add(f32[2,256,512]{2,1,0:T(8,128)S(1)} %copy-done.8, f32[2,256,512]{2,1,0:T(8,128)} %collective-permute-done) | non-fusion elementwise | flops 262144 | bytes 3145728 | tf_op jit(solution)/shard_map/add | solution.py:374
  82.2 1.5 %collective-permute-start.1 = (bf16[1,256,512]{2,1,0:T(8,128)(2,1)S(1)}, bf16[1,256,512]{2,1,0:T(8,128)(2,1)S(1)}, u32[]{:S(2)}, u32[]{:S(2)}) collective-permute-start(bf16[1,256,512]{2,1,0:T(8,128)(2,1)S(1)} %slice.13), channel_id=1, source_target_pairs={{0,2},{1,3},{2,0},{3,1},{4,6},{5,7},{6,4},{7,5},{8,10},{9,11},{10,... | collective-permute-start | bytes 786440 | tf_op jit(solution)/shard_map/ppermute | solution.py:31
  83.8 0.0 collective-permute-done.10.refs_3_
  83.8 0.0 collective-permute-done.9.refs_2_
  83.8 0.0 collective-permute-done.8.refs_1_
  83.8 0.0 copy-done.10
  83.8 0.4 expand.1
  84.2 0.1 collective-permute-start.11
  84.3 2.3 %collective-permute-start.12 = (bf16[64,512]{1,0:T(8,128)(2,1)S(1)}, bf16[64,512]{1,0:T(8,128)(2,1)S(1)}, u32[]{:S(2)}, u32[]{:S(2)}) collective-permute-start(bf16[64,512]{1,0:T(8,128)(2,1)S(1)} %get-tuple-element.30), channel_id=1, source_target_pairs={{0,8},{4,12},{8,0},{12,4},{1,9},{5,13},{9,1},{13,5},{2,10},{6,14},... | collective-permute-start | bytes 196616 | tf_op jit(solution)/shard_map/ppermute | solution.py:31
  86.6 2.0 %collective-permute-start.13 = (bf16[64,512]{1,0:T(8,128)(2,1)S(1)}, bf16[64,512]{1,0:T(8,128)(2,1)S(1)}, u32[]{:S(2)}, u32[]{:S(2)}) collective-permute-start(bf16[64,512]{1,0:T(8,128)(2,1)S(1)} %get-tuple-element.31), channel_id=1, source_target_pairs={{0,12},{4,8},{8,4},{12,0},{1,13},{5,9},{9,5},{13,1},{2,14},{6,10},... | collective-permute-start | bytes 196616 | tf_op jit(solution)/shard_map/ppermute | solution.py:31
  88.7 0.3 collective-permute-done.11.refs_1_
  89.0 2.8 %collective-permute-done.12.refs_2_ = bf16[64,512]{1,0:T(8,128)(2,1)S(1)} collective-permute-done((bf16[64,512]{1,0:T(8,128)(2,1)S(1)}, bf16[64,512]{1,0:T(8,128)(2,1)S(1)}, u32[]{:S(2)}, u32[]{:S(2)}) %collective-permute-start.12) | collective-permute-done | bytes 65568 | tf_op jit(solution)/shard_map/ppermute | solution.py:31
  91.8 1.0 collective-permute-done.13.refs_3_
  92.7 0.0 collective-permute-done.1
  92.7 31.7 %finish.1 = (bf16[4,64,2048]{2,1,0:T(8,128)(2,1)}, bf16[4,64,512]{2,1,0:T(8,128)(2,1)}) custom-call(bf16[64,64]{1,0:T(8,128)(2,1)S(1)} %get-tuple-element.17.back_ref, f32[256,512]{1,0:T(8,128)S(1)} %slice_bitcast_fusion.own_ref, bf16[256,512]{1,0:T(8,128)(2,1)S(1)} %bitcast.13, bf16[4,64,2048]{2,1,0:T(8,128)(2,1)S(1)} %copy-done.6, ...), custom_call_target="tpu_custom_call" | custom-call | flops 536870912 | bytes 5242880 | tf_op jit(solution)/shard_map/finish/pallas_call | solution.py:323
  (2 shorter events, 0.1 us)
Async XLA Ops:
  0.6 3.4 %copy-start = (bf16[2048,2048]{1,0:T(8,128)(2,1)S(1)}, bf16[2048,2048]{1,0:T(8,128)(2,1)}, u32[]{:S(2)}) copy-start(bf16[2048,2048]{1,0:T(8,128)(2,1)} %projection_ref.3) | copy-start | bytes 25165828
  4.0 1.2 copy-start.2
  5.2 3.1 %copy-start.3 = (bf16[4,64,2048]{2,1,0:T(8,128)(2,1)S(1)}, bf16[4,64,2048]{2,1,0:T(8,128)(2,1)}, u32[]{:S(2)}) copy-start(bf16[4,64,2048]{2,1,0:T(8,128)(2,1)} %hidden_ref.1) | copy-start | bytes 3145732
  5.2 3.1 %copy-start.11 = (s32[64]{0:T(128)S(1)}, s32[64]{0:T(128)}, u32[]{:S(2)}) copy-start(s32[64]{0:T(128)} %param.17) | copy-start | bytes 772
  5.2 3.1 %copy-start.12 = (s32[128]{0:T(128)S(1)}, s32[128]{0:T(128)}, u32[]{:S(2)}) copy-start(s32[128]{0:T(128)} %param.18) | copy-start | bytes 1540
  5.2 35.1 %copy-start.1 = (bf16[2048,2048]{1,0:T(8,128)(2,1)S(1)}, bf16[2048,2048]{1,0:T(8,128)(2,1)}, u32[]{:S(2)}) copy-start(bf16[2048,2048]{1,0:T(8,128)(2,1)} %projection_ref.3) | copy-start | bytes 25165828
  7.8 72.9 %collective-permute-start = (f32[2,256,512]{2,1,0:T(8,128)S(1)}, f32[2,256,512]{2,1,0:T(8,128)}, u32[]{:S(2)}, u32[]{:S(2)}) collective-permute-start(f32[2,256,512]{2,1,0:T(8,128)S(1)} %base_sent.1), channel_id=1, source_target_pairs={{0,1},{1,0},{2,3},{3,2},{4,5},{5,4},{6,7},{7,6},{8,9},{9,8},{10,11... | collective-permute-start | bytes 3145736 | tf_op jit(solution)/shard_map/ppermute | solution.py:31
  9.0 34.9 %collective-permute-start.2 = (bf16[64,2048]{1,0:T(8,128)(2,1)S(1)}, bf16[64,2048]{1,0:T(8,128)(2,1)S(1)}, u32[]{:S(2)}, u32[]{:S(2)}) collective-permute-start(bf16[64,2048]{1,0:T(8,128)(2,1)S(1)} %get-tuple-element.21), channel_id=1, source_target_pairs={{0,4},{4,0},{8,12},{12,8},{1,5},{5,1},{9,13},{13,9},{2,6},{6,2},{1... | collective-permute-start | bytes 786440 | tf_op jit(solution)/shard_map/ppermute | solution.py:31
  11.6 32.2 %collective-permute-start.3 = (bf16[64,2048]{1,0:T(8,128)(2,1)S(1)}, bf16[64,2048]{1,0:T(8,128)(2,1)S(1)}, u32[]{:S(2)}, u32[]{:S(2)}) collective-permute-start(bf16[64,2048]{1,0:T(8,128)(2,1)S(1)} %get-tuple-element.22), channel_id=1, source_target_pairs={{0,8},{4,12},{8,0},{12,4},{1,9},{5,13},{9,1},{13,5},{2,10},{6,14},... | collective-permute-start | bytes 786440 | tf_op jit(solution)/shard_map/ppermute | solution.py:31
  14.2 29.6 %collective-permute-start.4 = (bf16[64,2048]{1,0:T(8,128)(2,1)S(1)}, bf16[64,2048]{1,0:T(8,128)(2,1)S(1)}, u32[]{:S(2)}, u32[]{:S(2)}) collective-permute-start(bf16[64,2048]{1,0:T(8,128)(2,1)S(1)} %get-tuple-element.23), channel_id=1, source_target_pairs={{0,12},{4,8},{8,4},{12,0},{1,13},{5,9},{9,5},{13,1},{2,14},{6,10},... | collective-permute-start | bytes 786440 | tf_op jit(solution)/shard_map/ppermute | solution.py:31
  14.2 15.0 %collective-permute-start.5 = (s32[1,64]{1,0:T(1,128)S(1)}, s32[1,64]{1,0:T(1,128)S(1)}, u32[]{:S(2)}, u32[]{:S(2)}) collective-permute-start(s32[1,64]{1,0:T(1,128)S(1)} %get-tuple-element.25), channel_id=1, source_target_pairs={{0,4},{4,0},{8,12},{12,8},{1,5},{5,1},{9,13},{13,9},{2,6},{6,2},{1... | collective-permute-start | bytes 776 | tf_op jit(solution)/shard_map/ppermute | solution.py:31
  29.2 8.7 %collective-permute-start.6 = (s32[1,64]{1,0:T(1,128)S(1)}, s32[1,64]{1,0:T(1,128)S(1)}, u32[]{:S(2)}, u32[]{:S(2)}) collective-permute-start(s32[1,64]{1,0:T(1,128)S(1)} %get-tuple-element.26), channel_id=1, source_target_pairs={{0,8},{4,12},{8,0},{12,4},{1,9},{5,13},{9,1},{13,5},{2,10},{6,14},... | collective-permute-start | bytes 776 | tf_op jit(solution)/shard_map/ppermute | solution.py:31
  37.8 10.3 %copy-start.6 = (bf16[4,64,2048]{2,1,0:T(8,128)(2,1)S(1)}, bf16[4,64,2048]{2,1,0:T(8,128)(2,1)}, u32[]{:S(2)}) copy-start(bf16[4,64,2048]{2,1,0:T(8,128)(2,1)} %query_ref.3) | copy-start | bytes 3145732
  37.8 10.3 %copy-start.13 = (s32[64]{0:T(128)S(1)}, s32[64]{0:T(128)}, u32[]{:S(2)}) copy-start(s32[64]{0:T(128)} %lengths_ref.1) | copy-start | bytes 772
  37.8 6.0 %collective-permute-start.7 = (s32[1,64]{1,0:T(1,128)S(1)}, s32[1,64]{1,0:T(1,128)S(1)}, u32[]{:S(2)}, u32[]{:S(2)}) collective-permute-start(s32[1,64]{1,0:T(1,128)S(1)} %get-tuple-element.27), channel_id=1, source_target_pairs={{0,12},{4,8},{8,4},{12,0},{1,13},{5,9},{9,5},{13,1},{2,14},{6,10},... | collective-permute-start | bytes 776 | tf_op jit(solution)/shard_map/ppermute | solution.py:31
  40.3 7.9 %copy-start.4 = (bf16[64,2,128,128]{3,2,1,0:T(8,128)(2,1)S(1)}, bf16[64,2,128,128]{3,2,1,0:T(8,128)(2,1)}, u32[]{:S(2)}) copy-start(bf16[64,2,128,128]{3,2,1,0:T(8,128)(2,1)} %key_ref.1) | copy-start | bytes 12582916
  40.3 7.9 %copy-start.5 = (bf16[64,2,128,128]{3,2,1,0:T(8,128)(2,1)S(1)}, bf16[64,2,128,128]{3,2,1,0:T(8,128)(2,1)}, u32[]{:S(2)}) copy-start(bf16[64,2,128,128]{3,2,1,0:T(8,128)(2,1)} %value_ref.1) | copy-start | bytes 12582916
  42.9 1.0 copy-start.7
  43.9 1.6 %copy-start.9 = (bf16[32,16,2048]{2,1,0:T(8,128)(2,1)S(1)}, bf16[32,16,2048]{2,1,0:T(8,128)(2,1)}, u32[]{:S(2)}) copy-start(bf16[32,16,2048]{2,1,0:T(8,128)(2,1)} %param.15) | copy-start | bytes 6291460
  46.2 34.5 %copy-start.8 = (f32[2,256,512]{2,1,0:T(8,128)S(1)}, f32[2,256,512]{2,1,0:T(8,128)}, u32[]{:S(2)}) copy-start(f32[2,256,512]{2,1,0:T(8,128)} %copy-done.7) | copy-start | bytes 3145732
  46.2 37.6 %copy-start.10 = (bf16[32,16,512]{2,1,0:T(8,128)(2,1)S(1)}, bf16[32,16,512]{2,1,0:T(8,128)(2,1)}, u32[]{:S(2)}) copy-start(bf16[32,16,512]{2,1,0:T(8,128)(2,1)} %param.16) | copy-start | bytes 1572868
  46.2 37.5 %collective-permute-start.10 = (f32[16,256]{1,0:T(8,128)S(1)}, f32[16,256]{1,0:T(8,128)S(1)}, u32[]{:S(2)}, u32[]{:S(2)}) collective-permute-start(f32[16,256]{1,0:T(8,128)S(1)} %shrink.1.refs_0_), channel_id=1, source_target_pairs={{0,3},{1,2},{2,1},{3,0},{4,7},{5,6},{6,5},{7,4},{8,11},{9,10},{10,... | collective-permute-start | bytes 49160 | tf_op jit(solution)/shard_map/ppermute | solution.py:31
  46.3 37.5 %collective-permute-start.9 = (f32[16,256]{1,0:T(8,128)S(1)}, f32[16,256]{1,0:T(8,128)S(1)}, u32[]{:S(2)}, u32[]{:S(2)}) collective-permute-start(f32[16,256]{1,0:T(8,128)S(1)} %shrink.1.refs_0_), channel_id=1, source_target_pairs={{0,2},{1,3},{2,0},{3,1},{4,6},{5,7},{6,4},{7,5},{8,10},{9,11},{10,... | collective-permute-start | bytes 49160 | tf_op jit(solution)/shard_map/ppermute | solution.py:31
  47.9 35.9 %collective-permute-start.8 = (f32[16,256]{1,0:T(8,128)S(1)}, f32[16,256]{1,0:T(8,128)S(1)}, u32[]{:S(2)}, u32[]{:S(2)}) collective-permute-start(f32[16,256]{1,0:T(8,128)S(1)} %shrink.1.refs_0_), channel_id=1, source_target_pairs={{0,1},{1,0},{2,3},{3,2},{4,5},{5,4},{6,7},{7,6},{8,9},{9,8},{10,11... | collective-permute-start | bytes 49160 | tf_op jit(solution)/shard_map/ppermute | solution.py:31
  82.2 10.5 %collective-permute-start.1 = (bf16[1,256,512]{2,1,0:T(8,128)(2,1)S(1)}, bf16[1,256,512]{2,1,0:T(8,128)(2,1)S(1)}, u32[]{:S(2)}, u32[]{:S(2)}) collective-permute-start(bf16[1,256,512]{2,1,0:T(8,128)(2,1)S(1)} %slice.13), channel_id=1, source_target_pairs={{0,2},{1,3},{2,0},{3,1},{4,6},{5,7},{6,4},{7,5},{8,10},{9,11},{10,... | collective-permute-start | bytes 786440 | tf_op jit(solution)/shard_map/ppermute | solution.py:31
  84.2 4.8 %collective-permute-start.11 = (bf16[64,512]{1,0:T(8,128)(2,1)S(1)}, bf16[64,512]{1,0:T(8,128)(2,1)S(1)}, u32[]{:S(2)}, u32[]{:S(2)}) collective-permute-start(bf16[64,512]{1,0:T(8,128)(2,1)S(1)} %get-tuple-element.29), channel_id=1, source_target_pairs={{0,4},{4,0},{8,12},{12,8},{1,5},{5,1},{9,13},{13,9},{2,6},{6,2},{1... | collective-permute-start | bytes 196616 | tf_op jit(solution)/shard_map/ppermute | solution.py:31
  84.3 7.5 %collective-permute-start.12 = (bf16[64,512]{1,0:T(8,128)(2,1)S(1)}, bf16[64,512]{1,0:T(8,128)(2,1)S(1)}, u32[]{:S(2)}, u32[]{:S(2)}) collective-permute-start(bf16[64,512]{1,0:T(8,128)(2,1)S(1)} %get-tuple-element.30), channel_id=1, source_target_pairs={{0,8},{4,12},{8,0},{12,4},{1,9},{5,13},{9,1},{13,5},{2,10},{6,14},... | collective-permute-start | bytes 196616 | tf_op jit(solution)/shard_map/ppermute | solution.py:31
  86.6 6.1 %collective-permute-start.13 = (bf16[64,512]{1,0:T(8,128)(2,1)S(1)}, bf16[64,512]{1,0:T(8,128)(2,1)S(1)}, u32[]{:S(2)}, u32[]{:S(2)}) collective-permute-start(bf16[64,512]{1,0:T(8,128)(2,1)S(1)} %get-tuple-element.31), channel_id=1, source_target_pairs={{0,12},{4,8},{8,4},{12,0},{1,13},{5,9},{9,5},{13,1},{2,14},{6,10},... | collective-permute-start | bytes 196616 | tf_op jit(solution)/shard_map/ppermute | solution.py:31

commit v2 on v1

v2 whole, which is shorter than its diff:
```python
import functools
import math

import jax
import jax.numpy as jnp
from jax import lax
from jax.experimental import pallas as pl
from jax.experimental.pallas import tpu as pltpu
from jax.sharding import PartitionSpec as P

adapter_scale = 0.5
F32 = jnp.float32
BF16 = jnp.bfloat16
NT = (((1,), (1,)), ((), ()))
TN = (((0,), (0,)), ((), ()))
MIB = 1024 * 1024
LANES = 128


def params(mib):
    return pltpu.CompilerParams(vmem_limit_bytes=mib * MIB)


def cost(flops, nbytes, transcendentals=0):
    return pl.CostEstimate(
        flops=int(flops), bytes_accessed=int(nbytes), transcendentals=int(transcendentals)
    )


def swap(axis, size, distance):
    pairs = [(i, i ^ distance) for i in range(size)]
    return lambda value: lax.ppermute(value, axis, pairs)


def iota(shape, dim):
    return lax.broadcasted_iota(jnp.int32, shape, dim)


def column(row):
    size = row.shape[1]
    diagonal = iota((size, size), 0) == iota((size, size), 1)
    return jnp.sum(jnp.where(diagonal, row, 0.0), axis=1, keepdims=True)


def route_kernel(groups, cap, entries, requests_ref, store_ref, hidden_ref, *outs):
    blocks, back_ref = outs[:groups], outs[groups]
    steps, seqs, features = hidden_ref.shape
    tiles = features // LANES
    me = lax.axis_index("dp")
    store_col = column(store_ref[...].astype(F32))
    adapters = store_col.shape[0]
    rows = jnp.sum(
        jnp.where(iota((adapters, seqs), 0) == requests_ref[...], store_col, 0.0),
        axis=0,
        keepdims=True,
    ).astype(jnp.int32)
    owner = lax.div(rows, jnp.int32(entries))
    slot_col = column((rows - owner * entries).astype(F32))
    distance = jnp.bitwise_xor(owner, me).astype(F32)
    distance_col = column(distance)
    before = (distance_col == distance) & (iota((seqs, seqs), 0) < iota((seqs, seqs), 1))
    rank = jnp.sum(jnp.where(before, 1.0, 0.0), axis=0, keepdims=True)
    bucket = distance * cap + rank
    bucket_col = column(bucket).astype(jnp.int32)
    bucket = bucket.astype(jnp.int32)
    placed = jnp.where(iota((groups * cap, seqs), 0) == bucket, 1.0, 0.0).astype(BF16)
    back_ref[...] = jnp.where(bucket_col == iota((seqs, groups * cap), 1), 1.0, 0.0).astype(BF16)
    for k in range(groups):
        spot = lax.rem(iota((seqs, LANES), 1), jnp.int32(cap)) + k * cap
        slots = jnp.sum(jnp.where(bucket_col == spot, slot_col, 0.0), axis=0, keepdims=True)
        blocks[k][steps * tiles * cap :, :] = jnp.broadcast_to(slots, (cap, LANES)).astype(BF16)
    for s in range(steps):
        picked = jnp.dot(placed, hidden_ref[s], preferred_element_type=F32).astype(BF16)
        for k in range(groups):
            for c in range(tiles):
                first = (s * tiles + c) * cap
                blocks[k][first : first + cap, :] = picked[
                    k * cap : (k + 1) * cap, c * LANES : (c + 1) * LANES
                ]


def route(requests, store, hidden, groups, cap, entries):
    steps, seqs, features = hidden.shape
    rows = (steps * (features // LANES) + 1) * cap
    return pl.pallas_call(
        functools.partial(route_kernel, groups, cap, entries),
        out_shape=[jax.ShapeDtypeStruct((rows, LANES), BF16)] * groups
        + [jax.ShapeDtypeStruct((seqs, groups * cap), BF16)],
        compiler_params=params(10),
        cost_estimate=cost(
            2 * groups * cap * seqs * steps * features, 4 * steps * seqs * features
        ),
        name="route",
    )(requests[None, :], store[None, :], hidden)


def base_kernel(size, hidden_ref, projection_ref, *outs):
    width = outs[0].shape[1]
    me = lax.axis_index("tp")
    for k in list(range(1, size)) + [0]:
        first = pl.multiple_of(jnp.bitwise_xor(me, k) * width, width)
        part = jnp.dot(
            hidden_ref[...], projection_ref[:, pl.ds(first, width)], preferred_element_type=F32
        )
        outs[k][...] = part.astype(outs[k].dtype)


def base(hidden, projection, size):
    rows, _ = hidden.shape
    width = projection.shape[1] // size
    return pl.pallas_call(
        functools.partial(base_kernel, size),
        out_shape=[jax.ShapeDtypeStruct((rows, width), F32)]
        + [jax.ShapeDtypeStruct((rows, width), BF16)] * (size - 1),
        compiler_params=params(20),
        cost_estimate=cost(0, 4096),
        name="base",
    )(hidden, projection)


def past_kernel(lengths_ref, query_ref, key_ref, value_ref, mixed_ref, lse_ref):
    steps, chunk, width = query_ref.shape
    _, heads, positions, size = key_ref.shape
    share = width // (size * heads)
    rows = steps * share
    first = pl.program_id(0) * chunk
    scaling = 1.0 / math.sqrt(size)

    def lanes(g, h):
        return slice((g * share + h) * size, (g * share + h + 1) * size)

    by_seq = {}
    for s in range(steps):
        whole = query_ref[s].astype(F32)
        for g in range(heads):
            stacked = jnp.stack([whole[:, lanes(g, h)] for h in range(share)], axis=0)
            by_seq[s, g] = jnp.swapaxes(stacked, 0, 1)
    units = [(i, g) for i in range(chunk) for g in range(heads)]
    scores = []
    for i, g in units:
        q = jnp.concatenate([by_seq[s, g][i] for s in range(steps)], axis=0).astype(BF16)
        raw = lax.dot_general(q, key_ref[i, g], NT, preferred_element_type=F32) * scaling
        live = iota((rows, positions), 1) < lengths_ref[first + i]
        scores.append(jnp.where(live, raw, -jnp.inf))
    scores = jnp.concatenate(scores, axis=0)
    top = jnp.max(scores, axis=1, keepdims=True)
    raised = jnp.exp(scores - top)
    total = jnp.sum(raised, axis=1, keepdims=True)
    weights = raised.astype(BF16)
    mixed = [
        jnp.dot(weights[u * rows : (u + 1) * rows], value_ref[i, g], preferred_element_type=F32)
        for u, (i, g) in enumerate(units)
    ]
    mixed = jnp.concatenate(mixed, axis=0) * (1.0 / total)
    lse = jnp.broadcast_to(top + jnp.log(total), mixed.shape)
    mixed = mixed.reshape(chunk, heads, steps, share, size)
    lse = lse.reshape(chunk, heads, steps, share, size)
    for s in range(steps):
        for g in range(heads):
            mixed_by_head = jnp.swapaxes(mixed[:, g, s], 0, 1)
            lse_by_head = jnp.swapaxes(lse[:, g, s], 0, 1)
            for h in range(share):
                mixed_ref[s, :, lanes(g, h)] = mixed_by_head[h]
                lse_ref[s, :, lanes(g, h)] = lse_by_head[h]


def past(lengths, queries, keys, values):
    steps, seqs, width = queries.shape
    _, heads, positions, size = keys.shape
    chunk = 8
    cache_spec = pl.BlockSpec((chunk, heads, positions, size), lambda i, n: (i, 0, 0, 0))
    return pl.pallas_call(
        past_kernel,
        grid_spec=pltpu.PrefetchScalarGridSpec(
            num_scalar_prefetch=1,
            grid=(seqs // chunk,),
            in_specs=[
                pl.BlockSpec((steps, chunk, width), lambda i, n: (0, i, 0)),
                cache_spec,
                cache_spec,
            ],
            out_specs=[
                pl.BlockSpec((steps, chunk, width), lambda i, n: (0, i, 0)),
                pl.BlockSpec((steps, chunk, width), lambda i, n: (0, i, 0)),
            ],
        ),
        out_shape=[
            jax.ShapeDtypeStruct((steps, seqs, width), F32),
            jax.ShapeDtypeStruct((steps, seqs, width), F32),
        ],
        compiler_params=params(16),
        cost_estimate=cost(0, 4096),
        name="past",
    )(lengths, queries, keys, values)


def slot_mask(entries, rank, slots):
    return lax.div(iota((entries * rank, slots.shape[1]), 0), jnp.int32(rank)) == slots


def shrink_kernel(count, steps, cap, entries, rank, weight_ref, *refs):
    blocks, out_ref, slot_ref = refs[:count], refs[count], refs[count + 1]
    tiles = weight_ref.shape[1] // LANES
    rows = []
    for block in blocks:
        for s in range(steps):
            places = [(s * tiles + c) * cap for c in range(tiles)]
            rows.append(jnp.concatenate([block[p : p + cap, :] for p in places], axis=1))
    rows = jnp.concatenate(rows, axis=0)
    slots = [b[steps * tiles * cap :, :][:1, : steps * cap].astype(F32) for b in blocks]
    slots = jnp.concatenate(slots, axis=1).astype(jnp.int32)
    slot_ref[...] = slots
    every = lax.dot_general(weight_ref[...], rows, NT, preferred_element_type=F32)
    kept = jnp.where(slot_mask(entries, rank, slots), every, 0.0)
    out_ref[...] = jnp.sum(kept.reshape(entries, rank, kept.shape[1]), axis=0)


def shrink(weight, blocks, steps, cap):
    entries, rank, features = weight.shape
    count = len(blocks)
    rows = count * steps * cap
    return pl.pallas_call(
        functools.partial(shrink_kernel, count, steps, cap, entries, rank),
        out_shape=[
            jax.ShapeDtypeStruct((rank, rows), F32),
            jax.ShapeDtypeStruct((1, rows), jnp.int32),
        ],
        compiler_params=params(12),
        cost_estimate=cost(
            2 * entries * rank * features * rows, 2 * features * (entries * rank + rows)
        ),
        name="shrink",
    )(weight.reshape(entries * rank, features), *blocks)


def expand_kernel(groups, size, entries, rank, weight_ref, slot_ref, *refs):
    parts, outs = refs[:size], refs[size:]
    total = parts[0][...]
    for part in parts[1:]:
        total = total + part[...]
    shrunk = total.astype(BF16).astype(F32)
    spread = jnp.broadcast_to(shrunk[None], (entries,) + shrunk.shape).reshape(
        entries * rank, shrunk.shape[1]
    )
    spread = jnp.where(slot_mask(entries, rank, slot_ref[...]), spread, 0.0).astype(BF16)
    delta = adapter_scale * lax.dot_general(
        spread, weight_ref[...], TN, preferred_element_type=F32
    )
    delta = delta.astype(BF16)
    rows = outs[0].shape[0]
    for k in range(groups):
        outs[k][...] = delta[k * rows : (k + 1) * rows]


def expand(weight, parts, slots, groups):
    entries, rank, columns = weight.shape
    rows = parts[0].shape[1] // groups
    return pl.pallas_call(
        functools.partial(expand_kernel, groups, len(parts), entries, rank),
        out_shape=[jax.ShapeDtypeStruct((rows, columns), BF16)] * groups,
        compiler_params=params(8),
        cost_estimate=cost(
            2 * entries * rank * columns * rows * groups, 2 * entries * rank * columns
        ),
        name="expand",
    )(weight.reshape(entries * rank, columns), slots, *parts)


def finish_kernel(
    groups, size, cap, heads, back_ref, query_ref, mixed_ref, lse_ref, *refs
):
    summands, deltas = refs[:size], refs[size : size + groups]
    out_ref, new_ref = refs[size + groups :]
    steps, seqs, width = query_ref.shape
    columns = new_ref.shape[2]
    size = columns // (2 * heads)
    share = width // (size * heads)
    scaling = 1.0 / math.sqrt(size)
    back = back_ref[...]
    new = []
    for s in range(steps):
        delta = jnp.concatenate([r[s * cap : (s + 1) * cap, :] for r in deltas], axis=0)
        update = jnp.dot(back, delta, preferred_element_type=F32)
        rows = slice(s * seqs, (s + 1) * seqs)
        base = summands[0][rows, :]
        for summand in summands[1:]:
            base = base + summand[rows, :].astype(F32)
        new.append((base + update).astype(BF16))
        new_ref[s] = new[s]
    ones = jnp.ones((2 * size, size), BF16)
    for g in range(heads):
        left = g * 2 * size
        keys = [n[:, left : left + size].astype(F32) * scaling for n in new]
        values = [n[:, left + size : left + 2 * size].astype(F32) for n in new]
        for s in range(steps):
            for h in range(share):
                lanes = slice((g * share + h) * size, (g * share + h + 1) * size)
                q = query_ref[s, :, lanes].astype(F32)
                halves = []
                for t in range(s + 1):
                    product = q * keys[t]
                    high = product.astype(BF16)
                    low = (product - high.astype(F32)).astype(BF16)
                    halves.append(jnp.concatenate([high, low], axis=1))
                halves = jnp.concatenate(halves, axis=0)
                scores = jnp.dot(halves, ones, preferred_element_type=F32)
                scores = [scores[t * seqs : (t + 1) * seqs] for t in range(s + 1)]
                lse = lse_ref[s, :, lanes]
                top = lse
                for score in scores:
                    top = jnp.maximum(top, score)
                old = jnp.exp(lse - top)
                total = old
                mixed = mixed_ref[s, :, lanes] * old
                for t in range(s + 1):
                    raised = jnp.exp(scores[t] - top)
                    total = total + raised
                    mixed = mixed + raised * values[t]
                out_ref[s, :, lanes] = (mixed / total).astype(BF16)


def finish(back, summands, queries, mixed, lse, deltas, cap, heads):
    steps, seqs, width = queries.shape
    columns = summands[0].shape[1]
    return pl.pallas_call(
        functools.partial(finish_kernel, len(deltas), len(summands), cap, heads),
        out_shape=[
            jax.ShapeDtypeStruct((steps, seqs, width), BF16),
            jax.ShapeDtypeStruct((steps, seqs, columns), BF16),
        ],
        compiler_params=params(16),
        cost_estimate=cost(
            4 * steps * seqs * width * steps * LANES,
            8 * steps * seqs * width + 8 * steps * seqs * columns,
            steps * seqs * width * 2,
        ),
        name="finish",
    )(back, queries, mixed, lse, *summands, *deltas)


def body(
    hidden,
    queries,
    projection,
    cached_key_rows,
    cached_value_rows,
    adapter_shrink_weight,
    adapter_expand_weight,
    requests,
    adapter_store_row,
    lengths,
):
    steps, seqs, features = hidden.shape
    groups = lax.axis_size("dp")
    size = lax.axis_size("tp")
    cap = seqs // 4
    entries = adapter_shrink_weight.shape[0]
    heads = cached_key_rows.shape[1]

    routed = route(requests, adapter_store_row, hidden, groups, cap, entries)
    blocks, back = routed[:groups], routed[groups]
    over_dp = [None] + [swap("dp", groups, k) for k in range(1, groups)]
    over_tp = [None] + [swap("tp", size, k) for k in range(1, size)]
    got = {k: over_dp[k](blocks[k]) for k in reversed(range(1, groups))}

    late_hidden, _ = lax.optimization_barrier((hidden, back))
    parts = base(late_hidden.reshape(steps * seqs, features), projection, size)
    summands = [parts[0]] + [over_tp[k](parts[k]) for k in reversed(range(1, size))]

    mixed, lse = past(lengths, queries, cached_key_rows, cached_value_rows)

    block, _ = lax.optimization_barrier((blocks[0], (lse, parts[0])))
    gathered = [block] + [got[k] for k in range(1, groups)]
    shrunk, slots = shrink(adapter_shrink_weight, gathered, steps, cap)
    parts = [shrunk] + [over_tp[k](shrunk) for k in range(1, size)]
    deltas = expand(adapter_expand_weight, parts, slots, groups)
    deltas = [deltas[0]] + [over_dp[k](deltas[k]) for k in range(1, groups)]
    return tuple(finish(back, summands, queries, mixed, lse, deltas, cap, heads))


def solution(mesh):
    placed = (
        P(None, ("rep", "dp"), "tp"),
        P(None, ("rep", "dp"), "tp"),
        P("tp", None),
        P(("rep", "dp"), "tp", None, None),
        P(("rep", "dp"), "tp", None, None),
        P("dp", None, "tp"),
        P("dp", None, "tp"),
        P(("rep", "dp")),
        P("rep"),
        P(("rep", "dp")),
    )
    return jax.shard_map(
        body,
        mesh=mesh,
        in_specs=placed,
        out_specs=(P(None, ("rep", "dp"), "tp"), P(None, ("rep", "dp"), "tp")),
        check_vma=False,
    )
```

time: 125 us -> 51.9 us (0.42)
  Pallas kernels: 71.1 us -> 14.5 us
  waiting for transfers between devices: 23.4 us -> 12.5 us
  starting transfers between devices: 20.5 us -> 16.8 us
  other arithmetic: 1.43 us -> 0 us
    pallas_call x4 -> x3, Pallas kernels: 37.5 us -> 7.46 us  [the longest x1 4.36 us: finish(): pl.pallas_call(functools.partial(finish_kernel, len(deltas), len(summands...]
    pallas_call x1, Pallas kernels: 32.5 us -> 6.1 us  [past(): pl.pallas_call(past_kernel, grid_spec=pltpu.PrefetchScalarGridSpec(num_sc...]
    ppermute x14 -> x12, waiting for transfers between devices: 23.4 us -> 12.5 us  [swap(): return lambda value: lax.ppermute(value, axis, pairs)]
    ppermute x14 -> x12, starting transfers between devices: 20.5 us -> 16.8 us  [swap(): return lambda value: lax.ppermute(value, axis, pairs)]
    add x1 -> x0, other arithmetic: 1.43 us -> none  [body(): held = kept + over_tp[1](sent)]
    unnamed x28 -> x22, local copies, waits for them, and re-layouts: 7.19 us -> 7.16 us
  transfers between devices with their start and end apart: 14 -> 12, of which waited for: 5 -> 5; matrix products, arithmetic and copies ran while one was open for 1% -> 0% of each run, Pallas kernels for 30% -> 18%
where the time goes in v2:
time: 51.9 us; the launch traced here: 51.7 us
  starting transfers between devices  16.8 us (32%)
  Pallas kernels  14.5 us (28%)
  waiting for transfers between devices  12.5 us (24%)
  local copies, waits for them, and re-layouts  7.16 us (14%)
  between operations  0.72 us (1%)
    ppermute x12, starting transfers between devices, swap(): return lambda value: lax.ppermute(value, axis, pairs)  16.8 us
    ppermute x12, waiting for transfers between devices, swap(): return lambda value: lax.ppermute(value, axis, pairs)  12.5 us
    unnamed x22, local copies, waits for them, and re-layouts  7.16 us
    pallas_call x1, Pallas kernels, past(): pl.pallas_call(past_kernel, grid_spec=pltpu.PrefetchScalarGridSpec(num_sc...  6.1 us
    pallas_call x1, Pallas kernels, finish(): pl.pallas_call(functools.partial(finish_kernel, len(deltas), len(summands...  4.36 us
    pallas_call x1, Pallas kernels, base(): pl.pallas_call(functools.partial(base_kernel, size), out_shape=[jax.Shape...  2.35 us
  transfers between devices with their start and end apart: 12, of which 5 were waited for; matrix products, arithmetic and copies ran while one was open for 0% of the time, Pallas kernels for 18%

profile of v2, /device:TPU:0, one launch (start us, length us, event | category | flops | bytes accessed | tf_op | source)
XLA Modules:
  0.0 51.7 jit_solution(7089225294706880645)
XLA Ops:
  0.6 0.0 copy-start.3
  0.6 1.2 %copy-done.3 = bf16[4,64,2048]{2,1,0:T(8,128)(2,1)S(1)} copy-done((bf16[4,64,2048]{2,1,0:T(8,128)(2,1)S(1)}, bf16[4,64,2048]{2,1,0:T(8,128)(2,1)}, u32[]{:S(2)}) %copy-start.3) | copy-done | bytes 1048600
  1.9 0.0 copy-start.8
  1.9 0.7 %copy-done.8 = s32[64]{0:T(128)S(1)} copy-done((s32[64]{0:T(128)S(1)}, s32[64]{0:T(128)}, u32[]{:S(2)}) %copy-start.8) | copy-done | bytes 280
  2.5 0.0 copy-start.9
  2.5 0.7 %copy-done.9 = s32[128]{0:T(128)S(1)} copy-done((s32[128]{0:T(128)S(1)}, s32[128]{0:T(128)}, u32[]{:S(2)}) %copy-start.9) | copy-done | bytes 536
  3.2 0.6 %route.1 = (bf16[1040,128]{1,0:T(8,128)(2,1)S(1)}, bf16[1040,128]{1,0:T(8,128)(2,1)S(1)}, bf16[1040,128]{1,0:T(8,128)(2,1)S(1)}, bf16[1040,128]{1,0:T(8,128)(2,1)S(1)}, bf16[64,64]{1,0:T(8,128)(2,1)S(1)}) custom-call(s32[1,64]{1,0:T(1,128)S(1)} %bitcast.8, s32[1,128]{1,0:T(1,128)S(1)} %bitcast.9, bf16[4,64,2048]{2,1,0:T(8,128)(2,1)S(1)} %copy-done.3), custom_call_target="tpu_custom_call" | custom-call | flops 67108864 | bytes 2097152 | tf_op jit(solution)/shard_map/route/pallas_call | solution.py:85
  3.8 3.1 %collective-permute-start.3 = (bf16[1040,128]{1,0:T(8,128)(2,1)S(1)}, bf16[1040,128]{1,0:T(8,128)(2,1)S(1)}, u32[]{:S(2)}, u32[]{:S(2)}) collective-permute-start(bf16[1040,128]{1,0:T(8,128)(2,1)S(1)} %get-tuple-element.31), channel_id=1, source_target_pairs={{0,4},{4,0},{8,12},{12,8},{1,5},{5,1},{9,13},{13,9},{2,6},{6,2},{1... | collective-permute-start | bytes 798728 | tf_op jit(solution)/shard_map/ppermute | solution.py:32
  6.9 2.6 %collective-permute-start.4 = (bf16[1040,128]{1,0:T(8,128)(2,1)S(1)}, bf16[1040,128]{1,0:T(8,128)(2,1)S(1)}, u32[]{:S(2)}, u32[]{:S(2)}) collective-permute-start(bf16[1040,128]{1,0:T(8,128)(2,1)S(1)} %get-tuple-element.32), channel_id=1, source_target_pairs={{0,8},{4,12},{8,0},{12,4},{1,9},{5,13},{9,1},{13,5},{2,10},{6,14},... | collective-permute-start | bytes 798728 | tf_op jit(solution)/shard_map/ppermute | solution.py:32
  9.5 0.0 collective-permute-start.5
  9.5 0.0 copy-start
  9.5 3.4 %copy-done = bf16[2048,2048]{1,0:T(8,128)(2,1)S(1)} copy-done((bf16[2048,2048]{1,0:T(8,128)(2,1)S(1)}, bf16[2048,2048]{1,0:T(8,128)(2,1)}, u32[]{:S(2)}) %copy-start) | copy-done | bytes 8388632
  12.8 0.0 copy-start.4
  12.8 1.2 %copy-done.4 = bf16[4,64,2048]{2,1,0:T(8,128)(2,1)S(1)} copy-done((bf16[4,64,2048]{2,1,0:T(8,128)(2,1)S(1)}, bf16[4,64,2048]{2,1,0:T(8,128)(2,1)}, u32[]{:S(2)}) %copy-start.4) | copy-done | bytes 1048600
  14.1 0.0 copy-start.1
  14.1 0.0 copy-start.2
  14.1 0.0 copy-start.5
  14.1 0.0 copy-start.10
  14.1 2.4 %base.1 = (f32[256,512]{1,0:T(8,128)S(1)}, bf16[256,512]{1,0:T(8,128)(2,1)S(1)}, bf16[256,512]{1,0:T(8,128)(2,1)S(1)}, bf16[256,512]{1,0:T(8,128)(2,1)S(1)}) custom-call(bf16[256,2048]{1,0:T(8,128)(2,1)S(1)} %bitcast.5, bf16[2048,2048]{1,0:T(8,128)(2,1)S(1)} %copy-done), custom_call_target="tpu_custom_call" | custom-call | bytes 4096 | tf_op jit(solution)/shard_map/base/pallas_call | solution.py:111
  16.4 0.4 collective-permute-start
  16.9 1.4 %collective-permute-start.1 = (bf16[256,512]{1,0:T(8,128)(2,1)S(1)}, bf16[256,512]{1,0:T(8,128)(2,1)S(1)}, u32[]{:S(2)}, u32[]{:S(2)}) collective-permute-start(bf16[256,512]{1,0:T(8,128)(2,1)S(1)} %get-tuple-element.27), channel_id=1, source_target_pairs={{0,2},{1,3},{2,0},{3,1},{4,6},{5,7},{6,4},{7,5},{8,10},{9,11},{10,... | collective-permute-start | bytes 786440 | tf_op jit(solution)/shard_map/ppermute | solution.py:32
  18.3 0.0 collective-permute-done.3.refs_1_
  18.3 0.0 copy-start.6
  18.3 0.0 copy-start.7
  18.3 0.1 collective-permute-start.2
  18.4 0.0 copy-done.1
  18.4 0.0 copy-done.2
  18.5 0.0 copy-done.5
  18.5 0.0 copy-done.10
  18.5 6.1 %past.1 = (f32[4,64,2048]{2,1,0:T(8,128)S(1)}, f32[4,64,2048]{2,1,0:T(8,128)S(1)}) custom-call(s32[64]{0:T(128)S(1)} %copy-done.10, bf16[4,64,2048]{2,1,0:T(8,128)(2,1)S(1)} %copy-done.5, bf16[64,2,128,128]{3,2,1,0:T(8,128)(2,1)S(1)} %copy-done.1, bf16[64,2,128,128]{3,2,1,0:T(8,128)(2,1)S(1)} %copy-done.2), custom_call_target="tpu_custom_call" | custom-call | bytes 4096 | tf_op jit(solution)/shard_map/past/pallas_call | solution.py:172
  24.6 3.9 %collective-permute-done.4.refs_2_ = bf16[1040,128]{1,0:T(8,128)(2,1)S(1)} collective-permute-done((bf16[1040,128]{1,0:T(8,128)(2,1)S(1)}, bf16[1040,128]{1,0:T(8,128)(2,1)S(1)}, u32[]{:S(2)}, u32[]{:S(2)}) %collective-permute-start.4) | collective-permute-done | bytes 266272 | tf_op jit(solution)/shard_map/ppermute | solution.py:32
  28.5 0.0 collective-permute-done.5.refs_3_
  28.5 0.0 copy-done.6
  28.5 0.7 %shrink.1 = (f32[16,256]{1,0:T(8,128)S(1)}, s32[1,256]{1,0:T(1,128)S(1)}) custom-call(bf16[512,2048]{1,0:T(8,128)(2,1)S(1)} %bitcast.6, bf16[1040,128]{1,0:T(8,128)(2,1)S(1)} %get-tuple-element.30.refs_0_, bf16[1040,128]{1,0:T(8,128)(2,1)S(1)} %collective-permute-done.3.refs_1_, bf16[1040,128]{1,0:T(8,128)(2,1)S(1)} %collective-permute-done.4.refs_2_, ...), custom_call_target="tpu_custom_call" | custom-call | flops 536870912 | bytes 3145728 | tf_op jit(solution)/shard_map/shrink/pallas_call | solution.py:222
  29.3 0.1 collective-permute-start.8
  29.3 1.6 %collective-permute-start.7 = (f32[16,256]{1,0:T(8,128)S(1)}, f32[16,256]{1,0:T(8,128)S(1)}, u32[]{:S(2)}, u32[]{:S(2)}) collective-permute-start(f32[16,256]{1,0:T(8,128)S(1)} %get-tuple-element.35.refs_0_), channel_id=1, source_target_pairs={{0,2},{1,3},{2,0},{3,1},{4,6},{5,7},{6,4},{7,5},{8,10},{9,11},{10,... | collective-permute-start | bytes 49160 | tf_op jit(solution)/shard_map/ppermute | solution.py:32
  30.9 1.7 %collective-permute-done.8.refs_3_ = f32[16,256]{1,0:T(8,128)S(1)} collective-permute-done((f32[16,256]{1,0:T(8,128)S(1)}, f32[16,256]{1,0:T(8,128)S(1)}, u32[]{:S(2)}, u32[]{:S(2)}) %collective-permute-start.8) | collective-permute-done | bytes 16416 | tf_op jit(solution)/shard_map/ppermute | solution.py:32
  32.6 0.1 collective-permute-start.6
  32.7 0.4 collective-permute-done.7.refs_2_
  33.1 0.7 %collective-permute-done.6.refs_1_ = f32[16,256]{1,0:T(8,128)S(1)} collective-permute-done((f32[16,256]{1,0:T(8,128)S(1)}, f32[16,256]{1,0:T(8,128)S(1)}, u32[]{:S(2)}, u32[]{:S(2)}) %collective-permute-start.6) | collective-permute-done | bytes 16416 | tf_op jit(solution)/shard_map/ppermute | solution.py:32
  33.8 0.0 copy-done.7
  33.8 0.3 expand.1
  34.1 4.9 %collective-permute-start.9 = (bf16[64,512]{1,0:T(8,128)(2,1)S(1)}, bf16[64,512]{1,0:T(8,128)(2,1)S(1)}, u32[]{:S(2)}, u32[]{:S(2)}) collective-permute-start(bf16[64,512]{1,0:T(8,128)(2,1)S(1)} %get-tuple-element.37), channel_id=1, source_target_pairs={{0,4},{4,0},{8,12},{12,8},{1,5},{5,1},{9,13},{13,9},{2,6},{6,2},{1... | collective-permute-start | bytes 196616 | tf_op jit(solution)/shard_map/ppermute | solution.py:32
  39.0 1.1 %collective-permute-start.10 = (bf16[64,512]{1,0:T(8,128)(2,1)S(1)}, bf16[64,512]{1,0:T(8,128)(2,1)S(1)}, u32[]{:S(2)}, u32[]{:S(2)}) collective-permute-start(bf16[64,512]{1,0:T(8,128)(2,1)S(1)} %get-tuple-element.38), channel_id=1, source_target_pairs={{0,8},{4,12},{8,0},{12,4},{1,9},{5,13},{9,1},{13,5},{2,10},{6,14},... | collective-permute-start | bytes 196616 | tf_op jit(solution)/shard_map/ppermute | solution.py:32
  40.1 0.0 collective-permute-done.refs_1_
  40.1 1.4 %collective-permute-start.11 = (bf16[64,512]{1,0:T(8,128)(2,1)S(1)}, bf16[64,512]{1,0:T(8,128)(2,1)S(1)}, u32[]{:S(2)}, u32[]{:S(2)}) collective-permute-start(bf16[64,512]{1,0:T(8,128)(2,1)S(1)} %get-tuple-element.39), channel_id=1, source_target_pairs={{0,12},{4,8},{8,4},{12,0},{1,13},{5,9},{9,5},{13,1},{2,14},{6,10},... | collective-permute-start | bytes 196616 | tf_op jit(solution)/shard_map/ppermute | solution.py:32
  41.5 0.0 collective-permute-done.1.refs_2_
  41.5 0.0 collective-permute-done.2.refs_3_
  41.5 0.0 collective-permute-done.9.refs_5_
  41.5 5.8 %collective-permute-done.10.refs_6_ = bf16[64,512]{1,0:T(8,128)(2,1)S(1)} collective-permute-done((bf16[64,512]{1,0:T(8,128)(2,1)S(1)}, bf16[64,512]{1,0:T(8,128)(2,1)S(1)}, u32[]{:S(2)}, u32[]{:S(2)}) %collective-permute-start.10) | collective-permute-done | bytes 65568 | tf_op jit(solution)/shard_map/ppermute | solution.py:32
  47.3 0.0 collective-permute-done.11.refs_7_
  47.3 4.4 %finish.1 = (bf16[4,64,2048]{2,1,0:T(8,128)(2,1)}, bf16[4,64,512]{2,1,0:T(8,128)(2,1)}) custom-call(bf16[64,64]{1,0:T(8,128)(2,1)S(1)} %get-tuple-element.21.back_ref, bf16[4,64,2048]{2,1,0:T(8,128)(2,1)S(1)} %copy-done.5, f32[4,64,2048]{2,1,0:T(8,128)S(1)} %get-tuple-element.22.mixed_ref, f32[4,64,2048]{2,1,0:T(8,128)S(1)} %get-tuple-element.23.lse_ref, ...), custom_call_target="tpu_custom_call" | custom-call | flops 1073741824 | bytes 5242880 | tf_op jit(solution)/shard_map/finish/pallas_call | solution.py:325
Async XLA Ops:
  0.6 1.2 %copy-start.3 = (bf16[4,64,2048]{2,1,0:T(8,128)(2,1)S(1)}, bf16[4,64,2048]{2,1,0:T(8,128)(2,1)}, u32[]{:S(2)}) copy-start(bf16[4,64,2048]{2,1,0:T(8,128)(2,1)} %hidden_ref.1) | copy-start | bytes 3145732
  1.9 0.7 %copy-start.8 = (s32[64]{0:T(128)S(1)}, s32[64]{0:T(128)}, u32[]{:S(2)}) copy-start(s32[64]{0:T(128)} %param.17) | copy-start | bytes 772
  2.5 0.7 %copy-start.9 = (s32[128]{0:T(128)S(1)}, s32[128]{0:T(128)}, u32[]{:S(2)}) copy-start(s32[128]{0:T(128)} %param.18) | copy-start | bytes 1540
  3.8 14.5 %collective-permute-start.3 = (bf16[1040,128]{1,0:T(8,128)(2,1)S(1)}, bf16[1040,128]{1,0:T(8,128)(2,1)S(1)}, u32[]{:S(2)}, u32[]{:S(2)}) collective-permute-start(bf16[1040,128]{1,0:T(8,128)(2,1)S(1)} %get-tuple-element.31), channel_id=1, source_target_pairs={{0,4},{4,0},{8,12},{12,8},{1,5},{5,1},{9,13},{13,9},{2,6},{6,2},{1... | collective-permute-start | bytes 798728 | tf_op jit(solution)/shard_map/ppermute | solution.py:32
  6.9 21.6 %collective-permute-start.4 = (bf16[1040,128]{1,0:T(8,128)(2,1)S(1)}, bf16[1040,128]{1,0:T(8,128)(2,1)S(1)}, u32[]{:S(2)}, u32[]{:S(2)}) collective-permute-start(bf16[1040,128]{1,0:T(8,128)(2,1)S(1)} %get-tuple-element.32), channel_id=1, source_target_pairs={{0,8},{4,12},{8,0},{12,4},{1,9},{5,13},{9,1},{13,5},{2,10},{6,14},... | collective-permute-start | bytes 798728 | tf_op jit(solution)/shard_map/ppermute | solution.py:32
  9.5 19.0 %collective-permute-start.5 = (bf16[1040,128]{1,0:T(8,128)(2,1)S(1)}, bf16[1040,128]{1,0:T(8,128)(2,1)S(1)}, u32[]{:S(2)}, u32[]{:S(2)}) collective-permute-start(bf16[1040,128]{1,0:T(8,128)(2,1)S(1)} %get-tuple-element.33), channel_id=1, source_target_pairs={{0,12},{4,8},{8,4},{12,0},{1,13},{5,9},{9,5},{13,1},{2,14},{6,10},... | collective-permute-start | bytes 798728 | tf_op jit(solution)/shard_map/ppermute | solution.py:32
  9.5 3.4 %copy-start = (bf16[2048,2048]{1,0:T(8,128)(2,1)S(1)}, bf16[2048,2048]{1,0:T(8,128)(2,1)}, u32[]{:S(2)}) copy-start(bf16[2048,2048]{1,0:T(8,128)(2,1)} %projection_ref.1) | copy-start | bytes 25165828
  12.8 1.2 %copy-start.4 = (bf16[4,64,2048]{2,1,0:T(8,128)(2,1)S(1)}, bf16[4,64,2048]{2,1,0:T(8,128)(2,1)}, u32[]{:S(2)}) copy-start(bf16[4,64,2048]{2,1,0:T(8,128)(2,1)} %hidden_ref.1) | copy-start | bytes 3145732
  14.1 4.4 %copy-start.1 = (bf16[64,2,128,128]{3,2,1,0:T(8,128)(2,1)S(1)}, bf16[64,2,128,128]{3,2,1,0:T(8,128)(2,1)}, u32[]{:S(2)}) copy-start(bf16[64,2,128,128]{3,2,1,0:T(8,128)(2,1)} %key_ref.1) | copy-start | bytes 12582916
  14.1 4.4 %copy-start.2 = (bf16[64,2,128,128]{3,2,1,0:T(8,128)(2,1)S(1)}, bf16[64,2,128,128]{3,2,1,0:T(8,128)(2,1)}, u32[]{:S(2)}) copy-start(bf16[64,2,128,128]{3,2,1,0:T(8,128)(2,1)} %value_ref.1) | copy-start | bytes 12582916
  14.1 4.4 %copy-start.5 = (bf16[4,64,2048]{2,1,0:T(8,128)(2,1)S(1)}, bf16[4,64,2048]{2,1,0:T(8,128)(2,1)}, u32[]{:S(2)}) copy-start(bf16[4,64,2048]{2,1,0:T(8,128)(2,1)} %query_ref.3) | copy-start | bytes 3145732
  14.1 4.4 %copy-start.10 = (s32[64]{0:T(128)S(1)}, s32[64]{0:T(128)}, u32[]{:S(2)}) copy-start(s32[64]{0:T(128)} %lengths_ref.1) | copy-start | bytes 772
  16.4 23.7 %collective-permute-start = (bf16[256,512]{1,0:T(8,128)(2,1)S(1)}, bf16[256,512]{1,0:T(8,128)(2,1)S(1)}, u32[]{:S(2)}, u32[]{:S(2)}) collective-permute-start(bf16[256,512]{1,0:T(8,128)(2,1)S(1)} %get-tuple-element.26), channel_id=1, source_target_pairs={{0,3},{1,2},{2,1},{3,0},{4,7},{5,6},{6,5},{7,4},{8,11},{9,10},{10,... | collective-permute-start | bytes 786440 | tf_op jit(solution)/shard_map/ppermute | solution.py:32
  16.9 24.7 %collective-permute-start.1 = (bf16[256,512]{1,0:T(8,128)(2,1)S(1)}, bf16[256,512]{1,0:T(8,128)(2,1)S(1)}, u32[]{:S(2)}, u32[]{:S(2)}) collective-permute-start(bf16[256,512]{1,0:T(8,128)(2,1)S(1)} %get-tuple-element.27), channel_id=1, source_target_pairs={{0,2},{1,3},{2,0},{3,1},{4,6},{5,7},{6,4},{7,5},{8,10},{9,11},{10,... | collective-permute-start | bytes 786440 | tf_op jit(solution)/shard_map/ppermute | solution.py:32
  18.3 10.2 %copy-start.6 = (bf16[32,16,2048]{2,1,0:T(8,128)(2,1)S(1)}, bf16[32,16,2048]{2,1,0:T(8,128)(2,1)}, u32[]{:S(2)}) copy-start(bf16[32,16,2048]{2,1,0:T(8,128)(2,1)} %param.15) | copy-start | bytes 6291460
  18.3 15.5 %copy-start.7 = (bf16[32,16,512]{2,1,0:T(8,128)(2,1)S(1)}, bf16[32,16,512]{2,1,0:T(8,128)(2,1)}, u32[]{:S(2)}) copy-start(bf16[32,16,512]{2,1,0:T(8,128)(2,1)} %param.16) | copy-start | bytes 1572868
  18.3 23.2 %collective-permute-start.2 = (bf16[256,512]{1,0:T(8,128)(2,1)S(1)}, bf16[256,512]{1,0:T(8,128)(2,1)S(1)}, u32[]{:S(2)}, u32[]{:S(2)}) collective-permute-start(bf16[256,512]{1,0:T(8,128)(2,1)S(1)} %get-tuple-element.28), channel_id=1, source_target_pairs={{0,1},{1,0},{2,3},{3,2},{4,5},{5,4},{6,7},{7,6},{8,9},{9,8},{10,11... | collective-permute-start | bytes 786440 | tf_op jit(solution)/shard_map/ppermute | solution.py:32
  29.3 3.4 %collective-permute-start.8 = (f32[16,256]{1,0:T(8,128)S(1)}, f32[16,256]{1,0:T(8,128)S(1)}, u32[]{:S(2)}, u32[]{:S(2)}) collective-permute-start(f32[16,256]{1,0:T(8,128)S(1)} %get-tuple-element.35.refs_0_), channel_id=1, source_target_pairs={{0,3},{1,2},{2,1},{3,0},{4,7},{5,6},{6,5},{7,4},{8,11},{9,10},{10,... | collective-permute-start | bytes 49160 | tf_op jit(solution)/shard_map/ppermute | solution.py:32
  29.3 3.8 %collective-permute-start.7 = (f32[16,256]{1,0:T(8,128)S(1)}, f32[16,256]{1,0:T(8,128)S(1)}, u32[]{:S(2)}, u32[]{:S(2)}) collective-permute-start(f32[16,256]{1,0:T(8,128)S(1)} %get-tuple-element.35.refs_0_), channel_id=1, source_target_pairs={{0,2},{1,3},{2,0},{3,1},{4,6},{5,7},{6,4},{7,5},{8,10},{9,11},{10,... | collective-permute-start | bytes 49160 | tf_op jit(solution)/shard_map/ppermute | solution.py:32
  32.6 1.2 %collective-permute-start.6 = (f32[16,256]{1,0:T(8,128)S(1)}, f32[16,256]{1,0:T(8,128)S(1)}, u32[]{:S(2)}, u32[]{:S(2)}) collective-permute-start(f32[16,256]{1,0:T(8,128)S(1)} %get-tuple-element.35.refs_0_), channel_id=1, source_target_pairs={{0,1},{1,0},{2,3},{3,2},{4,5},{5,4},{6,7},{7,6},{8,9},{9,8},{10,11... | collective-permute-start | bytes 49160 | tf_op jit(solution)/shard_map/ppermute | solution.py:32
  34.1 7.4 %collective-permute-start.9 = (bf16[64,512]{1,0:T(8,128)(2,1)S(1)}, bf16[64,512]{1,0:T(8,128)(2,1)S(1)}, u32[]{:S(2)}, u32[]{:S(2)}) collective-permute-start(bf16[64,512]{1,0:T(8,128)(2,1)S(1)} %get-tuple-element.37), channel_id=1, source_target_pairs={{0,4},{4,0},{8,12},{12,8},{1,5},{5,1},{9,13},{13,9},{2,6},{6,2},{1... | collective-permute-start | bytes 196616 | tf_op jit(solution)/shard_map/ppermute | solution.py:32
  39.0 8.3 %collective-permute-start.10 = (bf16[64,512]{1,0:T(8,128)(2,1)S(1)}, bf16[64,512]{1,0:T(8,128)(2,1)S(1)}, u32[]{:S(2)}, u32[]{:S(2)}) collective-permute-start(bf16[64,512]{1,0:T(8,128)(2,1)S(1)} %get-tuple-element.38), channel_id=1, source_target_pairs={{0,8},{4,12},{8,0},{12,4},{1,9},{5,13},{9,1},{13,5},{2,10},{6,14},... | collective-permute-start | bytes 196616 | tf_op jit(solution)/shard_map/ppermute | solution.py:32
  40.1 7.2 %collective-permute-start.11 = (bf16[64,512]{1,0:T(8,128)(2,1)S(1)}, bf16[64,512]{1,0:T(8,128)(2,1)S(1)}, u32[]{:S(2)}, u32[]{:S(2)}) collective-permute-start(bf16[64,512]{1,0:T(8,128)(2,1)S(1)} %get-tuple-element.39), channel_id=1, source_target_pairs={{0,12},{4,8},{8,4},{12,0},{1,13},{5,9},{9,5},{13,1},{2,14},{6,10},... | collective-permute-start | bytes 196616 | tf_op jit(solution)/shard_map/ppermute | solution.py:32

commit v3 on v2

--- a/solution.py
+++ b/solution.py
@@ -42,11 +42,25 @@
     return jnp.sum(jnp.where(diagonal, row, 0.0), axis=1, keepdims=True)
 
 
-def route_kernel(groups, cap, entries, requests_ref, store_ref, hidden_ref, *outs):
-    blocks, back_ref = outs[:groups], outs[groups]
+def route_kernel(order, cap, entries, requests_hbm, store_hbm, hidden_hbm, *refs):
+    groups = len(order)
+    blocks, back_ref = refs[:groups], refs[groups]
+    requests_ref, store_ref, hidden_ref, index_sems, hidden_sems = refs[groups + 1 :]
     steps, seqs, features = hidden_ref.shape
     tiles = features // LANES
+    index_copies = [
+        pltpu.make_async_copy(requests_hbm, requests_ref, index_sems.at[0]),
+        pltpu.make_async_copy(store_hbm, store_ref, index_sems.at[1]),
+    ]
+    hidden_copies = [
+        pltpu.make_async_copy(hidden_hbm.at[s], hidden_ref.at[s], hidden_sems.at[s])
+        for s in range(steps)
+    ]
+    for copy in index_copies + hidden_copies:
+        copy.start()
     me = lax.axis_index("dp")
+    for copy in index_copies:
+        copy.wait()
     store_col = column(store_ref[...].astype(F32))
     adapters = store_col.shape[0]
     rows = jnp.sum(
@@ -56,11 +70,14 @@
     ).astype(jnp.int32)
     owner = lax.div(rows, jnp.int32(entries))
     slot_col = column((rows - owner * entries).astype(F32))
-    distance = jnp.bitwise_xor(owner, me).astype(F32)
-    distance_col = column(distance)
-    before = (distance_col == distance) & (iota((seqs, seqs), 0) < iota((seqs, seqs), 1))
+    distance = jnp.bitwise_xor(owner, me)
+    turn = jnp.zeros(distance.shape, F32)
+    for k, at in enumerate(order):
+        turn = jnp.where(distance == at, float(k), turn)
+    turn_col = column(turn)
+    before = (turn_col == turn) & (iota((seqs, seqs), 0) < iota((seqs, seqs), 1))
     rank = jnp.sum(jnp.where(before, 1.0, 0.0), axis=0, keepdims=True)
-    bucket = distance * cap + rank
+    bucket = turn * cap + rank
     bucket_col = column(bucket).astype(jnp.int32)
     bucket = bucket.astype(jnp.int32)
     placed = jnp.where(iota((groups * cap, seqs), 0) == bucket, 1.0, 0.0).astype(BF16)
@@ -70,6 +87,7 @@
         slots = jnp.sum(jnp.where(bucket_col == spot, slot_col, 0.0), axis=0, keepdims=True)
         blocks[k][steps * tiles * cap :, :] = jnp.broadcast_to(slots, (cap, LANES)).astype(BF16)
     for s in range(steps):
+        hidden_copies[s].wait()
         picked = jnp.dot(placed, hidden_ref[s], preferred_element_type=F32).astype(BF16)
         for k in range(groups):
             for c in range(tiles):
@@ -79,14 +97,23 @@
                 ]
 
 
-def route(requests, store, hidden, groups, cap, entries):
+def route(requests, store, hidden, order, cap, entries):
+    groups = len(order)
     steps, seqs, features = hidden.shape
     rows = (steps * (features // LANES) + 1) * cap
     return pl.pallas_call(
-        functools.partial(route_kernel, groups, cap, entries),
+        functools.partial(route_kernel, order, cap, entries),
         out_shape=[jax.ShapeDtypeStruct((rows, LANES), BF16)] * groups
         + [jax.ShapeDtypeStruct((seqs, groups * cap), BF16)],
-        compiler_params=params(10),
+        in_specs=[pl.BlockSpec(memory_space=pltpu.HBM)] * 3,
+        scratch_shapes=[
+            pltpu.VMEM((1, seqs), jnp.int32),
+            pltpu.VMEM((1, store.shape[0]), jnp.int32),
+            pltpu.VMEM(hidden.shape, BF16),
+            pltpu.SemaphoreType.DMA((2,)),
+            pltpu.SemaphoreType.DMA((steps,)),
+        ],
+        compiler_params=params(62),
         cost_estimate=cost(
             2 * groups * cap * seqs * steps * features, 4 * steps * seqs * features
         ),
@@ -96,8 +123,9 @@
 
 def base_kernel(size, hidden_ref, projection_ref, *outs):
     width = outs[0].shape[1]
+    half = size // 2
     me = lax.axis_index("tp")
-    for k in list(range(1, size)) + [0]:
+    for k in list(range(half, size)) + list(range(half)):
         first = pl.multiple_of(jnp.bitwise_xor(me, k) * width, width)
         part = jnp.dot(
             hidden_ref[...], projection_ref[:, pl.ds(first, width)], preferred_element_type=F32
@@ -108,10 +136,11 @@
 def base(hidden, projection, size):
     rows, _ = hidden.shape
     width = projection.shape[1] // size
+    half = size // 2
     return pl.pallas_call(
         functools.partial(base_kernel, size),
-        out_shape=[jax.ShapeDtypeStruct((rows, width), F32)]
-        + [jax.ShapeDtypeStruct((rows, width), BF16)] * (size - 1),
+        out_shape=[jax.ShapeDtypeStruct((rows, width), F32)] * half
+        + [jax.ShapeDtypeStruct((rows, width), BF16)] * half,
         compiler_params=params(20),
         cost_estimate=cost(0, 4096),
         name="base",
@@ -125,6 +154,10 @@
     rows = steps * share
     first = pl.program_id(0) * chunk
     scaling = 1.0 / math.sqrt(size)
+
+    @pl.when(first == 0)
+    def _():
+        lse_ref[...] = jnp.zeros_like(lse_ref)
 
     def lanes(g, h):
         return slice((g * share + h) * size, (g * share + h + 1) * size)
@@ -152,16 +185,21 @@
         for u, (i, g) in enumerate(units)
     ]
     mixed = jnp.concatenate(mixed, axis=0) * (1.0 / total)
-    lse = jnp.broadcast_to(top + jnp.log(total), mixed.shape)
+    lse = top + jnp.log(total)
+    seqs = pl.num_programs(0) * chunk
+    lane = lax.rem(iota((rows, LANES), 1), seqs)
+    for g in range(heads):
+        packed = lse_ref[g * rows : (g + 1) * rows, :]
+        for i in range(chunk):
+            u = i * heads + g
+            packed = jnp.where(lane == first + i, lse[u * rows : (u + 1) * rows], packed)
+        lse_ref[g * rows : (g + 1) * rows, :] = packed
     mixed = mixed.reshape(chunk, heads, steps, share, size)
-    lse = lse.reshape(chunk, heads, steps, share, size)
     for s in range(steps):
         for g in range(heads):
             mixed_by_head = jnp.swapaxes(mixed[:, g, s], 0, 1)
-            lse_by_head = jnp.swapaxes(lse[:, g, s], 0, 1)
             for h in range(share):
                 mixed_ref[s, :, lanes(g, h)] = mixed_by_head[h]
-                lse_ref[s, :, lanes(g, h)] = lse_by_head[h]
 
 
 def past(lengths, queries, keys, values):
@@ -181,12 +219,12 @@
             ],
             out_specs=[
                 pl.BlockSpec((steps, chunk, width), lambda i, n: (0, i, 0)),
-                pl.BlockSpec((steps, chunk, width), lambda i, n: (0, i, 0)),
+                pl.BlockSpec((steps * width // size, LANES), lambda i, n: (0, 0)),
             ],
         ),
         out_shape=[
             jax.ShapeDtypeStruct((steps, seqs, width), F32),
-            jax.ShapeDtypeStruct((steps, seqs, width), F32),
+            jax.ShapeDtypeStruct((steps * width // size, LANES), F32),
         ],
         compiler_params=params(16),
         cost_estimate=cost(0, 4096),
@@ -287,36 +325,57 @@
             base = base + summand[rows, :].astype(F32)
         new.append((base + update).astype(BF16))
         new_ref[s] = new[s]
-    ones = jnp.ones((2 * size, size), BF16)
+    same = lax.rem(iota((seqs, LANES), 1), jnp.int32(seqs)) == iota((seqs, LANES), 0)
+
+    def over_steps(parts, combine):
+        whole = functools.reduce(combine, parts)
+        turned = [pltpu.roll(whole, shift, 1) for shift in range(seqs, LANES, seqs)]
+        return functools.reduce(combine, turned, whole)
+
     for g in range(heads):
         left = g * 2 * size
-        keys = [n[:, left : left + size].astype(F32) * scaling for n in new]
-        values = [n[:, left + size : left + 2 * size].astype(F32) for n in new]
+        keys = jnp.concatenate([n[:, left : left + size] for n in new], axis=0)
+        values = jnp.concatenate([n[:, left + size : left + 2 * size] for n in new], axis=0)
         for s in range(steps):
+            lanes = [
+                slice((g * share + h) * size, (g * share + h + 1) * size) for h in range(share)
+            ]
+            count = pl.cdiv((s + 1) * seqs, LANES)
+            q = jnp.concatenate([query_ref[s, :, cut] for cut in lanes], axis=0)
+            scores = lax.dot_general(
+                q, keys[: count * LANES], NT, preferred_element_type=F32
+            )
+            fresh = []
+            for c in range(count):
+                block = scores[:, c * LANES : (c + 1) * LANES].reshape(share, seqs, LANES)
+                row = jnp.sum(jnp.where(same[None], block, 0.0), axis=1) * scaling
+                step = lax.div(iota((share, LANES), 1), jnp.int32(seqs)) + c * (LANES // seqs)
+                fresh.append(jnp.where(step <= s, row, -jnp.inf))
+            first = (g * steps + s) * share
+            lse = lse_ref[first : first + share, :]
+            top = jnp.maximum(over_steps(fresh, jnp.maximum), lse)
+            old = jnp.exp(lse - top)
+            raised = [jnp.exp(row - top) for row in fresh]
+            scale = 1.0 / (over_steps(raised, jnp.add) + old)
+            old = jnp.transpose(old * scale)[:seqs, :]
+            weights = jnp.concatenate(
+                [
+                    jnp.concatenate(
+                        [
+                            jnp.where(same, (row * scale)[h : h + 1, :], 0.0).astype(BF16)
+                            for row in raised
+                        ],
+                        axis=1,
+                    )
+                    for h in range(share)
+                ],
+                axis=0,
+            )
+            mixed = jnp.dot(weights, values[: count * LANES], preferred_element_type=F32)
             for h in range(share):
-                lanes = slice((g * share + h) * size, (g * share + h + 1) * size)
-                q = query_ref[s, :, lanes].astype(F32)
-                halves = []
-                for t in range(s + 1):
-                    product = q * keys[t]
-                    high = product.astype(BF16)
-                    low = (product - high.astype(F32)).astype(BF16)
-                    halves.append(jnp.concatenate([high, low], axis=1))
-                halves = jnp.concatenate(halves, axis=0)
-                scores = jnp.dot(halves, ones, preferred_element_type=F32)
-                scores = [scores[t * seqs : (t + 1) * seqs] for t in range(s + 1)]
-                lse = lse_ref[s, :, lanes]
-                top = lse
-                for score in scores:
-                    top = jnp.maximum(top, score)
-                old = jnp.exp(lse - top)
-                total = old
-                mixed = mixed_ref[s, :, lanes] * old
-                for t in range(s + 1):
-                    raised = jnp.exp(scores[t] - top)
-                    total = total + raised
-                    mixed = mixed + raised * values[t]
-                out_ref[s, :, lanes] = (mixed / total).astype(BF16)
+                total = mixed[h * seqs : (h + 1) * seqs]
+                total = total + mixed_ref[s, :, lanes[h]] * old[:, h : h + 1]
+                out_ref[s, :, lanes[h]] = total.astype(BF16)
 
 
 def finish(back, summands, queries, mixed, lse, deltas, cap, heads):
@@ -357,25 +416,35 @@
     entries = adapter_shrink_weight.shape[0]
     heads = cached_key_rows.shape[1]
 
-    routed = route(requests, adapter_store_row, hidden, groups, cap, entries)
-    blocks, back = routed[:groups], routed[groups]
-    over_dp = [None] + [swap("dp", groups, k) for k in range(1, groups)]
-    over_tp = [None] + [swap("tp", size, k) for k in range(1, size)]
-    got = {k: over_dp[k](blocks[k]) for k in reversed(range(1, groups))}
+    order = [0] + sorted(range(1, groups), key=lambda k: -k.bit_length())
+    *blocks, back = route(requests, adapter_store_row, hidden, order, cap, entries)
+    over_dp = [swap("dp", groups, k) for k in order[1:]]
+    over_tp = [swap("tp", size, k) for k in range(1, size)]
+    got = [move(block) for move, block in zip(over_dp, blocks[1:])]
 
     late_hidden, _ = lax.optimization_barrier((hidden, back))
-    parts = base(late_hidden.reshape(steps * seqs, features), projection, size)
-    summands = [parts[0]] + [over_tp[k](parts[k]) for k in reversed(range(1, size))]
+    terms = base(late_hidden.reshape(steps * seqs, features), projection, size)
+    distance = size // 2
+    move = swap("tp", size, distance)
+    terms = [[terms[k], move(terms[distance + k])] for k in range(distance)]
 
     mixed, lse = past(lengths, queries, cached_key_rows, cached_value_rows)
 
-    block, _ = lax.optimization_barrier((blocks[0], (lse, parts[0])))
-    gathered = [block] + [got[k] for k in range(1, groups)]
-    shrunk, slots = shrink(adapter_shrink_weight, gathered, steps, cap)
-    parts = [shrunk] + [over_tp[k](shrunk) for k in range(1, size)]
-    deltas = expand(adapter_expand_weight, parts, slots, groups)
-    deltas = [deltas[0]] + [over_dp[k](deltas[k]) for k in range(1, groups)]
-    return tuple(finish(back, summands, queries, mixed, lse, deltas, cap, heads))
+    block, _ = lax.optimization_barrier((blocks[0], lse))
+    shrunk, slots = shrink(adapter_shrink_weight, [block] + got, steps, cap)
+    partial = [shrunk] + [move(shrunk) for move in over_tp]
+    terms, _ = lax.optimization_barrier((terms, shrunk))
+    while distance > 1:
+        distance //= 2
+        move = swap("tp", size, distance)
+        for k in range(distance):
+            moved = sum(term.astype(F32) for term in terms[distance + k]).astype(BF16)
+            terms[k] = terms[k] + [move(moved)]
+    slots, _ = lax.optimization_barrier((slots, moved))
+    deltas = expand(adapter_expand_weight, partial, slots, groups)
+    returned = [deltas[0]] + [move(delta) for move, delta in zip(over_dp, deltas[1:])]
+    summands = terms[0]
+    return tuple(finish(back, summands, queries, mixed, lse, returned, cap, heads))
 
 
 def solution(mesh):

time: 51.9 us -> 50.9 us (0.981)
  local copies, waits for them, and re-layouts: 7.16 us -> 4.64 us
  Pallas kernels: 14.5 us -> 16 us
  starting transfers between devices: 16.8 us -> 15.9 us
  waiting for transfers between devices: 12.5 us -> 13.4 us
    unnamed x22 -> x20, local copies, waits for them, and re-layouts: 7.16 us -> 4.64 us
    pallas_call x1, Pallas kernels: 0.61 us -> 3.07 us  [route(): pl.pallas_call(functools.partial(route_kernel, order, cap, entries), out_...]
    ppermute x12, waiting for transfers between devices: 12.5 us -> 13.4 us  [swap(): return lambda value: lax.ppermute(value, axis, pairs)]
    ppermute x12, starting transfers between devices: 16.8 us -> 15.9 us  [swap(): return lambda value: lax.ppermute(value, axis, pairs)]
    pallas_call x1, Pallas kernels: 4.36 us -> 3.59 us  [finish(): pl.pallas_call(functools.partial(finish_kernel, len(deltas), len(summands...]
  transfers between devices with their start and end apart: 12 -> 12, of which waited for: 5 -> 7; matrix products, arithmetic and copies ran while one was open for 0% -> 0% of each run, Pallas kernels for 18% -> 18%
where the time goes in v3:
time: 50.9 us; the launch traced here: 50.7 us
  Pallas kernels  16 us (31%)
  starting transfers between devices  15.9 us (31%)
  waiting for transfers between devices  13.4 us (26%)
  local copies, waits for them, and re-layouts  4.64 us (9%)
  between operations  0.73 us (1%)
    ppermute x12, starting transfers between devices, swap(): return lambda value: lax.ppermute(value, axis, pairs)  15.9 us
    ppermute x12, waiting for transfers between devices, swap(): return lambda value: lax.ppermute(value, axis, pairs)  13.4 us
    pallas_call x1, Pallas kernels, past(): pl.pallas_call(past_kernel, grid_spec=pltpu.PrefetchScalarGridSpec(num_sc...  5.88 us
    unnamed x20, local copies, waits for them, and re-layouts  4.64 us
    pallas_call x1, Pallas kernels, finish(): pl.pallas_call(functools.partial(finish_kernel, len(deltas), len(summands...  3.59 us
    pallas_call x1, Pallas kernels, route(): pl.pallas_call(functools.partial(route_kernel, order, cap, entries), out_...  3.07 us
    pallas_call x1, Pallas kernels, base(): pl.pallas_call(functools.partial(base_kernel, size), out_shape=[jax.Shape...  2.36 us
  transfers between devices with their start and end apart: 12, of which 7 were waited for; matrix products, arithmetic and copies ran while one was open for 0% of the time, Pallas kernels for 18%

profile of v3, /device:TPU:0, one launch (start us, length us, event | category | flops | bytes accessed | tf_op | source)
XLA Modules:
  0.0 50.7 jit_solution(2033277369405264703)
XLA Ops:
  0.6 3.1 %route.1 = (bf16[1040,128]{1,0:T(8,128)(2,1)}, bf16[1040,128]{1,0:T(8,128)(2,1)}, bf16[1040,128]{1,0:T(8,128)(2,1)}, bf16[1040,128]{1,0:T(8,128)(2,1)}, bf16[64,64]{1,0:T(8,128)(2,1)}) custom-call(s32[1,64]{1,0:T(1,128)} %bitcast.8, s32[1,128]{1,0:T(1,128)} %bitcast.9, bf16[4,64,2048]{2,1,0:T(8,128)(2,1)} %hidden_hbm.1), custom_call_target="tpu_custom_call" | custom-call | flops 67108864 | bytes 2097152 | tf_op jit(solution)/shard_map/route/pallas_call | solution.py:104
  3.7 4.1 %collective-permute-start.2 = (bf16[1040,128]{1,0:T(8,128)(2,1)}, bf16[1040,128]{1,0:T(8,128)(2,1)S(1)}, u32[]{:S(2)}, u32[]{:S(2)}) collective-permute-start(bf16[1040,128]{1,0:T(8,128)(2,1)} %get-tuple-element.36), channel_id=1, source_target_pairs={{0,8},{4,12},{8,0},{12,4},{1,9},{5,13},{9,1},{13,5},{2,10},{6,14},... | collective-permute-start | bytes 798728 | tf_op jit(solution)/shard_map/ppermute | solution.py:32
  7.8 1.3 %collective-permute-start.3 = (bf16[1040,128]{1,0:T(8,128)(2,1)}, bf16[1040,128]{1,0:T(8,128)(2,1)S(1)}, u32[]{:S(2)}, u32[]{:S(2)}) collective-permute-start(bf16[1040,128]{1,0:T(8,128)(2,1)} %get-tuple-element.37), channel_id=1, source_target_pairs={{0,12},{4,8},{8,4},{12,0},{1,13},{5,9},{9,5},{13,1},{2,14},{6,10},... | collective-permute-start | bytes 798728 | tf_op jit(solution)/shard_map/ppermute | solution.py:32
  9.2 0.2 collective-permute-start.4
  9.4 0.0 copy-start
  9.4 3.4 %copy-done = bf16[2048,2048]{1,0:T(8,128)(2,1)S(1)} copy-done((bf16[2048,2048]{1,0:T(8,128)(2,1)S(1)}, bf16[2048,2048]{1,0:T(8,128)(2,1)}, u32[]{:S(2)}) %copy-start) | copy-done | bytes 8388632
  12.8 0.0 copy-start.4
  12.8 1.2 %copy-done.4 = bf16[4,64,2048]{2,1,0:T(8,128)(2,1)S(1)} copy-done((bf16[4,64,2048]{2,1,0:T(8,128)(2,1)S(1)}, bf16[4,64,2048]{2,1,0:T(8,128)(2,1)}, u32[]{:S(2)}) %copy-start.4) | copy-done | bytes 1048600
  14.0 0.0 copy-start.1
  14.0 0.0 copy-start.2
  14.0 0.0 copy-start.3
  14.0 0.0 copy-start.9
  14.0 2.4 %base.1 = (f32[256,512]{1,0:T(8,128)S(1)}, f32[256,512]{1,0:T(8,128)S(1)}, bf16[256,512]{1,0:T(8,128)(2,1)S(1)}, bf16[256,512]{1,0:T(8,128)(2,1)S(1)}) custom-call(bf16[256,2048]{1,0:T(8,128)(2,1)S(1)} %bitcast.5, bf16[2048,2048]{1,0:T(8,128)(2,1)S(1)} %copy-done), custom_call_target="tpu_custom_call" | custom-call | bytes 4096 | tf_op jit(solution)/shard_map/base/pallas_call | solution.py:140
  16.4 1.6 %collective-permute-start = (bf16[256,512]{1,0:T(8,128)(2,1)S(1)}, bf16[256,512]{1,0:T(8,128)(2,1)S(1)}, u32[]{:S(2)}, u32[]{:S(2)}) collective-permute-start(bf16[256,512]{1,0:T(8,128)(2,1)S(1)} %get-tuple-element.31), channel_id=1, source_target_pairs={{0,2},{1,3},{2,0},{3,1},{4,6},{5,7},{6,4},{7,5},{8,10},{9,11},{10,... | collective-permute-start | bytes 786440 | tf_op jit(solution)/shard_map/ppermute | solution.py:32
  17.9 0.0 copy-start.5
  17.9 0.0 copy-start.7
  17.9 0.5 %collective-permute-start.1 = (bf16[256,512]{1,0:T(8,128)(2,1)S(1)}, bf16[256,512]{1,0:T(8,128)(2,1)S(1)}, u32[]{:S(2)}, u32[]{:S(2)}) collective-permute-start(bf16[256,512]{1,0:T(8,128)(2,1)S(1)} %get-tuple-element.33), channel_id=1, source_target_pairs={{0,2},{1,3},{2,0},{3,1},{4,6},{5,7},{6,4},{7,5},{8,10},{9,11},{10,... | collective-permute-start | bytes 786440 | tf_op jit(solution)/shard_map/ppermute | solution.py:32
  18.5 0.0 copy-done.1
  18.5 0.0 copy-done.2
  18.5 0.0 copy-done.3
  18.5 0.0 copy-done.9
  18.5 5.9 %past.1 = (f32[4,64,2048]{2,1,0:T(8,128)S(1)}, f32[64,128]{1,0:T(8,128)S(1)}) custom-call(s32[64]{0:T(128)S(1)} %copy-done.9, bf16[4,64,2048]{2,1,0:T(8,128)(2,1)S(1)} %copy-done.1, bf16[64,2,128,128]{3,2,1,0:T(8,128)(2,1)S(1)} %copy-done.2, bf16[64,2,128,128]{3,2,1,0:T(8,128)(2,1)S(1)} %copy-done.3), custom_call_target="tpu_custom_call" | custom-call | bytes 4096 | tf_op jit(solution)/shard_map/past/pallas_call | solution.py:210
  24.4 0.0 copy-start.6
  24.4 0.0 copy-start.8
  24.4 2.3 %collective-permute-done.2.refs_1_ = bf16[1040,128]{1,0:T(8,128)(2,1)S(1)} collective-permute-done((bf16[1040,128]{1,0:T(8,128)(2,1)}, bf16[1040,128]{1,0:T(8,128)(2,1)S(1)}, u32[]{:S(2)}, u32[]{:S(2)}) %collective-permute-start.2) | collective-permute-done | bytes 266272 | tf_op jit(solution)/shard_map/ppermute | solution.py:32
  26.7 0.0 collective-permute-done.3.refs_2_
  26.7 0.5 %collective-permute-done.4.refs_3_ = bf16[1040,128]{1,0:T(8,128)(2,1)S(1)} collective-permute-done((bf16[1040,128]{1,0:T(8,128)(2,1)}, bf16[1040,128]{1,0:T(8,128)(2,1)S(1)}, u32[]{:S(2)}, u32[]{:S(2)}) %collective-permute-start.4) | collective-permute-done | bytes 266272 | tf_op jit(solution)/shard_map/ppermute | solution.py:32
  27.2 0.0 copy-done.5
  27.2 0.0 copy-done.7
  27.2 0.8 %shrink.1 = (f32[16,256]{1,0:T(8,128)S(1)}, s32[1,256]{1,0:T(1,128)S(1)}) custom-call(bf16[512,2048]{1,0:T(8,128)(2,1)S(1)} %bitcast.6, bf16[1040,128]{1,0:T(8,128)(2,1)S(1)} %copy-done.7, bf16[1040,128]{1,0:T(8,128)(2,1)S(1)} %collective-permute-done.2.refs_1_, bf16[1040,128]{1,0:T(8,128)(2,1)S(1)} %collective-permute-done.3.refs_2_, ...), custom_call_target="tpu_custom_call" | custom-call | flops 536870912 | bytes 3145728 | tf_op jit(solution)/shard_map/shrink/pallas_call | solution.py:260
  28.0 0.0 collective-permute-done.refs_1_
  28.0 1.5 %collective-permute-done.1 = bf16[256,512]{1,0:T(8,128)(2,1)S(1)} collective-permute-done((bf16[256,512]{1,0:T(8,128)(2,1)S(1)}, bf16[256,512]{1,0:T(8,128)(2,1)S(1)}, u32[]{:S(2)}, u32[]{:S(2)}) %collective-permute-start.1) | collective-permute-done | bytes 262176 | tf_op jit(solution)/shard_map/ppermute | solution.py:32
  29.5 0.1 add_convert_fusion
  29.6 0.1 collective-permute-start.5
  29.7 0.5 collective-permute-start.6
  30.2 1.5 %collective-permute-start.7 = (f32[16,256]{1,0:T(8,128)S(1)}, f32[16,256]{1,0:T(8,128)S(1)}, u32[]{:S(2)}, u32[]{:S(2)}) collective-permute-start(f32[16,256]{1,0:T(8,128)S(1)} %get-tuple-element.39.refs_0_), channel_id=1, source_target_pairs={{0,2},{1,3},{2,0},{3,1},{4,6},{5,7},{6,4},{7,5},{8,10},{9,11},{10,... | collective-permute-start | bytes 49160 | tf_op jit(solution)/shard_map/ppermute | solution.py:32
  31.7 0.0 collective-permute-start.8
  31.7 0.0 collective-permute-done.6.refs_1_
  31.7 2.2 %collective-permute-done.7.refs_2_ = f32[16,256]{1,0:T(8,128)S(1)} collective-permute-done((f32[16,256]{1,0:T(8,128)S(1)}, f32[16,256]{1,0:T(8,128)S(1)}, u32[]{:S(2)}, u32[]{:S(2)}) %collective-permute-start.7) | collective-permute-done | bytes 16416 | tf_op jit(solution)/shard_map/ppermute | solution.py:32
  33.9 1.1 %collective-permute-done.8.refs_3_ = f32[16,256]{1,0:T(8,128)S(1)} collective-permute-done((f32[16,256]{1,0:T(8,128)S(1)}, f32[16,256]{1,0:T(8,128)S(1)}, u32[]{:S(2)}, u32[]{:S(2)}) %collective-permute-start.8) | collective-permute-done | bytes 16416 | tf_op jit(solution)/shard_map/ppermute | solution.py:32
  35.0 0.0 copy-done.6
  35.0 0.3 expand.1
  35.3 2.7 %collective-permute-start.10 = (bf16[64,512]{1,0:T(8,128)(2,1)S(1)}, bf16[64,512]{1,0:T(8,128)(2,1)S(1)}, u32[]{:S(2)}, u32[]{:S(2)}) collective-permute-start(bf16[64,512]{1,0:T(8,128)(2,1)S(1)} %get-tuple-element.48), channel_id=1, source_target_pairs={{0,12},{4,8},{8,4},{12,0},{1,13},{5,9},{9,5},{13,1},{2,14},{6,10},... | collective-permute-start | bytes 196616 | tf_op jit(solution)/shard_map/ppermute | solution.py:32
  38.1 3.4 %collective-permute-start.11 = (bf16[64,512]{1,0:T(8,128)(2,1)S(1)}, bf16[64,512]{1,0:T(8,128)(2,1)S(1)}, u32[]{:S(2)}, u32[]{:S(2)}) collective-permute-start(bf16[64,512]{1,0:T(8,128)(2,1)S(1)} %get-tuple-element.49), channel_id=1, source_target_pairs={{0,4},{4,0},{8,12},{12,8},{1,5},{5,1},{9,13},{13,9},{2,6},{6,2},{1... | collective-permute-start | bytes 196616 | tf_op jit(solution)/shard_map/ppermute | solution.py:32
  41.4 0.0 collective-permute-start.9
  41.5 0.0 collective-permute-done.10.refs_5_
  41.5 2.2 %collective-permute-done.11.refs_6_ = bf16[64,512]{1,0:T(8,128)(2,1)S(1)} collective-permute-done((bf16[64,512]{1,0:T(8,128)(2,1)S(1)}, bf16[64,512]{1,0:T(8,128)(2,1)S(1)}, u32[]{:S(2)}, u32[]{:S(2)}) %collective-permute-start.11) | collective-permute-done | bytes 65568 | tf_op jit(solution)/shard_map/ppermute | solution.py:32
  43.7 3.4 %collective-permute-done.9.refs_4_ = bf16[64,512]{1,0:T(8,128)(2,1)S(1)} collective-permute-done((bf16[64,512]{1,0:T(8,128)(2,1)S(1)}, bf16[64,512]{1,0:T(8,128)(2,1)S(1)}, u32[]{:S(2)}, u32[]{:S(2)}) %collective-permute-start.9) | collective-permute-done | bytes 65568 | tf_op jit(solution)/shard_map/ppermute | solution.py:32
  47.1 0.0 collective-permute-done.5.refs_2_
  47.1 0.0 copy-done.8
  47.1 3.6 %finish.1 = (bf16[4,64,2048]{2,1,0:T(8,128)(2,1)}, bf16[4,64,512]{2,1,0:T(8,128)(2,1)}) custom-call(bf16[64,64]{1,0:T(8,128)(2,1)S(1)} %copy-done.8, bf16[4,64,2048]{2,1,0:T(8,128)(2,1)S(1)} %copy-done.1, f32[4,64,2048]{2,1,0:T(8,128)S(1)} %get-tuple-element.27.mixed_ref, f32[64,128]{1,0:T(8,128)S(1)} %get-tuple-element.28.lse_ref, ...), custom_call_target="tpu_custom_call" | custom-call | flops 1073741824 | bytes 5242880 | tf_op jit(solution)/shard_map/finish/pallas_call | solution.py:384
Async XLA Ops:
  3.7 23.0 %collective-permute-start.2 = (bf16[1040,128]{1,0:T(8,128)(2,1)}, bf16[1040,128]{1,0:T(8,128)(2,1)S(1)}, u32[]{:S(2)}, u32[]{:S(2)}) collective-permute-start(bf16[1040,128]{1,0:T(8,128)(2,1)} %get-tuple-element.36), channel_id=1, source_target_pairs={{0,8},{4,12},{8,0},{12,4},{1,9},{5,13},{9,1},{13,5},{2,10},{6,14},... | collective-permute-start | bytes 798728 | tf_op jit(solution)/shard_map/ppermute | solution.py:32
  7.8 18.9 %collective-permute-start.3 = (bf16[1040,128]{1,0:T(8,128)(2,1)}, bf16[1040,128]{1,0:T(8,128)(2,1)S(1)}, u32[]{:S(2)}, u32[]{:S(2)}) collective-permute-start(bf16[1040,128]{1,0:T(8,128)(2,1)} %get-tuple-element.37), channel_id=1, source_target_pairs={{0,12},{4,8},{8,4},{12,0},{1,13},{5,9},{9,5},{13,1},{2,14},{6,10},... | collective-permute-start | bytes 798728 | tf_op jit(solution)/shard_map/ppermute | solution.py:32
  9.2 18.1 %collective-permute-start.4 = (bf16[1040,128]{1,0:T(8,128)(2,1)}, bf16[1040,128]{1,0:T(8,128)(2,1)S(1)}, u32[]{:S(2)}, u32[]{:S(2)}) collective-permute-start(bf16[1040,128]{1,0:T(8,128)(2,1)} %get-tuple-element.38), channel_id=1, source_target_pairs={{0,4},{4,0},{8,12},{12,8},{1,5},{5,1},{9,13},{13,9},{2,6},{6,2},{1... | collective-permute-start | bytes 798728 | tf_op jit(solution)/shard_map/ppermute | solution.py:32
  9.4 3.4 %copy-start = (bf16[2048,2048]{1,0:T(8,128)(2,1)S(1)}, bf16[2048,2048]{1,0:T(8,128)(2,1)}, u32[]{:S(2)}) copy-start(bf16[2048,2048]{1,0:T(8,128)(2,1)} %projection_ref.1) | copy-start | bytes 25165828
  12.8 1.2 %copy-start.4 = (bf16[4,64,2048]{2,1,0:T(8,128)(2,1)S(1)}, bf16[4,64,2048]{2,1,0:T(8,128)(2,1)}, u32[]{:S(2)}) copy-start(bf16[4,64,2048]{2,1,0:T(8,128)(2,1)} %hidden_hbm.1) | copy-start | bytes 3145732
  14.0 4.5 %copy-start.1 = (bf16[4,64,2048]{2,1,0:T(8,128)(2,1)S(1)}, bf16[4,64,2048]{2,1,0:T(8,128)(2,1)}, u32[]{:S(2)}) copy-start(bf16[4,64,2048]{2,1,0:T(8,128)(2,1)} %query_ref.3) | copy-start | bytes 3145732
  14.0 4.5 %copy-start.2 = (bf16[64,2,128,128]{3,2,1,0:T(8,128)(2,1)S(1)}, bf16[64,2,128,128]{3,2,1,0:T(8,128)(2,1)}, u32[]{:S(2)}) copy-start(bf16[64,2,128,128]{3,2,1,0:T(8,128)(2,1)} %key_ref.1) | copy-start | bytes 12582916
  14.0 4.5 %copy-start.3 = (bf16[64,2,128,128]{3,2,1,0:T(8,128)(2,1)S(1)}, bf16[64,2,128,128]{3,2,1,0:T(8,128)(2,1)}, u32[]{:S(2)}) copy-start(bf16[64,2,128,128]{3,2,1,0:T(8,128)(2,1)} %value_ref.1) | copy-start | bytes 12582916
  14.0 4.5 %copy-start.9 = (s32[64]{0:T(128)S(1)}, s32[64]{0:T(128)}, u32[]{:S(2)}) copy-start(s32[64]{0:T(128)} %lengths_ref.1) | copy-start | bytes 772
  16.4 11.6 %collective-permute-start = (bf16[256,512]{1,0:T(8,128)(2,1)S(1)}, bf16[256,512]{1,0:T(8,128)(2,1)S(1)}, u32[]{:S(2)}, u32[]{:S(2)}) collective-permute-start(bf16[256,512]{1,0:T(8,128)(2,1)S(1)} %get-tuple-element.31), channel_id=1, source_target_pairs={{0,2},{1,3},{2,0},{3,1},{4,6},{5,7},{6,4},{7,5},{8,10},{9,11},{10,... | collective-permute-start | bytes 786440 | tf_op jit(solution)/shard_map/ppermute | solution.py:32
  17.9 9.3 %copy-start.5 = (bf16[32,16,2048]{2,1,0:T(8,128)(2,1)S(1)}, bf16[32,16,2048]{2,1,0:T(8,128)(2,1)}, u32[]{:S(2)}) copy-start(bf16[32,16,2048]{2,1,0:T(8,128)(2,1)} %param.15) | copy-start | bytes 6291460
  17.9 9.3 %copy-start.7 = (bf16[1040,128]{1,0:T(8,128)(2,1)S(1)}, bf16[1040,128]{1,0:T(8,128)(2,1)}, u32[]{:S(2)}) copy-start(bf16[1040,128]{1,0:T(8,128)(2,1)} %get-tuple-element.35.refs_0_) | copy-start | bytes 798724
  17.9 11.6 %collective-permute-start.1 = (bf16[256,512]{1,0:T(8,128)(2,1)S(1)}, bf16[256,512]{1,0:T(8,128)(2,1)S(1)}, u32[]{:S(2)}, u32[]{:S(2)}) collective-permute-start(bf16[256,512]{1,0:T(8,128)(2,1)S(1)} %get-tuple-element.33), channel_id=1, source_target_pairs={{0,2},{1,3},{2,0},{3,1},{4,6},{5,7},{6,4},{7,5},{8,10},{9,11},{10,... | collective-permute-start | bytes 786440 | tf_op jit(solution)/shard_map/ppermute | solution.py:32
  24.4 10.6 %copy-start.6 = (bf16[32,16,512]{2,1,0:T(8,128)(2,1)S(1)}, bf16[32,16,512]{2,1,0:T(8,128)(2,1)}, u32[]{:S(2)}) copy-start(bf16[32,16,512]{2,1,0:T(8,128)(2,1)} %param.16) | copy-start | bytes 1572868
  24.4 22.8 %copy-start.8 = (bf16[64,64]{1,0:T(8,128)(2,1)S(1)}, bf16[64,64]{1,0:T(8,128)(2,1)}, u32[]{:S(2)}) copy-start(bf16[64,64]{1,0:T(8,128)(2,1)} %get-tuple-element.26.back_ref) | copy-start | bytes 24580
  29.6 17.5 %collective-permute-start.5 = (bf16[256,512]{1,0:T(8,128)(2,1)S(1)}, bf16[256,512]{1,0:T(8,128)(2,1)S(1)}, u32[]{:S(2)}, u32[]{:S(2)}) collective-permute-start(bf16[256,512]{1,0:T(8,128)(2,1)S(1)} %add_convert_fusion), channel_id=1, source_target_pairs={{0,1},{1,0},{2,3},{3,2},{4,5},{5,4},{6,7},{7,6},{8,9},{9,8},{10,11... | collective-permute-start | bytes 786440 | tf_op jit(solution)/shard_map/ppermute | solution.py:32
  29.7 2.0 %collective-permute-start.6 = (f32[16,256]{1,0:T(8,128)S(1)}, f32[16,256]{1,0:T(8,128)S(1)}, u32[]{:S(2)}, u32[]{:S(2)}) collective-permute-start(f32[16,256]{1,0:T(8,128)S(1)} %get-tuple-element.39.refs_0_), channel_id=1, source_target_pairs={{0,1},{1,0},{2,3},{3,2},{4,5},{5,4},{6,7},{7,6},{8,9},{9,8},{10,11... | collective-permute-start | bytes 49160 | tf_op jit(solution)/shard_map/ppermute | solution.py:32
  30.2 3.7 %collective-permute-start.7 = (f32[16,256]{1,0:T(8,128)S(1)}, f32[16,256]{1,0:T(8,128)S(1)}, u32[]{:S(2)}, u32[]{:S(2)}) collective-permute-start(f32[16,256]{1,0:T(8,128)S(1)} %get-tuple-element.39.refs_0_), channel_id=1, source_target_pairs={{0,2},{1,3},{2,0},{3,1},{4,6},{5,7},{6,4},{7,5},{8,10},{9,11},{10,... | collective-permute-start | bytes 49160 | tf_op jit(solution)/shard_map/ppermute | solution.py:32
  31.7 3.3 %collective-permute-start.8 = (f32[16,256]{1,0:T(8,128)S(1)}, f32[16,256]{1,0:T(8,128)S(1)}, u32[]{:S(2)}, u32[]{:S(2)}) collective-permute-start(f32[16,256]{1,0:T(8,128)S(1)} %get-tuple-element.39.refs_0_), channel_id=1, source_target_pairs={{0,3},{1,2},{2,1},{3,0},{4,7},{5,6},{6,5},{7,4},{8,11},{9,10},{10,... | collective-permute-start | bytes 49160 | tf_op jit(solution)/shard_map/ppermute | solution.py:32
  35.3 6.1 %collective-permute-start.10 = (bf16[64,512]{1,0:T(8,128)(2,1)S(1)}, bf16[64,512]{1,0:T(8,128)(2,1)S(1)}, u32[]{:S(2)}, u32[]{:S(2)}) collective-permute-start(bf16[64,512]{1,0:T(8,128)(2,1)S(1)} %get-tuple-element.48), channel_id=1, source_target_pairs={{0,12},{4,8},{8,4},{12,0},{1,13},{5,9},{9,5},{13,1},{2,14},{6,10},... | collective-permute-start | bytes 196616 | tf_op jit(solution)/shard_map/ppermute | solution.py:32
  38.1 5.6 %collective-permute-start.11 = (bf16[64,512]{1,0:T(8,128)(2,1)S(1)}, bf16[64,512]{1,0:T(8,128)(2,1)S(1)}, u32[]{:S(2)}, u32[]{:S(2)}) collective-permute-start(bf16[64,512]{1,0:T(8,128)(2,1)S(1)} %get-tuple-element.49), channel_id=1, source_target_pairs={{0,4},{4,0},{8,12},{12,8},{1,5},{5,1},{9,13},{13,9},{2,6},{6,2},{1... | collective-permute-start | bytes 196616 | tf_op jit(solution)/shard_map/ppermute | solution.py:32
  41.4 5.7 %collective-permute-start.9 = (bf16[64,512]{1,0:T(8,128)(2,1)S(1)}, bf16[64,512]{1,0:T(8,128)(2,1)S(1)}, u32[]{:S(2)}, u32[]{:S(2)}) collective-permute-start(bf16[64,512]{1,0:T(8,128)(2,1)S(1)} %get-tuple-element.47), channel_id=1, source_target_pairs={{0,8},{4,12},{8,0},{12,4},{1,9},{5,13},{9,1},{13,5},{2,10},{6,14},... | collective-permute-start | bytes 196616 | tf_op jit(solution)/shard_map/ppermute | solution.py:32

commit v4 on v3

--- a/solution.py
+++ b/solution.py
@@ -15,6 +15,7 @@
 TN = (((0,), (0,)), ((), ()))
 MIB = 1024 * 1024
 LANES = 128
+BASE_MIB = 53
 
 
 def params(mib):
@@ -121,27 +122,44 @@
     )(requests[None, :], store[None, :], hidden)
 
 
-def base_kernel(size, hidden_ref, projection_ref, *outs):
+def base_kernel(size, hidden_hbm, projection_hbm, *refs):
+    outs, (hidden_ref, projection_ref, hidden_sem, block_sems) = refs[:size], refs[size:]
     width = outs[0].shape[1]
     half = size // 2
     me = lax.axis_index("tp")
-    for k in list(range(half, size)) + list(range(half)):
+    order = list(range(half, size)) + list(range(half))
+    hidden_copy = pltpu.make_async_copy(hidden_hbm, hidden_ref, hidden_sem.at[0])
+    hidden_copy.start()
+    copies = {}
+    for k in order:
         first = pl.multiple_of(jnp.bitwise_xor(me, k) * width, width)
-        part = jnp.dot(
-            hidden_ref[...], projection_ref[:, pl.ds(first, width)], preferred_element_type=F32
+        copies[k] = pltpu.make_async_copy(
+            projection_hbm.at[:, pl.ds(first, width)], projection_ref.at[k], block_sems.at[k]
         )
+        copies[k].start()
+    hidden_copy.wait()
+    for k in order:
+        copies[k].wait()
+        part = jnp.dot(hidden_ref[...], projection_ref[k], preferred_element_type=F32)
         outs[k][...] = part.astype(outs[k].dtype)
 
 
 def base(hidden, projection, size):
-    rows, _ = hidden.shape
+    rows, features = hidden.shape
     width = projection.shape[1] // size
     half = size // 2
     return pl.pallas_call(
         functools.partial(base_kernel, size),
         out_shape=[jax.ShapeDtypeStruct((rows, width), F32)] * half
         + [jax.ShapeDtypeStruct((rows, width), BF16)] * half,
-        compiler_params=params(20),
+        in_specs=[pl.BlockSpec(memory_space=pltpu.HBM)] * 2,
+        scratch_shapes=[
+            pltpu.VMEM((rows, features), BF16),
+            pltpu.VMEM((size, features, width), BF16),
+            pltpu.SemaphoreType.DMA((1,)),
+            pltpu.SemaphoreType.DMA((size,)),
+        ],
+        compiler_params=params(BASE_MIB),
         cost_estimate=cost(0, 4096),
         name="base",
     )(hidden, projection)
@@ -308,7 +326,7 @@
     groups, size, cap, heads, back_ref, query_ref, mixed_ref, lse_ref, *refs
 ):
     summands, deltas = refs[:size], refs[size : size + groups]
-    out_ref, new_ref = refs[size + groups :]
+    out_hbm, new_hbm, out_ref, new_ref, out_sems, new_sems = refs[size + groups :]
     steps, seqs, width = query_ref.shape
     columns = new_ref.shape[2]
     size = columns // (2 * heads)
@@ -316,6 +334,7 @@
     scaling = 1.0 / math.sqrt(size)
     back = back_ref[...]
     new = []
+    copies = []
     for s in range(steps):
         delta = jnp.concatenate([r[s * cap : (s + 1) * cap, :] for r in deltas], axis=0)
         update = jnp.dot(back, delta, preferred_element_type=F32)
@@ -325,6 +344,8 @@
             base = base + summand[rows, :].astype(F32)
         new.append((base + update).astype(BF16))
         new_ref[s] = new[s]
+        copies.append(pltpu.make_async_copy(new_ref.at[s], new_hbm.at[s], new_sems.at[s]))
+        copies[-1].start()
     same = lax.rem(iota((seqs, LANES), 1), jnp.int32(seqs)) == iota((seqs, LANES), 0)
 
     def over_steps(parts, combine):
@@ -332,50 +353,78 @@
         turned = [pltpu.roll(whole, shift, 1) for shift in range(seqs, LANES, seqs)]
         return functools.reduce(combine, turned, whole)
 
+    parts = steps * seqs // LANES
+    rows = heads * steps * share
+    units = [(g, s) for g in range(heads) for s in range(steps)]
+
+    def lanes(g, h):
+        return slice((g * share + h) * size, (g * share + h + 1) * size)
+
+    fresh = [[] for _ in range(parts)]
+    values = []
     for g in range(heads):
         left = g * 2 * size
         keys = jnp.concatenate([n[:, left : left + size] for n in new], axis=0)
-        values = jnp.concatenate([n[:, left + size : left + 2 * size] for n in new], axis=0)
+        values.append(
+            jnp.concatenate([n[:, left + size : left + 2 * size] for n in new], axis=0)
+        )
         for s in range(steps):
-            lanes = [
-                slice((g * share + h) * size, (g * share + h + 1) * size) for h in range(share)
-            ]
             count = pl.cdiv((s + 1) * seqs, LANES)
-            q = jnp.concatenate([query_ref[s, :, cut] for cut in lanes], axis=0)
-            scores = lax.dot_general(
-                q, keys[: count * LANES], NT, preferred_element_type=F32
+            q = jnp.concatenate([query_ref[s, :, lanes(g, h)] for h in range(share)], axis=0)
+            scores = lax.dot_general(q, keys[: count * LANES], NT, preferred_element_type=F32)
+            for c in range(parts):
+                if c < count:
+                    block = scores[:, c * LANES : (c + 1) * LANES].reshape(share, seqs, LANES)
+                    fresh[c].append(jnp.sum(jnp.where(same[None], block, 0.0), axis=1))
+                else:
+                    fresh[c].append(jnp.zeros((share, LANES), F32))
+    now = lax.rem(lax.div(iota((rows, LANES), 0), jnp.int32(share)), jnp.int32(steps))
+    step = lax.div(iota((rows, LANES), 1), jnp.int32(seqs))
+    fresh = [
+        jnp.where(
+            step + c * (LANES // seqs) <= now,
+            jnp.concatenate(fresh[c], axis=0) * scaling,
+            -jnp.inf,
+        )
+        for c in range(parts)
+    ]
+    lse = lse_ref[...]
+    top = jnp.maximum(over_steps(fresh, jnp.maximum), lse)
+    old = jnp.exp(lse - top)
+    raised = [jnp.exp(part - top) for part in fresh]
+    scale = 1.0 / (over_steps(raised, jnp.add) + old)
+    weights = [part * scale for part in raised]
+    old = jnp.transpose(old * scale)[:seqs, :]
+    for g, s in units:
+        count = pl.cdiv((s + 1) * seqs, LANES)
+        first = (g * steps + s) * share
+        spread = []
+        for h in range(share):
+            row = slice(first + h, first + h + 1)
+            spread.append(
+                jnp.concatenate(
+                    [jnp.where(same, weights[c][row], 0.0).astype(BF16) for c in range(count)],
+                    axis=1,
+                )
             )
-            fresh = []
-            for c in range(count):
-                block = scores[:, c * LANES : (c + 1) * LANES].reshape(share, seqs, LANES)
-                row = jnp.sum(jnp.where(same[None], block, 0.0), axis=1) * scaling
-                step = lax.div(iota((share, LANES), 1), jnp.int32(seqs)) + c * (LANES // seqs)
-                fresh.append(jnp.where(step <= s, row, -jnp.inf))
-            first = (g * steps + s) * share
-            lse = lse_ref[first : first + share, :]
-            top = jnp.maximum(over_steps(fresh, jnp.maximum), lse)
-            old = jnp.exp(lse - top)
-            raised = [jnp.exp(row - top) for row in fresh]
-            scale = 1.0 / (over_steps(raised, jnp.add) + old)
-            old = jnp.transpose(old * scale)[:seqs, :]
-            weights = jnp.concatenate(
-                [
-                    jnp.concatenate(
-                        [
-                            jnp.where(same, (row * scale)[h : h + 1, :], 0.0).astype(BF16)
-                            for row in raised
-                        ],
-                        axis=1,
-                    )
-                    for h in range(share)
-                ],
-                axis=0,
+        mixed = jnp.dot(
+            jnp.concatenate(spread, axis=0),
+            values[g][: count * LANES],
+            preferred_element_type=F32,
+        )
+        for h in range(share):
+            total = mixed[h * seqs : (h + 1) * seqs]
+            total = total + mixed_ref[s, :, lanes(g, h)] * old[:, first + h : first + h + 1]
+            out_ref[s, :, lanes(g, h)] = total.astype(BF16)
+        part = (s, slice(None), pl.ds(g * share * size, share * size))
+        copies.append(
+            pltpu.make_async_copy(
+                out_ref.at[part], out_hbm.at[part], out_sems.at[g * steps + s]
             )
-            mixed = jnp.dot(weights, values[: count * LANES], preferred_element_type=F32)
-            for h in range(share):
-                total = mixed[h * seqs : (h + 1) * seqs]
-                total = total + mixed_ref[s, :, lanes[h]] * old[:, h : h + 1]
-                out_ref[s, :, lanes[h]] = total.astype(BF16)
+        )
+        copies[-1].start()
+    for copy in copies:
+        copy.wait()
 
 
 def finish(back, summands, queries, mixed, lse, deltas, cap, heads):
@@ -386,6 +435,13 @@
         out_shape=[
             jax.ShapeDtypeStruct((steps, seqs, width), BF16),
             jax.ShapeDtypeStruct((steps, seqs, columns), BF16),
+        ],
+        out_specs=[pl.BlockSpec(memory_space=pltpu.HBM)] * 2,
+        scratch_shapes=[
+            pltpu.VMEM((steps, seqs, width), BF16),
+            pltpu.VMEM((steps, seqs, columns), BF16),
+            pltpu.SemaphoreType.DMA((heads * steps,)),
+            pltpu.SemaphoreType.DMA((steps,)),
         ],
         compiler_params=params(16),
         cost_estimate=cost(
@@ -419,7 +475,7 @@
     order = [0] + sorted(range(1, groups), key=lambda k: -k.bit_length())
     *blocks, back = route(requests, adapter_store_row, hidden, order, cap, entries)
     over_dp = [swap("dp", groups, k) for k in order[1:]]
-    over_tp = [swap("tp", size, k) for k in range(1, size)]
+    over_tp = [swap("tp", size, k) for k in reversed(range(1, size))]
     got = [move(block) for move, block in zip(over_dp, blocks[1:])]
 
     late_hidden, _ = lax.optimization_barrier((hidden, back))
@@ -433,16 +489,15 @@
     block, _ = lax.optimization_barrier((blocks[0], lse))
     shrunk, slots = shrink(adapter_shrink_weight, [block] + got, steps, cap)
     partial = [shrunk] + [move(shrunk) for move in over_tp]
-    terms, _ = lax.optimization_barrier((terms, shrunk))
+    deltas = expand(adapter_expand_weight, partial, slots, groups)
+    returned = [deltas[0]] + [move(delta) for move, delta in zip(over_dp, deltas[1:])]
+    terms, _ = lax.optimization_barrier((terms, deltas[0]))
     while distance > 1:
         distance //= 2
         move = swap("tp", size, distance)
         for k in range(distance):
             moved = sum(term.astype(F32) for term in terms[distance + k]).astype(BF16)
             terms[k] = terms[k] + [move(moved)]
-    slots, _ = lax.optimization_barrier((slots, moved))
-    deltas = expand(adapter_expand_weight, partial, slots, groups)
-    returned = [deltas[0]] + [move(delta) for move, delta in zip(over_dp, deltas[1:])]
     summands = terms[0]
     return tuple(finish(back, summands, queries, mixed, lse, returned, cap, heads))
 

time: 50.9 us -> 50.1 us (0.984)
  local copies, waits for them, and re-layouts: 4.64 us -> 0.04 us
  Pallas kernels: 16 us -> 18.6 us
  starting transfers between devices: 15.9 us -> 18.5 us
  waiting for transfers between devices: 13.4 us -> 12 us
    unnamed x20, local copies, waits for them, and re-layouts: 4.64 us -> 0.04 us
    pallas_call x1, Pallas kernels: 2.36 us -> 5.73 us  [base(): pl.pallas_call(functools.partial(base_kernel, size), out_shape=[jax.Shape...]
    ppermute x12, starting transfers between devices: 15.9 us -> 18.5 us  [swap(): return lambda value: lax.ppermute(value, axis, pairs)]
    ppermute x12, waiting for transfers between devices: 13.4 us -> 12 us  [swap(): return lambda value: lax.ppermute(value, axis, pairs)]
    pallas_call x1, Pallas kernels: 3.59 us -> 2.86 us  [finish(): pl.pallas_call(functools.partial(finish_kernel, len(deltas), len(summands...]
  transfers between devices with their start and end apart: 12 -> 12, of which waited for: 7 -> 6; matrix products, arithmetic and copies ran while one was open for 0% -> 0% of each run, Pallas kernels for 18% -> 25%
where the time goes in v4:
time: 50.1 us; the launch traced here: 50 us
  Pallas kernels  18.6 us (37%)
  starting transfers between devices  18.5 us (37%)
  waiting for transfers between devices  12 us (24%)
  between operations  0.75 us (1%)
    ppermute x12, starting transfers between devices, swap(): return lambda value: lax.ppermute(value, axis, pairs)  18.5 us
    ppermute x12, waiting for transfers between devices, swap(): return lambda value: lax.ppermute(value, axis, pairs)  12 us
    pallas_call x1, Pallas kernels, past(): pl.pallas_call(past_kernel, grid_spec=pltpu.PrefetchScalarGridSpec(num_sc...  5.88 us
    pallas_call x1, Pallas kernels, base(): pl.pallas_call(functools.partial(base_kernel, size), out_shape=[jax.Shape...  5.73 us
    pallas_call x1, Pallas kernels, route(): pl.pallas_call(functools.partial(route_kernel, order, cap, entries), out_...  3.09 us
    pallas_call x1, Pallas kernels, finish(): pl.pallas_call(functools.partial(finish_kernel, len(deltas), len(summands...  2.86 us
  transfers between devices with their start and end apart: 12, of which 6 were waited for; matrix products, arithmetic and copies ran while one was open for 0% of the time, Pallas kernels for 25%

profile of v4, /device:TPU:0, one launch (start us, length us, event | category | flops | bytes accessed | tf_op | source)
XLA Modules:
  0.0 50.0 jit_solution(17057555440807723251)
XLA Ops:
  0.6 3.1 %route.1 = (bf16[1040,128]{1,0:T(8,128)(2,1)}, bf16[1040,128]{1,0:T(8,128)(2,1)}, bf16[1040,128]{1,0:T(8,128)(2,1)}, bf16[1040,128]{1,0:T(8,128)(2,1)}, bf16[64,64]{1,0:T(8,128)(2,1)}) custom-call(s32[1,64]{1,0:T(1,128)} %bitcast.8, s32[1,128]{1,0:T(1,128)} %bitcast.9, bf16[4,64,2048]{2,1,0:T(8,128)(2,1)} %hidden_hbm.1), custom_call_target="tpu_custom_call" | custom-call | flops 67108864 | bytes 2097152 | tf_op jit(solution)/shard_map/route/pallas_call | solution.py:105
  3.7 4.1 %collective-permute-start.2 = (bf16[1040,128]{1,0:T(8,128)(2,1)}, bf16[1040,128]{1,0:T(8,128)(2,1)S(1)}, u32[]{:S(2)}, u32[]{:S(2)}) collective-permute-start(bf16[1040,128]{1,0:T(8,128)(2,1)} %get-tuple-element.35), channel_id=1, source_target_pairs={{0,8},{4,12},{8,0},{12,4},{1,9},{5,13},{9,1},{13,5},{2,10},{6,14},... | collective-permute-start | bytes 798728 | tf_op jit(solution)/shard_map/ppermute | solution.py:33
  7.8 1.3 %collective-permute-start.3 = (bf16[1040,128]{1,0:T(8,128)(2,1)}, bf16[1040,128]{1,0:T(8,128)(2,1)S(1)}, u32[]{:S(2)}, u32[]{:S(2)}) collective-permute-start(bf16[1040,128]{1,0:T(8,128)(2,1)} %get-tuple-element.36), channel_id=1, source_target_pairs={{0,12},{4,8},{8,4},{12,0},{1,13},{5,9},{9,5},{13,1},{2,14},{6,10},... | collective-permute-start | bytes 798728 | tf_op jit(solution)/shard_map/ppermute | solution.py:33
  9.2 0.2 collective-permute-start.4
  9.4 0.0 copy-start
  9.4 0.0 copy-start.1
  9.4 0.0 copy-start.2
  9.4 0.0 copy-start.8
  9.4 5.7 %base.1 = (f32[256,512]{1,0:T(8,128)}, f32[256,512]{1,0:T(8,128)}, bf16[256,512]{1,0:T(8,128)(2,1)S(1)}, bf16[256,512]{1,0:T(8,128)(2,1)S(1)}) custom-call(bf16[256,2048]{1,0:T(8,128)(2,1)} %bitcast.7, bf16[2048,2048]{1,0:T(8,128)(2,1)} %projection_hbm.1), custom_call_target="tpu_custom_call" | custom-call | bytes 4096 | tf_op jit(solution)/shard_map/base/pallas_call | solution.py:151
  15.2 1.6 %collective-permute-start = (bf16[256,512]{1,0:T(8,128)(2,1)S(1)}, bf16[256,512]{1,0:T(8,128)(2,1)S(1)}, u32[]{:S(2)}, u32[]{:S(2)}) collective-permute-start(bf16[256,512]{1,0:T(8,128)(2,1)S(1)} %get-tuple-element.30), channel_id=1, source_target_pairs={{0,2},{1,3},{2,0},{3,1},{4,6},{5,7},{6,4},{7,5},{8,10},{9,11},{10,... | collective-permute-start | bytes 786440 | tf_op jit(solution)/shard_map/ppermute | solution.py:33
  16.7 0.0 copy-start.3
  16.7 0.0 copy-start.6
  16.7 0.0 copy-start.5
  16.7 0.0 copy-start.9
  16.7 0.6 %collective-permute-start.1 = (bf16[256,512]{1,0:T(8,128)(2,1)S(1)}, bf16[256,512]{1,0:T(8,128)(2,1)S(1)}, u32[]{:S(2)}, u32[]{:S(2)}) collective-permute-start(bf16[256,512]{1,0:T(8,128)(2,1)S(1)} %get-tuple-element.32), channel_id=1, source_target_pairs={{0,2},{1,3},{2,0},{3,1},{4,6},{5,7},{6,4},{7,5},{8,10},{9,11},{10,... | collective-permute-start | bytes 786440 | tf_op jit(solution)/shard_map/ppermute | solution.py:33
  17.3 0.0 copy-done
  17.3 0.0 copy-done.1
  17.3 0.0 copy-done.2
  17.3 0.0 copy-done.8
  17.3 5.9 %past.1 = (f32[4,64,2048]{2,1,0:T(8,128)S(1)}, f32[64,128]{1,0:T(8,128)S(1)}) custom-call(s32[64]{0:T(128)S(1)} %copy-done.8, bf16[4,64,2048]{2,1,0:T(8,128)(2,1)S(1)} %copy-done, bf16[64,2,128,128]{3,2,1,0:T(8,128)(2,1)S(1)} %copy-done.1, bf16[64,2,128,128]{3,2,1,0:T(8,128)(2,1)S(1)} %copy-done.2), custom_call_target="tpu_custom_call" | custom-call | bytes 4096 | tf_op jit(solution)/shard_map/past/pallas_call | solution.py:228
  23.2 0.0 copy-start.4
  23.2 0.0 copy-start.7
  23.2 3.5 %collective-permute-done.2.refs_1_ = bf16[1040,128]{1,0:T(8,128)(2,1)S(1)} collective-permute-done((bf16[1040,128]{1,0:T(8,128)(2,1)}, bf16[1040,128]{1,0:T(8,128)(2,1)S(1)}, u32[]{:S(2)}, u32[]{:S(2)}) %collective-permute-start.2) | collective-permute-done | bytes 266272 | tf_op jit(solution)/shard_map/ppermute | solution.py:33
  26.7 0.0 collective-permute-done.3.refs_2_
  26.7 0.5 %collective-permute-done.4.refs_3_ = bf16[1040,128]{1,0:T(8,128)(2,1)S(1)} collective-permute-done((bf16[1040,128]{1,0:T(8,128)(2,1)}, bf16[1040,128]{1,0:T(8,128)(2,1)S(1)}, u32[]{:S(2)}, u32[]{:S(2)}) %collective-permute-start.4) | collective-permute-done | bytes 266272 | tf_op jit(solution)/shard_map/ppermute | solution.py:33
  27.2 0.0 copy-done.3
  27.2 0.0 copy-done.6
  27.2 0.8 %shrink.1 = (f32[16,256]{1,0:T(8,128)S(1)}, s32[1,256]{1,0:T(1,128)S(1)}) custom-call(bf16[512,2048]{1,0:T(8,128)(2,1)S(1)} %bitcast.5, bf16[1040,128]{1,0:T(8,128)(2,1)S(1)} %copy-done.6, bf16[1040,128]{1,0:T(8,128)(2,1)S(1)} %collective-permute-done.2.refs_1_, bf16[1040,128]{1,0:T(8,128)(2,1)S(1)} %collective-permute-done.3.refs_2_, ...), custom_call_target="tpu_custom_call" | custom-call | flops 536870912 | bytes 3145728 | tf_op jit(solution)/shard_map/shrink/pallas_call | solution.py:278
  28.0 0.1 collective-permute-start.5
  28.1 1.6 %collective-permute-start.6 = (f32[16,256]{1,0:T(8,128)S(1)}, f32[16,256]{1,0:T(8,128)S(1)}, u32[]{:S(2)}, u32[]{:S(2)}) collective-permute-start(f32[16,256]{1,0:T(8,128)S(1)} %get-tuple-element.39.refs_0_), channel_id=1, source_target_pairs={{0,2},{1,3},{2,0},{3,1},{4,6},{5,7},{6,4},{7,5},{8,10},{9,11},{10,... | collective-permute-start | bytes 49160 | tf_op jit(solution)/shard_map/ppermute | solution.py:33
  29.7 0.3 collective-permute-start.7
  29.9 1.4 %collective-permute-done.5.refs_1_ = f32[16,256]{1,0:T(8,128)S(1)} collective-permute-done((f32[16,256]{1,0:T(8,128)S(1)}, f32[16,256]{1,0:T(8,128)S(1)}, u32[]{:S(2)}, u32[]{:S(2)}) %collective-permute-start.5) | collective-permute-done | bytes 16416 | tf_op jit(solution)/shard_map/ppermute | solution.py:33
  31.3 0.6 %collective-permute-done.6.refs_2_ = f32[16,256]{1,0:T(8,128)S(1)} collective-permute-done((f32[16,256]{1,0:T(8,128)S(1)}, f32[16,256]{1,0:T(8,128)S(1)}, u32[]{:S(2)}, u32[]{:S(2)}) %collective-permute-start.6) | collective-permute-done | bytes 16416 | tf_op jit(solution)/shard_map/ppermute | solution.py:33
  31.9 0.0 collective-permute-done.7.refs_3_
  31.9 0.0 copy-done.5
  31.9 0.3 expand.1
  32.2 0.0 collective-permute-done.refs_1_
  32.2 0.0 collective-permute-done.1
  32.3 0.0 copy-done.9
  32.3 0.1 add_convert_fusion
  32.4 0.5 collective-permute-start.8
  32.8 3.5 %collective-permute-start.10 = (bf16[64,512]{1,0:T(8,128)(2,1)S(1)}, bf16[64,512]{1,0:T(8,128)(2,1)S(1)}, u32[]{:S(2)}, u32[]{:S(2)}) collective-permute-start(bf16[64,512]{1,0:T(8,128)(2,1)S(1)} %get-tuple-element.46), channel_id=1, source_target_pairs={{0,12},{4,8},{8,4},{12,0},{1,13},{5,9},{9,5},{13,1},{2,14},{6,10},... | collective-permute-start | bytes 196616 | tf_op jit(solution)/shard_map/ppermute | solution.py:33
  36.3 4.8 %collective-permute-start.11 = (bf16[64,512]{1,0:T(8,128)(2,1)S(1)}, bf16[64,512]{1,0:T(8,128)(2,1)S(1)}, u32[]{:S(2)}, u32[]{:S(2)}) collective-permute-start(bf16[64,512]{1,0:T(8,128)(2,1)S(1)} %get-tuple-element.47), channel_id=1, source_target_pairs={{0,4},{4,0},{8,12},{12,8},{1,5},{5,1},{9,13},{13,9},{2,6},{6,2},{1... | collective-permute-start | bytes 196616 | tf_op jit(solution)/shard_map/ppermute | solution.py:33
  41.1 0.0 collective-permute-start.9
  41.1 0.0 collective-permute-done.10.refs_5_
  41.1 2.4 %collective-permute-done.11.refs_6_ = bf16[64,512]{1,0:T(8,128)(2,1)S(1)} collective-permute-done((bf16[64,512]{1,0:T(8,128)(2,1)S(1)}, bf16[64,512]{1,0:T(8,128)(2,1)S(1)}, u32[]{:S(2)}, u32[]{:S(2)}) %collective-permute-start.11) | collective-permute-done | bytes 65568 | tf_op jit(solution)/shard_map/ppermute | solution.py:33
  43.5 3.6 %collective-permute-done.9.refs_4_ = bf16[64,512]{1,0:T(8,128)(2,1)S(1)} collective-permute-done((bf16[64,512]{1,0:T(8,128)(2,1)S(1)}, bf16[64,512]{1,0:T(8,128)(2,1)S(1)}, u32[]{:S(2)}, u32[]{:S(2)}) %collective-permute-start.9) | collective-permute-done | bytes 65568 | tf_op jit(solution)/shard_map/ppermute | solution.py:33
  47.1 0.0 collective-permute-done.8.refs_2_
  47.1 0.0 copy-done.4
  47.1 0.0 copy-done.7
  47.1 2.9 %finish.1 = (bf16[4,64,2048]{2,1,0:T(8,128)(2,1)}, bf16[4,64,512]{2,1,0:T(8,128)(2,1)}) custom-call(bf16[64,64]{1,0:T(8,128)(2,1)S(1)} %copy-done.7, bf16[4,64,2048]{2,1,0:T(8,128)(2,1)S(1)} %copy-done, f32[4,64,2048]{2,1,0:T(8,128)S(1)} %get-tuple-element.26.mixed_ref, f32[64,128]{1,0:T(8,128)S(1)} %get-tuple-element.27.lse_ref, f32[256,512]{1,0:T(8,128)S(1)} %copy-done.4, ...), custom_call_target="tpu_custom_call" | custom-call | flops 1073741824 | bytes 5242880 | tf_op jit(solution)/shard_map/finish/pallas_call | solution.py:433
Async XLA Ops:
  3.7 23.0 %collective-permute-start.2 = (bf16[1040,128]{1,0:T(8,128)(2,1)}, bf16[1040,128]{1,0:T(8,128)(2,1)S(1)}, u32[]{:S(2)}, u32[]{:S(2)}) collective-permute-start(bf16[1040,128]{1,0:T(8,128)(2,1)} %get-tuple-element.35), channel_id=1, source_target_pairs={{0,8},{4,12},{8,0},{12,4},{1,9},{5,13},{9,1},{13,5},{2,10},{6,14},... | collective-permute-start | bytes 798728 | tf_op jit(solution)/shard_map/ppermute | solution.py:33
  7.8 18.9 %collective-permute-start.3 = (bf16[1040,128]{1,0:T(8,128)(2,1)}, bf16[1040,128]{1,0:T(8,128)(2,1)S(1)}, u32[]{:S(2)}, u32[]{:S(2)}) collective-permute-start(bf16[1040,128]{1,0:T(8,128)(2,1)} %get-tuple-element.36), channel_id=1, source_target_pairs={{0,12},{4,8},{8,4},{12,0},{1,13},{5,9},{9,5},{13,1},{2,14},{6,10},... | collective-permute-start | bytes 798728 | tf_op jit(solution)/shard_map/ppermute | solution.py:33
  9.2 18.1 %collective-permute-start.4 = (bf16[1040,128]{1,0:T(8,128)(2,1)}, bf16[1040,128]{1,0:T(8,128)(2,1)S(1)}, u32[]{:S(2)}, u32[]{:S(2)}) collective-permute-start(bf16[1040,128]{1,0:T(8,128)(2,1)} %get-tuple-element.37), channel_id=1, source_target_pairs={{0,4},{4,0},{8,12},{12,8},{1,5},{5,1},{9,13},{13,9},{2,6},{6,2},{1... | collective-permute-start | bytes 798728 | tf_op jit(solution)/shard_map/ppermute | solution.py:33
  9.4 7.9 %copy-start = (bf16[4,64,2048]{2,1,0:T(8,128)(2,1)S(1)}, bf16[4,64,2048]{2,1,0:T(8,128)(2,1)}, u32[]{:S(2)}) copy-start(bf16[4,64,2048]{2,1,0:T(8,128)(2,1)} %query_ref.3) | copy-start | bytes 3145732
  9.4 7.9 %copy-start.1 = (bf16[64,2,128,128]{3,2,1,0:T(8,128)(2,1)S(1)}, bf16[64,2,128,128]{3,2,1,0:T(8,128)(2,1)}, u32[]{:S(2)}) copy-start(bf16[64,2,128,128]{3,2,1,0:T(8,128)(2,1)} %key_ref.1) | copy-start | bytes 12582916
  9.4 7.9 %copy-start.2 = (bf16[64,2,128,128]{3,2,1,0:T(8,128)(2,1)S(1)}, bf16[64,2,128,128]{3,2,1,0:T(8,128)(2,1)}, u32[]{:S(2)}) copy-start(bf16[64,2,128,128]{3,2,1,0:T(8,128)(2,1)} %value_ref.1) | copy-start | bytes 12582916
  9.4 7.9 %copy-start.8 = (s32[64]{0:T(128)S(1)}, s32[64]{0:T(128)}, u32[]{:S(2)}) copy-start(s32[64]{0:T(128)} %lengths_ref.1) | copy-start | bytes 772
  15.2 17.1 %collective-permute-start = (bf16[256,512]{1,0:T(8,128)(2,1)S(1)}, bf16[256,512]{1,0:T(8,128)(2,1)S(1)}, u32[]{:S(2)}, u32[]{:S(2)}) collective-permute-start(bf16[256,512]{1,0:T(8,128)(2,1)S(1)} %get-tuple-element.30), channel_id=1, source_target_pairs={{0,2},{1,3},{2,0},{3,1},{4,6},{5,7},{6,4},{7,5},{8,10},{9,11},{10,... | collective-permute-start | bytes 786440 | tf_op jit(solution)/shard_map/ppermute | solution.py:33
  16.7 10.5 %copy-start.3 = (bf16[32,16,2048]{2,1,0:T(8,128)(2,1)S(1)}, bf16[32,16,2048]{2,1,0:T(8,128)(2,1)}, u32[]{:S(2)}) copy-start(bf16[32,16,2048]{2,1,0:T(8,128)(2,1)} %param.15) | copy-start | bytes 6291460
  16.7 10.5 %copy-start.6 = (bf16[1040,128]{1,0:T(8,128)(2,1)S(1)}, bf16[1040,128]{1,0:T(8,128)(2,1)}, u32[]{:S(2)}) copy-start(bf16[1040,128]{1,0:T(8,128)(2,1)} %get-tuple-element.34.refs_0_) | copy-start | bytes 798724
  16.7 15.2 %copy-start.5 = (bf16[32,16,512]{2,1,0:T(8,128)(2,1)S(1)}, bf16[32,16,512]{2,1,0:T(8,128)(2,1)}, u32[]{:S(2)}) copy-start(bf16[32,16,512]{2,1,0:T(8,128)(2,1)} %param.16) | copy-start | bytes 1572868
  16.7 15.5 %copy-start.9 = (f32[256,512]{1,0:T(8,128)S(1)}, f32[256,512]{1,0:T(8,128)}, u32[]{:S(2)}) copy-start(f32[256,512]{1,0:T(8,128)} %get-tuple-element.43) | copy-start | bytes 1572868
  16.7 15.5 %collective-permute-start.1 = (bf16[256,512]{1,0:T(8,128)(2,1)S(1)}, bf16[256,512]{1,0:T(8,128)(2,1)S(1)}, u32[]{:S(2)}, u32[]{:S(2)}) collective-permute-start(bf16[256,512]{1,0:T(8,128)(2,1)S(1)} %get-tuple-element.32), channel_id=1, source_target_pairs={{0,2},{1,3},{2,0},{3,1},{4,6},{5,7},{6,4},{7,5},{8,10},{9,11},{10,... | collective-permute-start | bytes 786440 | tf_op jit(solution)/shard_map/ppermute | solution.py:33
  23.2 23.9 %copy-start.4 = (f32[256,512]{1,0:T(8,128)S(1)}, f32[256,512]{1,0:T(8,128)}, u32[]{:S(2)}) copy-start(f32[256,512]{1,0:T(8,128)} %get-tuple-element.41.refs_0_) | copy-start | bytes 1572868
  23.2 23.9 %copy-start.7 = (bf16[64,64]{1,0:T(8,128)(2,1)S(1)}, bf16[64,64]{1,0:T(8,128)(2,1)}, u32[]{:S(2)}) copy-start(bf16[64,64]{1,0:T(8,128)(2,1)} %get-tuple-element.25.back_ref) | copy-start | bytes 24580
  28.0 3.3 %collective-permute-start.5 = (f32[16,256]{1,0:T(8,128)S(1)}, f32[16,256]{1,0:T(8,128)S(1)}, u32[]{:S(2)}, u32[]{:S(2)}) collective-permute-start(f32[16,256]{1,0:T(8,128)S(1)} %get-tuple-element.39.refs_0_), channel_id=1, source_target_pairs={{0,3},{1,2},{2,1},{3,0},{4,7},{5,6},{6,5},{7,4},{8,11},{9,10},{10,... | collective-permute-start | bytes 49160 | tf_op jit(solution)/shard_map/ppermute | solution.py:33
  28.1 3.8 %collective-permute-start.6 = (f32[16,256]{1,0:T(8,128)S(1)}, f32[16,256]{1,0:T(8,128)S(1)}, u32[]{:S(2)}, u32[]{:S(2)}) collective-permute-start(f32[16,256]{1,0:T(8,128)S(1)} %get-tuple-element.39.refs_0_), channel_id=1, source_target_pairs={{0,2},{1,3},{2,0},{3,1},{4,6},{5,7},{6,4},{7,5},{8,10},{9,11},{10,... | collective-permute-start | bytes 49160 | tf_op jit(solution)/shard_map/ppermute | solution.py:33
  29.7 2.2 %collective-permute-start.7 = (f32[16,256]{1,0:T(8,128)S(1)}, f32[16,256]{1,0:T(8,128)S(1)}, u32[]{:S(2)}, u32[]{:S(2)}) collective-permute-start(f32[16,256]{1,0:T(8,128)S(1)} %get-tuple-element.39.refs_0_), channel_id=1, source_target_pairs={{0,1},{1,0},{2,3},{3,2},{4,5},{5,4},{6,7},{7,6},{8,9},{9,8},{10,11... | collective-permute-start | bytes 49160 | tf_op jit(solution)/shard_map/ppermute | solution.py:33
  32.4 14.8 %collective-permute-start.8 = (bf16[256,512]{1,0:T(8,128)(2,1)S(1)}, bf16[256,512]{1,0:T(8,128)(2,1)S(1)}, u32[]{:S(2)}, u32[]{:S(2)}) collective-permute-start(bf16[256,512]{1,0:T(8,128)(2,1)S(1)} %add_convert_fusion), channel_id=1, source_target_pairs={{0,1},{1,0},{2,3},{3,2},{4,5},{5,4},{6,7},{7,6},{8,9},{9,8},{10,11... | collective-permute-start | bytes 786440 | tf_op jit(solution)/shard_map/ppermute | solution.py:33
  32.8 8.3 %collective-permute-start.10 = (bf16[64,512]{1,0:T(8,128)(2,1)S(1)}, bf16[64,512]{1,0:T(8,128)(2,1)S(1)}, u32[]{:S(2)}, u32[]{:S(2)}) collective-permute-start(bf16[64,512]{1,0:T(8,128)(2,1)S(1)} %get-tuple-element.46), channel_id=1, source_target_pairs={{0,12},{4,8},{8,4},{12,0},{1,13},{5,9},{9,5},{13,1},{2,14},{6,10},... | collective-permute-start | bytes 196616 | tf_op jit(solution)/shard_map/ppermute | solution.py:33
  36.3 7.2 %collective-permute-start.11 = (bf16[64,512]{1,0:T(8,128)(2,1)S(1)}, bf16[64,512]{1,0:T(8,128)(2,1)S(1)}, u32[]{:S(2)}, u32[]{:S(2)}) collective-permute-start(bf16[64,512]{1,0:T(8,128)(2,1)S(1)} %get-tuple-element.47), channel_id=1, source_target_pairs={{0,4},{4,0},{8,12},{12,8},{1,5},{5,1},{9,13},{13,9},{2,6},{6,2},{1... | collective-permute-start | bytes 196616 | tf_op jit(solution)/shard_map/ppermute | solution.py:33
  41.1 6.0 %collective-permute-start.9 = (bf16[64,512]{1,0:T(8,128)(2,1)S(1)}, bf16[64,512]{1,0:T(8,128)(2,1)S(1)}, u32[]{:S(2)}, u32[]{:S(2)}) collective-permute-start(bf16[64,512]{1,0:T(8,128)(2,1)S(1)} %get-tuple-element.45), channel_id=1, source_target_pairs={{0,8},{4,12},{8,0},{12,4},{1,9},{5,13},{9,1},{13,5},{2,10},{6,14},... | collective-permute-start | bytes 196616 | tf_op jit(solution)/shard_map/ppermute | solution.py:33

commit v5 on v4

--- a/solution.py
+++ b/solution.py
@@ -323,9 +323,11 @@
 
 
 def finish_kernel(
-    groups, size, cap, heads, back_ref, query_ref, mixed_ref, lse_ref, *refs
+    turns, size, cap, heads, back_ref, query_ref, mixed_ref, lse_ref, *refs
 ):
-    summands, deltas = refs[:size], refs[size : size + groups]
+    groups = len(turns)
+    summands = refs[:size]
+    deltas = [refs[size + turns.index(k)] for k in range(groups)]
     out_hbm, new_hbm, out_ref, new_ref, out_sems, new_sems = refs[size + groups :]
     steps, seqs, width = query_ref.shape
     columns = new_ref.shape[2]
@@ -427,11 +429,11 @@
         copy.wait()
 
 
-def finish(back, summands, queries, mixed, lse, deltas, cap, heads):
+def finish(back, summands, queries, mixed, lse, deltas, turns, cap, heads):
     steps, seqs, width = queries.shape
     columns = summands[0].shape[1]
     return pl.pallas_call(
-        functools.partial(finish_kernel, len(deltas), len(summands), cap, heads),
+        functools.partial(finish_kernel, turns, len(summands), cap, heads),
         out_shape=[
             jax.ShapeDtypeStruct((steps, seqs, width), BF16),
             jax.ShapeDtypeStruct((steps, seqs, columns), BF16),
@@ -450,7 +452,7 @@
             steps * seqs * width * 2,
         ),
         name="finish",
-    )(back, queries, mixed, lse, *summands, *deltas)
+    )(back, queries, mixed, lse, *summands, *[deltas[k] for k in turns])
 
 
 def body(
@@ -472,7 +474,8 @@
     entries = adapter_shrink_weight.shape[0]
     heads = cached_key_rows.shape[1]
 
-    order = [0] + sorted(range(1, groups), key=lambda k: -k.bit_length())
+    order = [0] + sorted(range(1, groups), reverse=True)
+    turns = [0, groups - 1] + list(range(1, groups - 1))
     *blocks, back = route(requests, adapter_store_row, hidden, order, cap, entries)
     over_dp = [swap("dp", groups, k) for k in order[1:]]
     over_tp = [swap("tp", size, k) for k in reversed(range(1, size))]
@@ -499,7 +502,7 @@
             moved = sum(term.astype(F32) for term in terms[distance + k]).astype(BF16)
             terms[k] = terms[k] + [move(moved)]
     summands = terms[0]
-    return tuple(finish(back, summands, queries, mixed, lse, returned, cap, heads))
+    return tuple(finish(back, summands, queries, mixed, lse, returned, turns, cap, heads))
 
 
 def solution(mesh):

time: 50.1 us -> 49.2 us (0.982)
  starting transfers between devices: 18.5 us -> 14.5 us
  waiting for transfers between devices: 12 us -> 15 us
    ppermute x12, starting transfers between devices: 18.5 us -> 14.5 us  [swap(): return lambda value: lax.ppermute(value, axis, pairs)]
    ppermute x12, waiting for transfers between devices: 12 us -> 15 us  [swap(): return lambda value: lax.ppermute(value, axis, pairs)]
  transfers between devices with their start and end apart: 12 -> 12, of which waited for: 6 -> 5; matrix products, arithmetic and copies ran while one was open for 0% -> 0% of each run, Pallas kernels for 25% -> 26%
where the time goes in v5:
time: 49.2 us; the launch traced here: 49.1 us
  Pallas kernels  18.6 us (38%)
  waiting for transfers between devices  15 us (30%)
  starting transfers between devices  14.5 us (29%)
  between operations  0.76 us (2%)
    ppermute x12, waiting for transfers between devices, swap(): return lambda value: lax.ppermute(value, axis, pairs)  15 us
    ppermute x12, starting transfers between devices, swap(): return lambda value: lax.ppermute(value, axis, pairs)  14.5 us
    pallas_call x1, Pallas kernels, past(): pl.pallas_call(past_kernel, grid_spec=pltpu.PrefetchScalarGridSpec(num_sc...  5.88 us
    pallas_call x1, Pallas kernels, base(): pl.pallas_call(functools.partial(base_kernel, size), out_shape=[jax.Shape...  5.73 us
    pallas_call x1, Pallas kernels, route(): pl.pallas_call(functools.partial(route_kernel, order, cap, entries), out_...  3.09 us
    pallas_call x1, Pallas kernels, finish(): pl.pallas_call(functools.partial(finish_kernel, turns, len(summands), cap...  2.86 us
  transfers between devices with their start and end apart: 12, of which 5 were waited for; matrix products, arithmetic and copies ran while one was open for 0% of the time, Pallas kernels for 26%

profile of v5, /device:TPU:0, one launch (start us, length us, event | category | flops | bytes accessed | tf_op | source)
XLA Modules:
  0.0 49.1 jit_solution(7334828763690780799)
XLA Ops:
  0.6 3.1 %route.1 = (bf16[1040,128]{1,0:T(8,128)(2,1)}, bf16[1040,128]{1,0:T(8,128)(2,1)}, bf16[1040,128]{1,0:T(8,128)(2,1)}, bf16[1040,128]{1,0:T(8,128)(2,1)}, bf16[64,64]{1,0:T(8,128)(2,1)}) custom-call(s32[1,64]{1,0:T(1,128)} %bitcast.8, s32[1,128]{1,0:T(1,128)} %bitcast.9, bf16[4,64,2048]{2,1,0:T(8,128)(2,1)} %hidden_hbm.1), custom_call_target="tpu_custom_call" | custom-call | flops 67108864 | bytes 2097152 | tf_op jit(solution)/shard_map/route/pallas_call | solution.py:105
  3.7 5.1 %collective-permute-start.2 = (bf16[1040,128]{1,0:T(8,128)(2,1)}, bf16[1040,128]{1,0:T(8,128)(2,1)S(1)}, u32[]{:S(2)}, u32[]{:S(2)}) collective-permute-start(bf16[1040,128]{1,0:T(8,128)(2,1)} %get-tuple-element.35), channel_id=1, source_target_pairs={{0,12},{4,8},{8,4},{12,0},{1,13},{5,9},{9,5},{13,1},{2,14},{6,10},... | collective-permute-start | bytes 798728 | tf_op jit(solution)/shard_map/ppermute | solution.py:33
  8.8 0.0 collective-permute-start.3
  8.8 0.6 %collective-permute-start.4 = (bf16[1040,128]{1,0:T(8,128)(2,1)}, bf16[1040,128]{1,0:T(8,128)(2,1)S(1)}, u32[]{:S(2)}, u32[]{:S(2)}) collective-permute-start(bf16[1040,128]{1,0:T(8,128)(2,1)} %get-tuple-element.37), channel_id=1, source_target_pairs={{0,4},{4,0},{8,12},{12,8},{1,5},{5,1},{9,13},{13,9},{2,6},{6,2},{1... | collective-permute-start | bytes 798728 | tf_op jit(solution)/shard_map/ppermute | solution.py:33
  9.5 0.0 copy-start
  9.5 0.0 copy-start.1
  9.5 0.0 copy-start.2
  9.5 0.0 copy-start.8
  9.5 5.7 %base.1 = (f32[256,512]{1,0:T(8,128)}, f32[256,512]{1,0:T(8,128)}, bf16[256,512]{1,0:T(8,128)(2,1)S(1)}, bf16[256,512]{1,0:T(8,128)(2,1)S(1)}) custom-call(bf16[256,2048]{1,0:T(8,128)(2,1)} %bitcast.7, bf16[2048,2048]{1,0:T(8,128)(2,1)} %projection_hbm.1), custom_call_target="tpu_custom_call" | custom-call | bytes 4096 | tf_op jit(solution)/shard_map/base/pallas_call | solution.py:151
  15.2 1.7 %collective-permute-start = (bf16[256,512]{1,0:T(8,128)(2,1)S(1)}, bf16[256,512]{1,0:T(8,128)(2,1)S(1)}, u32[]{:S(2)}, u32[]{:S(2)}) collective-permute-start(bf16[256,512]{1,0:T(8,128)(2,1)S(1)} %get-tuple-element.30), channel_id=1, source_target_pairs={{0,2},{1,3},{2,0},{3,1},{4,6},{5,7},{6,4},{7,5},{8,10},{9,11},{10,... | collective-permute-start | bytes 786440 | tf_op jit(solution)/shard_map/ppermute | solution.py:33
  16.9 0.0 copy-start.3
  16.9 0.0 copy-start.6
  16.9 0.0 copy-start.5
  16.9 0.0 copy-start.9
  17.0 0.4 collective-permute-start.1
  17.4 0.0 copy-done
  17.4 0.0 copy-done.1
  17.4 0.0 copy-done.2
  17.4 0.0 copy-done.8
  17.4 5.9 %past.1 = (f32[4,64,2048]{2,1,0:T(8,128)S(1)}, f32[64,128]{1,0:T(8,128)S(1)}) custom-call(s32[64]{0:T(128)S(1)} %copy-done.8, bf16[4,64,2048]{2,1,0:T(8,128)(2,1)S(1)} %copy-done, bf16[64,2,128,128]{3,2,1,0:T(8,128)(2,1)S(1)} %copy-done.1, bf16[64,2,128,128]{3,2,1,0:T(8,128)(2,1)S(1)} %copy-done.2), custom_call_target="tpu_custom_call" | custom-call | bytes 4096 | tf_op jit(solution)/shard_map/past/pallas_call | solution.py:228
  23.3 0.0 copy-start.4
  23.3 0.0 copy-start.7
  23.3 0.0 collective-permute-done.2.refs_1_
  23.3 8.4 %collective-permute-done.3.refs_2_ = bf16[1040,128]{1,0:T(8,128)(2,1)S(1)} collective-permute-done((bf16[1040,128]{1,0:T(8,128)(2,1)}, bf16[1040,128]{1,0:T(8,128)(2,1)S(1)}, u32[]{:S(2)}, u32[]{:S(2)}) %collective-permute-start.3) | collective-permute-done | bytes 266272 | tf_op jit(solution)/shard_map/ppermute | solution.py:33
  31.7 0.0 collective-permute-done.4.refs_3_
  31.7 0.0 copy-done.3
  31.7 0.0 copy-done.6
  31.7 0.8 %shrink.1 = (f32[16,256]{1,0:T(8,128)S(1)}, s32[1,256]{1,0:T(1,128)S(1)}) custom-call(bf16[512,2048]{1,0:T(8,128)(2,1)S(1)} %bitcast.5, bf16[1040,128]{1,0:T(8,128)(2,1)S(1)} %copy-done.6, bf16[1040,128]{1,0:T(8,128)(2,1)S(1)} %collective-permute-done.2.refs_1_, bf16[1040,128]{1,0:T(8,128)(2,1)S(1)} %collective-permute-done.3.refs_2_, ...), custom_call_target="tpu_custom_call" | custom-call | flops 536870912 | bytes 3145728 | tf_op jit(solution)/shard_map/shrink/pallas_call | solution.py:278
  32.5 0.3 collective-permute-start.5
  32.8 1.3 %collective-permute-start.6 = (f32[16,256]{1,0:T(8,128)S(1)}, f32[16,256]{1,0:T(8,128)S(1)}, u32[]{:S(2)}, u32[]{:S(2)}) collective-permute-start(f32[16,256]{1,0:T(8,128)S(1)} %get-tuple-element.39.refs_0_), channel_id=1, source_target_pairs={{0,2},{1,3},{2,0},{3,1},{4,6},{5,7},{6,4},{7,5},{8,10},{9,11},{10,... | collective-permute-start | bytes 49160 | tf_op jit(solution)/shard_map/ppermute | solution.py:33
  34.1 0.3 collective-permute-start.7
  34.4 1.4 %collective-permute-done.5.refs_1_ = f32[16,256]{1,0:T(8,128)S(1)} collective-permute-done((f32[16,256]{1,0:T(8,128)S(1)}, f32[16,256]{1,0:T(8,128)S(1)}, u32[]{:S(2)}, u32[]{:S(2)}) %collective-permute-start.5) | collective-permute-done | bytes 16416 | tf_op jit(solution)/shard_map/ppermute | solution.py:33
  35.8 0.7 %collective-permute-done.6.refs_2_ = f32[16,256]{1,0:T(8,128)S(1)} collective-permute-done((f32[16,256]{1,0:T(8,128)S(1)}, f32[16,256]{1,0:T(8,128)S(1)}, u32[]{:S(2)}, u32[]{:S(2)}) %collective-permute-start.6) | collective-permute-done | bytes 16416 | tf_op jit(solution)/shard_map/ppermute | solution.py:33
  36.5 0.0 collective-permute-done.7.refs_3_
  36.5 0.0 copy-done.5
  36.5 0.3 expand.1
  36.9 0.0 collective-permute-done.refs_1_
  36.9 0.0 collective-permute-done.1
  36.9 0.0 copy-done.9
  36.9 0.1 add_convert_fusion
  37.0 0.3 collective-permute-start.8
  37.3 2.5 %collective-permute-start.10 = (bf16[64,512]{1,0:T(8,128)(2,1)S(1)}, bf16[64,512]{1,0:T(8,128)(2,1)S(1)}, u32[]{:S(2)}, u32[]{:S(2)}) collective-permute-start(bf16[64,512]{1,0:T(8,128)(2,1)S(1)} %get-tuple-element.46), channel_id=1, source_target_pairs={{0,12},{4,8},{8,4},{12,0},{1,13},{5,9},{9,5},{13,1},{2,14},{6,10},... | collective-permute-start | bytes 196616 | tf_op jit(solution)/shard_map/ppermute | solution.py:33
  39.7 0.0 collective-permute-start.11
  39.8 1.9 %collective-permute-start.9 = (bf16[64,512]{1,0:T(8,128)(2,1)S(1)}, bf16[64,512]{1,0:T(8,128)(2,1)S(1)}, u32[]{:S(2)}, u32[]{:S(2)}) collective-permute-start(bf16[64,512]{1,0:T(8,128)(2,1)S(1)} %get-tuple-element.45), channel_id=1, source_target_pairs={{0,4},{4,0},{8,12},{12,8},{1,5},{5,1},{9,13},{13,9},{2,6},{6,2},{1... | collective-permute-start | bytes 196616 | tf_op jit(solution)/shard_map/ppermute | solution.py:33
  41.7 2.4 %collective-permute-done.10.refs_5_ = bf16[64,512]{1,0:T(8,128)(2,1)S(1)} collective-permute-done((bf16[64,512]{1,0:T(8,128)(2,1)S(1)}, bf16[64,512]{1,0:T(8,128)(2,1)S(1)}, u32[]{:S(2)}, u32[]{:S(2)}) %collective-permute-start.10) | collective-permute-done | bytes 65568 | tf_op jit(solution)/shard_map/ppermute | solution.py:33
  44.1 2.1 %collective-permute-done.11.refs_6_ = bf16[64,512]{1,0:T(8,128)(2,1)S(1)} collective-permute-done((bf16[64,512]{1,0:T(8,128)(2,1)S(1)}, bf16[64,512]{1,0:T(8,128)(2,1)S(1)}, u32[]{:S(2)}, u32[]{:S(2)}) %collective-permute-start.11) | collective-permute-done | bytes 65568 | tf_op jit(solution)/shard_map/ppermute | solution.py:33
  46.2 0.0 collective-permute-done.9.refs_4_
  46.2 0.0 collective-permute-done.8.refs_2_
  46.2 0.0 copy-done.4
  46.2 0.0 copy-done.7
  46.2 2.9 %finish.1 = (bf16[4,64,2048]{2,1,0:T(8,128)(2,1)}, bf16[4,64,512]{2,1,0:T(8,128)(2,1)}) custom-call(bf16[64,64]{1,0:T(8,128)(2,1)S(1)} %copy-done.7, bf16[4,64,2048]{2,1,0:T(8,128)(2,1)S(1)} %copy-done, f32[4,64,2048]{2,1,0:T(8,128)S(1)} %get-tuple-element.26.mixed_ref, f32[64,128]{1,0:T(8,128)S(1)} %get-tuple-element.27.lse_ref, f32[256,512]{1,0:T(8,128)S(1)} %copy-done.4, ...), custom_call_target="tpu_custom_call" | custom-call | flops 1073741824 | bytes 5242880 | tf_op jit(solution)/shard_map/finish/pallas_call | solution.py:435
Async XLA Ops:
  3.7 19.6 %collective-permute-start.2 = (bf16[1040,128]{1,0:T(8,128)(2,1)}, bf16[1040,128]{1,0:T(8,128)(2,1)S(1)}, u32[]{:S(2)}, u32[]{:S(2)}) collective-permute-start(bf16[1040,128]{1,0:T(8,128)(2,1)} %get-tuple-element.35), channel_id=1, source_target_pairs={{0,12},{4,8},{8,4},{12,0},{1,13},{5,9},{9,5},{13,1},{2,14},{6,10},... | collective-permute-start | bytes 798728 | tf_op jit(solution)/shard_map/ppermute | solution.py:33
  8.8 22.9 %collective-permute-start.3 = (bf16[1040,128]{1,0:T(8,128)(2,1)}, bf16[1040,128]{1,0:T(8,128)(2,1)S(1)}, u32[]{:S(2)}, u32[]{:S(2)}) collective-permute-start(bf16[1040,128]{1,0:T(8,128)(2,1)} %get-tuple-element.36), channel_id=1, source_target_pairs={{0,8},{4,12},{8,0},{12,4},{1,9},{5,13},{9,1},{13,5},{2,10},{6,14},... | collective-permute-start | bytes 798728 | tf_op jit(solution)/shard_map/ppermute | solution.py:33
  8.8 22.9 %collective-permute-start.4 = (bf16[1040,128]{1,0:T(8,128)(2,1)}, bf16[1040,128]{1,0:T(8,128)(2,1)S(1)}, u32[]{:S(2)}, u32[]{:S(2)}) collective-permute-start(bf16[1040,128]{1,0:T(8,128)(2,1)} %get-tuple-element.37), channel_id=1, source_target_pairs={{0,4},{4,0},{8,12},{12,8},{1,5},{5,1},{9,13},{13,9},{2,6},{6,2},{1... | collective-permute-start | bytes 798728 | tf_op jit(solution)/shard_map/ppermute | solution.py:33
  9.5 7.9 %copy-start = (bf16[4,64,2048]{2,1,0:T(8,128)(2,1)S(1)}, bf16[4,64,2048]{2,1,0:T(8,128)(2,1)}, u32[]{:S(2)}) copy-start(bf16[4,64,2048]{2,1,0:T(8,128)(2,1)} %query_ref.3) | copy-start | bytes 3145732
  9.5 7.9 %copy-start.1 = (bf16[64,2,128,128]{3,2,1,0:T(8,128)(2,1)S(1)}, bf16[64,2,128,128]{3,2,1,0:T(8,128)(2,1)}, u32[]{:S(2)}) copy-start(bf16[64,2,128,128]{3,2,1,0:T(8,128)(2,1)} %key_ref.1) | copy-start | bytes 12582916
  9.5 7.9 %copy-start.2 = (bf16[64,2,128,128]{3,2,1,0:T(8,128)(2,1)S(1)}, bf16[64,2,128,128]{3,2,1,0:T(8,128)(2,1)}, u32[]{:S(2)}) copy-start(bf16[64,2,128,128]{3,2,1,0:T(8,128)(2,1)} %value_ref.1) | copy-start | bytes 12582916
  9.5 7.9 %copy-start.8 = (s32[64]{0:T(128)S(1)}, s32[64]{0:T(128)}, u32[]{:S(2)}) copy-start(s32[64]{0:T(128)} %lengths_ref.1) | copy-start | bytes 772
  15.2 21.7 %collective-permute-start = (bf16[256,512]{1,0:T(8,128)(2,1)S(1)}, bf16[256,512]{1,0:T(8,128)(2,1)S(1)}, u32[]{:S(2)}, u32[]{:S(2)}) collective-permute-start(bf16[256,512]{1,0:T(8,128)(2,1)S(1)} %get-tuple-element.30), channel_id=1, source_target_pairs={{0,2},{1,3},{2,0},{3,1},{4,6},{5,7},{6,4},{7,5},{8,10},{9,11},{10,... | collective-permute-start | bytes 786440 | tf_op jit(solution)/shard_map/ppermute | solution.py:33
  16.9 14.8 %copy-start.3 = (bf16[32,16,2048]{2,1,0:T(8,128)(2,1)S(1)}, bf16[32,16,2048]{2,1,0:T(8,128)(2,1)}, u32[]{:S(2)}) copy-start(bf16[32,16,2048]{2,1,0:T(8,128)(2,1)} %param.15) | copy-start | bytes 6291460
  16.9 14.8 %copy-start.6 = (bf16[1040,128]{1,0:T(8,128)(2,1)S(1)}, bf16[1040,128]{1,0:T(8,128)(2,1)}, u32[]{:S(2)}) copy-start(bf16[1040,128]{1,0:T(8,128)(2,1)} %get-tuple-element.34.refs_0_) | copy-start | bytes 798724
  16.9 19.6 %copy-start.5 = (bf16[32,16,512]{2,1,0:T(8,128)(2,1)S(1)}, bf16[32,16,512]{2,1,0:T(8,128)(2,1)}, u32[]{:S(2)}) copy-start(bf16[32,16,512]{2,1,0:T(8,128)(2,1)} %param.16) | copy-start | bytes 1572868
  16.9 20.0 %copy-start.9 = (f32[256,512]{1,0:T(8,128)S(1)}, f32[256,512]{1,0:T(8,128)}, u32[]{:S(2)}) copy-start(f32[256,512]{1,0:T(8,128)} %get-tuple-element.43) | copy-start | bytes 1572868
  17.0 19.9 %collective-permute-start.1 = (bf16[256,512]{1,0:T(8,128)(2,1)S(1)}, bf16[256,512]{1,0:T(8,128)(2,1)S(1)}, u32[]{:S(2)}, u32[]{:S(2)}) collective-permute-start(bf16[256,512]{1,0:T(8,128)(2,1)S(1)} %get-tuple-element.32), channel_id=1, source_target_pairs={{0,2},{1,3},{2,0},{3,1},{4,6},{5,7},{6,4},{7,5},{8,10},{9,11},{10,... | collective-permute-start | bytes 786440 | tf_op jit(solution)/shard_map/ppermute | solution.py:33
  23.3 22.9 %copy-start.4 = (f32[256,512]{1,0:T(8,128)S(1)}, f32[256,512]{1,0:T(8,128)}, u32[]{:S(2)}) copy-start(f32[256,512]{1,0:T(8,128)} %get-tuple-element.41.refs_0_) | copy-start | bytes 1572868
  23.3 22.9 %copy-start.7 = (bf16[64,64]{1,0:T(8,128)(2,1)S(1)}, bf16[64,64]{1,0:T(8,128)(2,1)}, u32[]{:S(2)}) copy-start(bf16[64,64]{1,0:T(8,128)(2,1)} %get-tuple-element.25.back_ref) | copy-start | bytes 24580
  32.5 3.4 %collective-permute-start.5 = (f32[16,256]{1,0:T(8,128)S(1)}, f32[16,256]{1,0:T(8,128)S(1)}, u32[]{:S(2)}, u32[]{:S(2)}) collective-permute-start(f32[16,256]{1,0:T(8,128)S(1)} %get-tuple-element.39.refs_0_), channel_id=1, source_target_pairs={{0,3},{1,2},{2,1},{3,0},{4,7},{5,6},{6,5},{7,4},{8,11},{9,10},{10,... | collective-permute-start | bytes 49160 | tf_op jit(solution)/shard_map/ppermute | solution.py:33
  32.8 3.7 %collective-permute-start.6 = (f32[16,256]{1,0:T(8,128)S(1)}, f32[16,256]{1,0:T(8,128)S(1)}, u32[]{:S(2)}, u32[]{:S(2)}) collective-permute-start(f32[16,256]{1,0:T(8,128)S(1)} %get-tuple-element.39.refs_0_), channel_id=1, source_target_pairs={{0,2},{1,3},{2,0},{3,1},{4,6},{5,7},{6,4},{7,5},{8,10},{9,11},{10,... | collective-permute-start | bytes 49160 | tf_op jit(solution)/shard_map/ppermute | solution.py:33
  34.1 2.4 %collective-permute-start.7 = (f32[16,256]{1,0:T(8,128)S(1)}, f32[16,256]{1,0:T(8,128)S(1)}, u32[]{:S(2)}, u32[]{:S(2)}) collective-permute-start(f32[16,256]{1,0:T(8,128)S(1)} %get-tuple-element.39.refs_0_), channel_id=1, source_target_pairs={{0,1},{1,0},{2,3},{3,2},{4,5},{5,4},{6,7},{7,6},{8,9},{9,8},{10,11... | collective-permute-start | bytes 49160 | tf_op jit(solution)/shard_map/ppermute | solution.py:33
  37.0 9.2 %collective-permute-start.8 = (bf16[256,512]{1,0:T(8,128)(2,1)S(1)}, bf16[256,512]{1,0:T(8,128)(2,1)S(1)}, u32[]{:S(2)}, u32[]{:S(2)}) collective-permute-start(bf16[256,512]{1,0:T(8,128)(2,1)S(1)} %add_convert_fusion), channel_id=1, source_target_pairs={{0,1},{1,0},{2,3},{3,2},{4,5},{5,4},{6,7},{7,6},{8,9},{9,8},{10,11... | collective-permute-start | bytes 786440 | tf_op jit(solution)/shard_map/ppermute | solution.py:33
  37.3 6.8 %collective-permute-start.10 = (bf16[64,512]{1,0:T(8,128)(2,1)S(1)}, bf16[64,512]{1,0:T(8,128)(2,1)S(1)}, u32[]{:S(2)}, u32[]{:S(2)}) collective-permute-start(bf16[64,512]{1,0:T(8,128)(2,1)S(1)} %get-tuple-element.46), channel_id=1, source_target_pairs={{0,12},{4,8},{8,4},{12,0},{1,13},{5,9},{9,5},{13,1},{2,14},{6,10},... | collective-permute-start | bytes 196616 | tf_op jit(solution)/shard_map/ppermute | solution.py:33
  39.7 6.4 %collective-permute-start.11 = (bf16[64,512]{1,0:T(8,128)(2,1)S(1)}, bf16[64,512]{1,0:T(8,128)(2,1)S(1)}, u32[]{:S(2)}, u32[]{:S(2)}) collective-permute-start(bf16[64,512]{1,0:T(8,128)(2,1)S(1)} %get-tuple-element.47), channel_id=1, source_target_pairs={{0,8},{4,12},{8,0},{12,4},{1,9},{5,13},{9,1},{13,5},{2,10},{6,14},... | collective-permute-start | bytes 196616 | tf_op jit(solution)/shard_map/ppermute | solution.py:33
  39.8 6.4 %collective-permute-start.9 = (bf16[64,512]{1,0:T(8,128)(2,1)S(1)}, bf16[64,512]{1,0:T(8,128)(2,1)S(1)}, u32[]{:S(2)}, u32[]{:S(2)}) collective-permute-start(bf16[64,512]{1,0:T(8,128)(2,1)S(1)} %get-tuple-element.45), channel_id=1, source_target_pairs={{0,4},{4,0},{8,12},{12,8},{1,5},{5,1},{9,13},{13,9},{2,6},{6,2},{1... | collective-permute-start | bytes 196616 | tf_op jit(solution)/shard_map/ppermute | solution.py:33

commit v6 on v5

--- a/solution.py
+++ b/solution.py
@@ -396,27 +396,31 @@
     raised = [jnp.exp(part - top) for part in fresh]
     scale = 1.0 / (over_steps(raised, jnp.add) + old)
     weights = [part * scale for part in raised]
-    old = jnp.transpose(old * scale)[:seqs, :]
+    old = old * scale
+    high = old.astype(BF16).astype(F32)
+    halves = jnp.where(iota((rows, LANES), 1) < seqs, high, old - high)
+    ones = jnp.ones((LANES, size), BF16)
+
+    def diagonal(packed, row):
+        return jnp.where(same, packed[row : row + 1], 0.0).astype(BF16)
+
     for g, s in units:
         count = pl.cdiv((s + 1) * seqs, LANES)
         first = (g * steps + s) * share
-        spread = []
-        for h in range(share):
-            row = slice(first + h, first + h + 1)
-            spread.append(
-                jnp.concatenate(
-                    [jnp.where(same, weights[c][row], 0.0).astype(BF16) for c in range(count)],
-                    axis=1,
-                )
-            )
+        spread = [
+            jnp.concatenate([diagonal(part, first + h) for part in weights[:count]], axis=1)
+            for h in range(share)
+        ]
         mixed = jnp.dot(
             jnp.concatenate(spread, axis=0),
             values[g][: count * LANES],
             preferred_element_type=F32,
         )
+        spread = [diagonal(halves, first + h) for h in range(share)]
+        kept = jnp.dot(jnp.concatenate(spread, axis=0), ones, preferred_element_type=F32)
         for h in range(share):
-            total = mixed[h * seqs : (h + 1) * seqs]
-            total = total + mixed_ref[s, :, lanes(g, h)] * old[:, first + h : first + h + 1]
+            cut = slice(h * seqs, (h + 1) * seqs)
+            total = mixed[cut] + mixed_ref[s, :, lanes(g, h)] * kept[cut]
             out_ref[s, :, lanes(g, h)] = total.astype(BF16)
         part = (s, slice(None), pl.ds(g * share * size, share * size))
         copies.append(

time: 49.2 us -> 48.5 us (0.986)
  Pallas kernels: 18.6 us -> 18 us
    pallas_call x1, Pallas kernels: 2.86 us -> 2.18 us  [finish(): pl.pallas_call(functools.partial(finish_kernel, turns, len(summands), cap...]
where the time goes in v6:
time: 48.5 us; the launch traced here: 48.4 us
  Pallas kernels  18 us (37%)
  waiting for transfers between devices  15 us (31%)
  starting transfers between devices  14.5 us (30%)
  between operations  0.76 us (2%)
    ppermute x12, waiting for transfers between devices, swap(): return lambda value: lax.ppermute(value, axis, pairs)  15 us
    ppermute x12, starting transfers between devices, swap(): return lambda value: lax.ppermute(value, axis, pairs)  14.5 us
    pallas_call x1, Pallas kernels, past(): pl.pallas_call(past_kernel, grid_spec=pltpu.PrefetchScalarGridSpec(num_sc...  5.88 us
    pallas_call x1, Pallas kernels, base(): pl.pallas_call(functools.partial(base_kernel, size), out_shape=[jax.Shape...  5.73 us
    pallas_call x1, Pallas kernels, route(): pl.pallas_call(functools.partial(route_kernel, order, cap, entries), out_...  3.09 us
    pallas_call x1, Pallas kernels, finish(): pl.pallas_call(functools.partial(finish_kernel, turns, len(summands), cap...  2.18 us
  transfers between devices with their start and end apart: 12, of which 5 were waited for; matrix products, arithmetic and copies ran while one was open for 0% of the time, Pallas kernels for 26%

profile of v6, /device:TPU:0, one launch (start us, length us, event | category | flops | bytes accessed | tf_op | source)
XLA Modules:
  0.0 48.4 jit_solution(14036002514294594233)
XLA Ops:
  0.6 3.1 %route.1 = (bf16[1040,128]{1,0:T(8,128)(2,1)}, bf16[1040,128]{1,0:T(8,128)(2,1)}, bf16[1040,128]{1,0:T(8,128)(2,1)}, bf16[1040,128]{1,0:T(8,128)(2,1)}, bf16[64,64]{1,0:T(8,128)(2,1)}) custom-call(s32[1,64]{1,0:T(1,128)} %bitcast.8, s32[1,128]{1,0:T(1,128)} %bitcast.9, bf16[4,64,2048]{2,1,0:T(8,128)(2,1)} %hidden_hbm.1), custom_call_target="tpu_custom_call" | custom-call | flops 67108864 | bytes 2097152 | tf_op jit(solution)/shard_map/route/pallas_call | solution.py:105
  3.7 5.1 %collective-permute-start.2 = (bf16[1040,128]{1,0:T(8,128)(2,1)}, bf16[1040,128]{1,0:T(8,128)(2,1)S(1)}, u32[]{:S(2)}, u32[]{:S(2)}) collective-permute-start(bf16[1040,128]{1,0:T(8,128)(2,1)} %get-tuple-element.35), channel_id=1, source_target_pairs={{0,12},{4,8},{8,4},{12,0},{1,13},{5,9},{9,5},{13,1},{2,14},{6,10},... | collective-permute-start | bytes 798728 | tf_op jit(solution)/shard_map/ppermute | solution.py:33
  8.8 0.0 collective-permute-start.3
  8.8 0.6 %collective-permute-start.4 = (bf16[1040,128]{1,0:T(8,128)(2,1)}, bf16[1040,128]{1,0:T(8,128)(2,1)S(1)}, u32[]{:S(2)}, u32[]{:S(2)}) collective-permute-start(bf16[1040,128]{1,0:T(8,128)(2,1)} %get-tuple-element.37), channel_id=1, source_target_pairs={{0,4},{4,0},{8,12},{12,8},{1,5},{5,1},{9,13},{13,9},{2,6},{6,2},{1... | collective-permute-start | bytes 798728 | tf_op jit(solution)/shard_map/ppermute | solution.py:33
  9.5 0.0 copy-start
  9.5 0.0 copy-start.1
  9.5 0.0 copy-start.2
  9.5 0.0 copy-start.8
  9.5 5.7 %base.1 = (f32[256,512]{1,0:T(8,128)}, f32[256,512]{1,0:T(8,128)}, bf16[256,512]{1,0:T(8,128)(2,1)S(1)}, bf16[256,512]{1,0:T(8,128)(2,1)S(1)}) custom-call(bf16[256,2048]{1,0:T(8,128)(2,1)} %bitcast.7, bf16[2048,2048]{1,0:T(8,128)(2,1)} %projection_hbm.1), custom_call_target="tpu_custom_call" | custom-call | bytes 4096 | tf_op jit(solution)/shard_map/base/pallas_call | solution.py:151
  15.2 1.7 %collective-permute-start = (bf16[256,512]{1,0:T(8,128)(2,1)S(1)}, bf16[256,512]{1,0:T(8,128)(2,1)S(1)}, u32[]{:S(2)}, u32[]{:S(2)}) collective-permute-start(bf16[256,512]{1,0:T(8,128)(2,1)S(1)} %get-tuple-element.30), channel_id=1, source_target_pairs={{0,2},{1,3},{2,0},{3,1},{4,6},{5,7},{6,4},{7,5},{8,10},{9,11},{10,... | collective-permute-start | bytes 786440 | tf_op jit(solution)/shard_map/ppermute | solution.py:33
  16.9 0.0 copy-start.3
  16.9 0.0 copy-start.6
  16.9 0.0 copy-start.5
  16.9 0.0 copy-start.9
  17.0 0.4 collective-permute-start.1
  17.4 0.0 copy-done
  17.4 0.0 copy-done.1
  17.4 0.0 copy-done.2
  17.4 0.0 copy-done.8
  17.4 5.9 %past.1 = (f32[4,64,2048]{2,1,0:T(8,128)S(1)}, f32[64,128]{1,0:T(8,128)S(1)}) custom-call(s32[64]{0:T(128)S(1)} %copy-done.8, bf16[4,64,2048]{2,1,0:T(8,128)(2,1)S(1)} %copy-done, bf16[64,2,128,128]{3,2,1,0:T(8,128)(2,1)S(1)} %copy-done.1, bf16[64,2,128,128]{3,2,1,0:T(8,128)(2,1)S(1)} %copy-done.2), custom_call_target="tpu_custom_call" | custom-call | bytes 4096 | tf_op jit(solution)/shard_map/past/pallas_call | solution.py:228
  23.3 0.0 copy-start.4
  23.3 0.0 copy-start.7
  23.3 0.0 collective-permute-done.2.refs_1_
  23.3 8.4 %collective-permute-done.3.refs_2_ = bf16[1040,128]{1,0:T(8,128)(2,1)S(1)} collective-permute-done((bf16[1040,128]{1,0:T(8,128)(2,1)}, bf16[1040,128]{1,0:T(8,128)(2,1)S(1)}, u32[]{:S(2)}, u32[]{:S(2)}) %collective-permute-start.3) | collective-permute-done | bytes 266272 | tf_op jit(solution)/shard_map/ppermute | solution.py:33
  31.7 0.0 collective-permute-done.4.refs_3_
  31.7 0.0 copy-done.3
  31.7 0.0 copy-done.6
  31.7 0.8 %shrink.1 = (f32[16,256]{1,0:T(8,128)S(1)}, s32[1,256]{1,0:T(1,128)S(1)}) custom-call(bf16[512,2048]{1,0:T(8,128)(2,1)S(1)} %bitcast.5, bf16[1040,128]{1,0:T(8,128)(2,1)S(1)} %copy-done.6, bf16[1040,128]{1,0:T(8,128)(2,1)S(1)} %collective-permute-done.2.refs_1_, bf16[1040,128]{1,0:T(8,128)(2,1)S(1)} %collective-permute-done.3.refs_2_, ...), custom_call_target="tpu_custom_call" | custom-call | flops 536870912 | bytes 3145728 | tf_op jit(solution)/shard_map/shrink/pallas_call | solution.py:278
  32.5 0.3 collective-permute-start.5
  32.8 1.3 %collective-permute-start.6 = (f32[16,256]{1,0:T(8,128)S(1)}, f32[16,256]{1,0:T(8,128)S(1)}, u32[]{:S(2)}, u32[]{:S(2)}) collective-permute-start(f32[16,256]{1,0:T(8,128)S(1)} %get-tuple-element.39.refs_0_), channel_id=1, source_target_pairs={{0,2},{1,3},{2,0},{3,1},{4,6},{5,7},{6,4},{7,5},{8,10},{9,11},{10,... | collective-permute-start | bytes 49160 | tf_op jit(solution)/shard_map/ppermute | solution.py:33
  34.1 0.3 collective-permute-start.7
  34.4 1.4 %collective-permute-done.5.refs_1_ = f32[16,256]{1,0:T(8,128)S(1)} collective-permute-done((f32[16,256]{1,0:T(8,128)S(1)}, f32[16,256]{1,0:T(8,128)S(1)}, u32[]{:S(2)}, u32[]{:S(2)}) %collective-permute-start.5) | collective-permute-done | bytes 16416 | tf_op jit(solution)/shard_map/ppermute | solution.py:33
  35.8 0.7 %collective-permute-done.6.refs_2_ = f32[16,256]{1,0:T(8,128)S(1)} collective-permute-done((f32[16,256]{1,0:T(8,128)S(1)}, f32[16,256]{1,0:T(8,128)S(1)}, u32[]{:S(2)}, u32[]{:S(2)}) %collective-permute-start.6) | collective-permute-done | bytes 16416 | tf_op jit(solution)/shard_map/ppermute | solution.py:33
  36.5 0.0 collective-permute-done.7.refs_3_
  36.5 0.0 copy-done.5
  36.5 0.3 expand.1
  36.9 0.0 collective-permute-done.refs_1_
  36.9 0.0 collective-permute-done.1
  36.9 0.0 copy-done.9
  36.9 0.1 add_convert_fusion
  37.0 0.3 collective-permute-start.8
  37.3 2.5 %collective-permute-start.10 = (bf16[64,512]{1,0:T(8,128)(2,1)S(1)}, bf16[64,512]{1,0:T(8,128)(2,1)S(1)}, u32[]{:S(2)}, u32[]{:S(2)}) collective-permute-start(bf16[64,512]{1,0:T(8,128)(2,1)S(1)} %get-tuple-element.46), channel_id=1, source_target_pairs={{0,12},{4,8},{8,4},{12,0},{1,13},{5,9},{9,5},{13,1},{2,14},{6,10},... | collective-permute-start | bytes 196616 | tf_op jit(solution)/shard_map/ppermute | solution.py:33
  39.7 0.0 collective-permute-start.11
  39.8 1.9 %collective-permute-start.9 = (bf16[64,512]{1,0:T(8,128)(2,1)S(1)}, bf16[64,512]{1,0:T(8,128)(2,1)S(1)}, u32[]{:S(2)}, u32[]{:S(2)}) collective-permute-start(bf16[64,512]{1,0:T(8,128)(2,1)S(1)} %get-tuple-element.45), channel_id=1, source_target_pairs={{0,4},{4,0},{8,12},{12,8},{1,5},{5,1},{9,13},{13,9},{2,6},{6,2},{1... | collective-permute-start | bytes 196616 | tf_op jit(solution)/shard_map/ppermute | solution.py:33
  41.7 2.4 %collective-permute-done.10.refs_5_ = bf16[64,512]{1,0:T(8,128)(2,1)S(1)} collective-permute-done((bf16[64,512]{1,0:T(8,128)(2,1)S(1)}, bf16[64,512]{1,0:T(8,128)(2,1)S(1)}, u32[]{:S(2)}, u32[]{:S(2)}) %collective-permute-start.10) | collective-permute-done | bytes 65568 | tf_op jit(solution)/shard_map/ppermute | solution.py:33
  44.1 2.1 %collective-permute-done.11.refs_6_ = bf16[64,512]{1,0:T(8,128)(2,1)S(1)} collective-permute-done((bf16[64,512]{1,0:T(8,128)(2,1)S(1)}, bf16[64,512]{1,0:T(8,128)(2,1)S(1)}, u32[]{:S(2)}, u32[]{:S(2)}) %collective-permute-start.11) | collective-permute-done | bytes 65568 | tf_op jit(solution)/shard_map/ppermute | solution.py:33
  46.2 0.0 collective-permute-done.9.refs_4_
  46.2 0.0 collective-permute-done.8.refs_2_
  46.2 0.0 copy-done.4
  46.2 0.0 copy-done.7
  46.2 2.2 %finish.1 = (bf16[4,64,2048]{2,1,0:T(8,128)(2,1)}, bf16[4,64,512]{2,1,0:T(8,128)(2,1)}) custom-call(bf16[64,64]{1,0:T(8,128)(2,1)S(1)} %copy-done.7, bf16[4,64,2048]{2,1,0:T(8,128)(2,1)S(1)} %copy-done, f32[4,64,2048]{2,1,0:T(8,128)S(1)} %get-tuple-element.26.mixed_ref, f32[64,128]{1,0:T(8,128)S(1)} %get-tuple-element.27.lse_ref, f32[256,512]{1,0:T(8,128)S(1)} %copy-done.4, ...), custom_call_target="tpu_custom_call" | custom-call | flops 1073741824 | bytes 5242880 | tf_op jit(solution)/shard_map/finish/pallas_call | solution.py:439
Async XLA Ops:
  3.7 19.6 %collective-permute-start.2 = (bf16[1040,128]{1,0:T(8,128)(2,1)}, bf16[1040,128]{1,0:T(8,128)(2,1)S(1)}, u32[]{:S(2)}, u32[]{:S(2)}) collective-permute-start(bf16[1040,128]{1,0:T(8,128)(2,1)} %get-tuple-element.35), channel_id=1, source_target_pairs={{0,12},{4,8},{8,4},{12,0},{1,13},{5,9},{9,5},{13,1},{2,14},{6,10},... | collective-permute-start | bytes 798728 | tf_op jit(solution)/shard_map/ppermute | solution.py:33
  8.8 22.9 %collective-permute-start.3 = (bf16[1040,128]{1,0:T(8,128)(2,1)}, bf16[1040,128]{1,0:T(8,128)(2,1)S(1)}, u32[]{:S(2)}, u32[]{:S(2)}) collective-permute-start(bf16[1040,128]{1,0:T(8,128)(2,1)} %get-tuple-element.36), channel_id=1, source_target_pairs={{0,8},{4,12},{8,0},{12,4},{1,9},{5,13},{9,1},{13,5},{2,10},{6,14},... | collective-permute-start | bytes 798728 | tf_op jit(solution)/shard_map/ppermute | solution.py:33
  8.8 22.9 %collective-permute-start.4 = (bf16[1040,128]{1,0:T(8,128)(2,1)}, bf16[1040,128]{1,0:T(8,128)(2,1)S(1)}, u32[]{:S(2)}, u32[]{:S(2)}) collective-permute-start(bf16[1040,128]{1,0:T(8,128)(2,1)} %get-tuple-element.37), channel_id=1, source_target_pairs={{0,4},{4,0},{8,12},{12,8},{1,5},{5,1},{9,13},{13,9},{2,6},{6,2},{1... | collective-permute-start | bytes 798728 | tf_op jit(solution)/shard_map/ppermute | solution.py:33
  9.5 7.9 %copy-start = (bf16[4,64,2048]{2,1,0:T(8,128)(2,1)S(1)}, bf16[4,64,2048]{2,1,0:T(8,128)(2,1)}, u32[]{:S(2)}) copy-start(bf16[4,64,2048]{2,1,0:T(8,128)(2,1)} %query_ref.3) | copy-start | bytes 3145732
  9.5 7.9 %copy-start.1 = (bf16[64,2,128,128]{3,2,1,0:T(8,128)(2,1)S(1)}, bf16[64,2,128,128]{3,2,1,0:T(8,128)(2,1)}, u32[]{:S(2)}) copy-start(bf16[64,2,128,128]{3,2,1,0:T(8,128)(2,1)} %key_ref.1) | copy-start | bytes 12582916
  9.5 7.9 %copy-start.2 = (bf16[64,2,128,128]{3,2,1,0:T(8,128)(2,1)S(1)}, bf16[64,2,128,128]{3,2,1,0:T(8,128)(2,1)}, u32[]{:S(2)}) copy-start(bf16[64,2,128,128]{3,2,1,0:T(8,128)(2,1)} %value_ref.1) | copy-start | bytes 12582916
  9.5 7.9 %copy-start.8 = (s32[64]{0:T(128)S(1)}, s32[64]{0:T(128)}, u32[]{:S(2)}) copy-start(s32[64]{0:T(128)} %lengths_ref.1) | copy-start | bytes 772
  15.2 21.7 %collective-permute-start = (bf16[256,512]{1,0:T(8,128)(2,1)S(1)}, bf16[256,512]{1,0:T(8,128)(2,1)S(1)}, u32[]{:S(2)}, u32[]{:S(2)}) collective-permute-start(bf16[256,512]{1,0:T(8,128)(2,1)S(1)} %get-tuple-element.30), channel_id=1, source_target_pairs={{0,2},{1,3},{2,0},{3,1},{4,6},{5,7},{6,4},{7,5},{8,10},{9,11},{10,... | collective-permute-start | bytes 786440 | tf_op jit(solution)/shard_map/ppermute | solution.py:33
  16.9 14.8 %copy-start.3 = (bf16[32,16,2048]{2,1,0:T(8,128)(2,1)S(1)}, bf16[32,16,2048]{2,1,0:T(8,128)(2,1)}, u32[]{:S(2)}) copy-start(bf16[32,16,2048]{2,1,0:T(8,128)(2,1)} %param.15) | copy-start | bytes 6291460
  16.9 14.8 %copy-start.6 = (bf16[1040,128]{1,0:T(8,128)(2,1)S(1)}, bf16[1040,128]{1,0:T(8,128)(2,1)}, u32[]{:S(2)}) copy-start(bf16[1040,128]{1,0:T(8,128)(2,1)} %get-tuple-element.34.refs_0_) | copy-start | bytes 798724
  16.9 19.6 %copy-start.5 = (bf16[32,16,512]{2,1,0:T(8,128)(2,1)S(1)}, bf16[32,16,512]{2,1,0:T(8,128)(2,1)}, u32[]{:S(2)}) copy-start(bf16[32,16,512]{2,1,0:T(8,128)(2,1)} %param.16) | copy-start | bytes 1572868
  16.9 20.0 %copy-start.9 = (f32[256,512]{1,0:T(8,128)S(1)}, f32[256,512]{1,0:T(8,128)}, u32[]{:S(2)}) copy-start(f32[256,512]{1,0:T(8,128)} %get-tuple-element.43) | copy-start | bytes 1572868
  17.0 19.9 %collective-permute-start.1 = (bf16[256,512]{1,0:T(8,128)(2,1)S(1)}, bf16[256,512]{1,0:T(8,128)(2,1)S(1)}, u32[]{:S(2)}, u32[]{:S(2)}) collective-permute-start(bf16[256,512]{1,0:T(8,128)(2,1)S(1)} %get-tuple-element.32), channel_id=1, source_target_pairs={{0,2},{1,3},{2,0},{3,1},{4,6},{5,7},{6,4},{7,5},{8,10},{9,11},{10,... | collective-permute-start | bytes 786440 | tf_op jit(solution)/shard_map/ppermute | solution.py:33
  23.3 22.9 %copy-start.4 = (f32[256,512]{1,0:T(8,128)S(1)}, f32[256,512]{1,0:T(8,128)}, u32[]{:S(2)}) copy-start(f32[256,512]{1,0:T(8,128)} %get-tuple-element.41.refs_0_) | copy-start | bytes 1572868
  23.3 22.9 %copy-start.7 = (bf16[64,64]{1,0:T(8,128)(2,1)S(1)}, bf16[64,64]{1,0:T(8,128)(2,1)}, u32[]{:S(2)}) copy-start(bf16[64,64]{1,0:T(8,128)(2,1)} %get-tuple-element.25.back_ref) | copy-start | bytes 24580
  32.5 3.4 %collective-permute-start.5 = (f32[16,256]{1,0:T(8,128)S(1)}, f32[16,256]{1,0:T(8,128)S(1)}, u32[]{:S(2)}, u32[]{:S(2)}) collective-permute-start(f32[16,256]{1,0:T(8,128)S(1)} %get-tuple-element.39.refs_0_), channel_id=1, source_target_pairs={{0,3},{1,2},{2,1},{3,0},{4,7},{5,6},{6,5},{7,4},{8,11},{9,10},{10,... | collective-permute-start | bytes 49160 | tf_op jit(solution)/shard_map/ppermute | solution.py:33
  32.8 3.7 %collective-permute-start.6 = (f32[16,256]{1,0:T(8,128)S(1)}, f32[16,256]{1,0:T(8,128)S(1)}, u32[]{:S(2)}, u32[]{:S(2)}) collective-permute-start(f32[16,256]{1,0:T(8,128)S(1)} %get-tuple-element.39.refs_0_), channel_id=1, source_target_pairs={{0,2},{1,3},{2,0},{3,1},{4,6},{5,7},{6,4},{7,5},{8,10},{9,11},{10,... | collective-permute-start | bytes 49160 | tf_op jit(solution)/shard_map/ppermute | solution.py:33
  34.1 2.4 %collective-permute-start.7 = (f32[16,256]{1,0:T(8,128)S(1)}, f32[16,256]{1,0:T(8,128)S(1)}, u32[]{:S(2)}, u32[]{:S(2)}) collective-permute-start(f32[16,256]{1,0:T(8,128)S(1)} %get-tuple-element.39.refs_0_), channel_id=1, source_target_pairs={{0,1},{1,0},{2,3},{3,2},{4,5},{5,4},{6,7},{7,6},{8,9},{9,8},{10,11... | collective-permute-start | bytes 49160 | tf_op jit(solution)/shard_map/ppermute | solution.py:33
  37.0 9.2 %collective-permute-start.8 = (bf16[256,512]{1,0:T(8,128)(2,1)S(1)}, bf16[256,512]{1,0:T(8,128)(2,1)S(1)}, u32[]{:S(2)}, u32[]{:S(2)}) collective-permute-start(bf16[256,512]{1,0:T(8,128)(2,1)S(1)} %add_convert_fusion), channel_id=1, source_target_pairs={{0,1},{1,0},{2,3},{3,2},{4,5},{5,4},{6,7},{7,6},{8,9},{9,8},{10,11... | collective-permute-start | bytes 786440 | tf_op jit(solution)/shard_map/ppermute | solution.py:33
  37.3 6.8 %collective-permute-start.10 = (bf16[64,512]{1,0:T(8,128)(2,1)S(1)}, bf16[64,512]{1,0:T(8,128)(2,1)S(1)}, u32[]{:S(2)}, u32[]{:S(2)}) collective-permute-start(bf16[64,512]{1,0:T(8,128)(2,1)S(1)} %get-tuple-element.46), channel_id=1, source_target_pairs={{0,12},{4,8},{8,4},{12,0},{1,13},{5,9},{9,5},{13,1},{2,14},{6,10},... | collective-permute-start | bytes 196616 | tf_op jit(solution)/shard_map/ppermute | solution.py:33
  39.7 6.4 %collective-permute-start.11 = (bf16[64,512]{1,0:T(8,128)(2,1)S(1)}, bf16[64,512]{1,0:T(8,128)(2,1)S(1)}, u32[]{:S(2)}, u32[]{:S(2)}) collective-permute-start(bf16[64,512]{1,0:T(8,128)(2,1)S(1)} %get-tuple-element.47), channel_id=1, source_target_pairs={{0,8},{4,12},{8,0},{12,4},{1,9},{5,13},{9,1},{13,5},{2,10},{6,14},... | collective-permute-start | bytes 196616 | tf_op jit(solution)/shard_map/ppermute | solution.py:33
  39.8 6.4 %collective-permute-start.9 = (bf16[64,512]{1,0:T(8,128)(2,1)S(1)}, bf16[64,512]{1,0:T(8,128)(2,1)S(1)}, u32[]{:S(2)}, u32[]{:S(2)}) collective-permute-start(bf16[64,512]{1,0:T(8,128)(2,1)S(1)} %get-tuple-element.45), channel_id=1, source_target_pairs={{0,4},{4,0},{8,12},{12,8},{1,5},{5,1},{9,13},{13,9},{2,6},{6,2},{1... | collective-permute-start | bytes 196616 | tf_op jit(solution)/shard_map/ppermute | solution.py:33

commit v7 on v6

--- a/solution.py
+++ b/solution.py
@@ -46,18 +46,15 @@
 def route_kernel(order, cap, entries, requests_hbm, store_hbm, hidden_hbm, *refs):
     groups = len(order)
     blocks, back_ref = refs[:groups], refs[groups]
-    requests_ref, store_ref, hidden_ref, index_sems, hidden_sems = refs[groups + 1 :]
+    requests_ref, store_ref, hidden_ref, index_sems, hidden_sem = refs[groups + 1 :]
     steps, seqs, features = hidden_ref.shape
     tiles = features // LANES
     index_copies = [
         pltpu.make_async_copy(requests_hbm, requests_ref, index_sems.at[0]),
         pltpu.make_async_copy(store_hbm, store_ref, index_sems.at[1]),
     ]
-    hidden_copies = [
-        pltpu.make_async_copy(hidden_hbm.at[s], hidden_ref.at[s], hidden_sems.at[s])
-        for s in range(steps)
-    ]
-    for copy in index_copies + hidden_copies:
+    hidden_copy = pltpu.make_async_copy(hidden_hbm, hidden_ref, hidden_sem.at[0])
+    for copy in index_copies + [hidden_copy]:
         copy.start()
     me = lax.axis_index("dp")
     for copy in index_copies:
@@ -87,8 +84,8 @@
         spot = lax.rem(iota((seqs, LANES), 1), jnp.int32(cap)) + k * cap
         slots = jnp.sum(jnp.where(bucket_col == spot, slot_col, 0.0), axis=0, keepdims=True)
         blocks[k][steps * tiles * cap :, :] = jnp.broadcast_to(slots, (cap, LANES)).astype(BF16)
+    hidden_copy.wait()
     for s in range(steps):
-        hidden_copies[s].wait()
         picked = jnp.dot(placed, hidden_ref[s], preferred_element_type=F32).astype(BF16)
         for k in range(groups):
             for c in range(tiles):
@@ -112,7 +109,7 @@
             pltpu.VMEM((1, store.shape[0]), jnp.int32),
             pltpu.VMEM(hidden.shape, BF16),
             pltpu.SemaphoreType.DMA((2,)),
-            pltpu.SemaphoreType.DMA((steps,)),
+            pltpu.SemaphoreType.DMA((1,)),
         ],
         compiler_params=params(62),
         cost_estimate=cost(
@@ -328,7 +325,7 @@
     groups = len(turns)
     summands = refs[:size]
     deltas = [refs[size + turns.index(k)] for k in range(groups)]
-    out_hbm, new_hbm, out_ref, new_ref, out_sems, new_sems = refs[size + groups :]
+    out_hbm, new_hbm, out_ref, new_ref, out_sems, new_sem = refs[size + groups :]
     steps, seqs, width = query_ref.shape
     columns = new_ref.shape[2]
     size = columns // (2 * heads)
@@ -346,8 +343,8 @@
             base = base + summand[rows, :].astype(F32)
         new.append((base + update).astype(BF16))
         new_ref[s] = new[s]
-        copies.append(pltpu.make_async_copy(new_ref.at[s], new_hbm.at[s], new_sems.at[s]))
-        copies[-1].start()
+    copies.append(pltpu.make_async_copy(new_ref, new_hbm, new_sem.at[0]))
+    copies[-1].start()
     same = lax.rem(iota((seqs, LANES), 1), jnp.int32(seqs)) == iota((seqs, LANES), 0)
 
     def over_steps(parts, combine):
@@ -447,7 +444,7 @@
             pltpu.VMEM((steps, seqs, width), BF16),
             pltpu.VMEM((steps, seqs, columns), BF16),
             pltpu.SemaphoreType.DMA((heads * steps,)),
-            pltpu.SemaphoreType.DMA((steps,)),
+            pltpu.SemaphoreType.DMA((1,)),
         ],
         compiler_params=params(16),
         cost_estimate=cost(

time: 48.5 us -> 48.1 us (level)
  Pallas kernels: 18 us -> 17.5 us
where the time goes in v7:
time: 48.1 us; the launch traced here: 48 us
  Pallas kernels  17.5 us (36%)
  waiting for transfers between devices  15.1 us (31%)
  starting transfers between devices  14.5 us (30%)
  between operations  0.76 us (2%)
    ppermute x12, waiting for transfers between devices, swap(): return lambda value: lax.ppermute(value, axis, pairs)  15.1 us
    ppermute x12, starting transfers between devices, swap(): return lambda value: lax.ppermute(value, axis, pairs)  14.5 us
    pallas_call x1, Pallas kernels, past(): pl.pallas_call(past_kernel, grid_spec=pltpu.PrefetchScalarGridSpec(num_sc...  5.88 us
    pallas_call x1, Pallas kernels, base(): pl.pallas_call(functools.partial(base_kernel, size), out_shape=[jax.Shape...  5.73 us
    pallas_call x1, Pallas kernels, route(): pl.pallas_call(functools.partial(route_kernel, order, cap, entries), out_...  2.69 us
    pallas_call x1, Pallas kernels, finish(): pl.pallas_call(functools.partial(finish_kernel, turns, len(summands), cap...  2.16 us
  transfers between devices with their start and end apart: 12, of which 5 were waited for; matrix products, arithmetic and copies ran while one was open for 0% of the time, Pallas kernels for 26%

profile of v7, /device:TPU:0, one launch (start us, length us, event | category | flops | bytes accessed | tf_op | source)
XLA Modules:
  0.0 48.0 jit_solution(2440458009464516585)
XLA Ops:
  0.6 2.7 %route.1 = (bf16[1040,128]{1,0:T(8,128)(2,1)}, bf16[1040,128]{1,0:T(8,128)(2,1)}, bf16[1040,128]{1,0:T(8,128)(2,1)}, bf16[1040,128]{1,0:T(8,128)(2,1)}, bf16[64,64]{1,0:T(8,128)(2,1)}) custom-call(s32[1,64]{1,0:T(1,128)} %bitcast.8, s32[1,128]{1,0:T(1,128)} %bitcast.9, bf16[4,64,2048]{2,1,0:T(8,128)(2,1)} %hidden_hbm.1), custom_call_target="tpu_custom_call" | custom-call | flops 67108864 | bytes 2097152 | tf_op jit(solution)/shard_map/route/pallas_call | solution.py:102
  3.3 5.1 %collective-permute-start.2 = (bf16[1040,128]{1,0:T(8,128)(2,1)}, bf16[1040,128]{1,0:T(8,128)(2,1)S(1)}, u32[]{:S(2)}, u32[]{:S(2)}) collective-permute-start(bf16[1040,128]{1,0:T(8,128)(2,1)} %get-tuple-element.35), channel_id=1, source_target_pairs={{0,12},{4,8},{8,4},{12,0},{1,13},{5,9},{9,5},{13,1},{2,14},{6,10},... | collective-permute-start | bytes 798728 | tf_op jit(solution)/shard_map/ppermute | solution.py:33
  8.4 0.0 collective-permute-start.3
  8.4 0.6 %collective-permute-start.4 = (bf16[1040,128]{1,0:T(8,128)(2,1)}, bf16[1040,128]{1,0:T(8,128)(2,1)S(1)}, u32[]{:S(2)}, u32[]{:S(2)}) collective-permute-start(bf16[1040,128]{1,0:T(8,128)(2,1)} %get-tuple-element.37), channel_id=1, source_target_pairs={{0,4},{4,0},{8,12},{12,8},{1,5},{5,1},{9,13},{13,9},{2,6},{6,2},{1... | collective-permute-start | bytes 798728 | tf_op jit(solution)/shard_map/ppermute | solution.py:33
  9.1 0.0 copy-start
  9.1 0.0 copy-start.1
  9.1 0.0 copy-start.2
  9.1 0.0 copy-start.8
  9.1 5.7 %base.1 = (f32[256,512]{1,0:T(8,128)}, f32[256,512]{1,0:T(8,128)}, bf16[256,512]{1,0:T(8,128)(2,1)S(1)}, bf16[256,512]{1,0:T(8,128)(2,1)S(1)}) custom-call(bf16[256,2048]{1,0:T(8,128)(2,1)} %bitcast.7, bf16[2048,2048]{1,0:T(8,128)(2,1)} %projection_hbm.1), custom_call_target="tpu_custom_call" | custom-call | bytes 4096 | tf_op jit(solution)/shard_map/base/pallas_call | solution.py:148
  14.8 1.7 %collective-permute-start = (bf16[256,512]{1,0:T(8,128)(2,1)S(1)}, bf16[256,512]{1,0:T(8,128)(2,1)S(1)}, u32[]{:S(2)}, u32[]{:S(2)}) collective-permute-start(bf16[256,512]{1,0:T(8,128)(2,1)S(1)} %get-tuple-element.30), channel_id=1, source_target_pairs={{0,2},{1,3},{2,0},{3,1},{4,6},{5,7},{6,4},{7,5},{8,10},{9,11},{10,... | collective-permute-start | bytes 786440 | tf_op jit(solution)/shard_map/ppermute | solution.py:33
  16.5 0.0 copy-start.3
  16.5 0.0 copy-start.6
  16.5 0.0 copy-start.5
  16.5 0.0 copy-start.9
  16.5 0.4 collective-permute-start.1
  17.0 0.0 copy-done
  17.0 0.0 copy-done.1
  17.0 0.0 copy-done.2
  17.0 0.0 copy-done.8
  17.0 5.9 %past.1 = (f32[4,64,2048]{2,1,0:T(8,128)S(1)}, f32[64,128]{1,0:T(8,128)S(1)}) custom-call(s32[64]{0:T(128)S(1)} %copy-done.8, bf16[4,64,2048]{2,1,0:T(8,128)(2,1)S(1)} %copy-done, bf16[64,2,128,128]{3,2,1,0:T(8,128)(2,1)S(1)} %copy-done.1, bf16[64,2,128,128]{3,2,1,0:T(8,128)(2,1)S(1)} %copy-done.2), custom_call_target="tpu_custom_call" | custom-call | bytes 4096 | tf_op jit(solution)/shard_map/past/pallas_call | solution.py:225
  22.9 0.0 copy-start.4
  22.9 0.0 copy-start.7
  22.9 0.0 collective-permute-done.2.refs_1_
  22.9 8.4 %collective-permute-done.3.refs_2_ = bf16[1040,128]{1,0:T(8,128)(2,1)S(1)} collective-permute-done((bf16[1040,128]{1,0:T(8,128)(2,1)}, bf16[1040,128]{1,0:T(8,128)(2,1)S(1)}, u32[]{:S(2)}, u32[]{:S(2)}) %collective-permute-start.3) | collective-permute-done | bytes 266272 | tf_op jit(solution)/shard_map/ppermute | solution.py:33
  31.3 0.0 collective-permute-done.4.refs_3_
  31.3 0.0 copy-done.3
  31.3 0.0 copy-done.6
  31.3 0.8 %shrink.1 = (f32[16,256]{1,0:T(8,128)S(1)}, s32[1,256]{1,0:T(1,128)S(1)}) custom-call(bf16[512,2048]{1,0:T(8,128)(2,1)S(1)} %bitcast.5, bf16[1040,128]{1,0:T(8,128)(2,1)S(1)} %copy-done.6, bf16[1040,128]{1,0:T(8,128)(2,1)S(1)} %collective-permute-done.2.refs_1_, bf16[1040,128]{1,0:T(8,128)(2,1)S(1)} %collective-permute-done.3.refs_2_, ...), custom_call_target="tpu_custom_call" | custom-call | flops 536870912 | bytes 3145728 | tf_op jit(solution)/shard_map/shrink/pallas_call | solution.py:275
  32.1 0.3 collective-permute-start.5
  32.4 1.3 %collective-permute-start.6 = (f32[16,256]{1,0:T(8,128)S(1)}, f32[16,256]{1,0:T(8,128)S(1)}, u32[]{:S(2)}, u32[]{:S(2)}) collective-permute-start(f32[16,256]{1,0:T(8,128)S(1)} %get-tuple-element.39.refs_0_), channel_id=1, source_target_pairs={{0,2},{1,3},{2,0},{3,1},{4,6},{5,7},{6,4},{7,5},{8,10},{9,11},{10,... | collective-permute-start | bytes 49160 | tf_op jit(solution)/shard_map/ppermute | solution.py:33
  33.7 0.3 collective-permute-start.7
  34.0 1.4 %collective-permute-done.5.refs_1_ = f32[16,256]{1,0:T(8,128)S(1)} collective-permute-done((f32[16,256]{1,0:T(8,128)S(1)}, f32[16,256]{1,0:T(8,128)S(1)}, u32[]{:S(2)}, u32[]{:S(2)}) %collective-permute-start.5) | collective-permute-done | bytes 16416 | tf_op jit(solution)/shard_map/ppermute | solution.py:33
  35.4 0.7 %collective-permute-done.6.refs_2_ = f32[16,256]{1,0:T(8,128)S(1)} collective-permute-done((f32[16,256]{1,0:T(8,128)S(1)}, f32[16,256]{1,0:T(8,128)S(1)}, u32[]{:S(2)}, u32[]{:S(2)}) %collective-permute-start.6) | collective-permute-done | bytes 16416 | tf_op jit(solution)/shard_map/ppermute | solution.py:33
  36.1 0.0 collective-permute-done.7.refs_3_
  36.2 0.0 copy-done.5
  36.2 0.3 expand.1
  36.5 0.0 collective-permute-done.refs_1_
  36.5 0.0 collective-permute-done.1
  36.5 0.0 copy-done.9
  36.5 0.1 add_convert_fusion
  36.6 0.3 collective-permute-start.8
  36.9 2.5 %collective-permute-start.10 = (bf16[64,512]{1,0:T(8,128)(2,1)S(1)}, bf16[64,512]{1,0:T(8,128)(2,1)S(1)}, u32[]{:S(2)}, u32[]{:S(2)}) collective-permute-start(bf16[64,512]{1,0:T(8,128)(2,1)S(1)} %get-tuple-element.46), channel_id=1, source_target_pairs={{0,12},{4,8},{8,4},{12,0},{1,13},{5,9},{9,5},{13,1},{2,14},{6,10},... | collective-permute-start | bytes 196616 | tf_op jit(solution)/shard_map/ppermute | solution.py:33
  39.3 0.0 collective-permute-start.11
  39.3 1.9 %collective-permute-start.9 = (bf16[64,512]{1,0:T(8,128)(2,1)S(1)}, bf16[64,512]{1,0:T(8,128)(2,1)S(1)}, u32[]{:S(2)}, u32[]{:S(2)}) collective-permute-start(bf16[64,512]{1,0:T(8,128)(2,1)S(1)} %get-tuple-element.45), channel_id=1, source_target_pairs={{0,4},{4,0},{8,12},{12,8},{1,5},{5,1},{9,13},{13,9},{2,6},{6,2},{1... | collective-permute-start | bytes 196616 | tf_op jit(solution)/shard_map/ppermute | solution.py:33
  41.3 2.4 %collective-permute-done.10.refs_5_ = bf16[64,512]{1,0:T(8,128)(2,1)S(1)} collective-permute-done((bf16[64,512]{1,0:T(8,128)(2,1)S(1)}, bf16[64,512]{1,0:T(8,128)(2,1)S(1)}, u32[]{:S(2)}, u32[]{:S(2)}) %collective-permute-start.10) | collective-permute-done | bytes 65568 | tf_op jit(solution)/shard_map/ppermute | solution.py:33
  43.7 2.1 %collective-permute-done.11.refs_6_ = bf16[64,512]{1,0:T(8,128)(2,1)S(1)} collective-permute-done((bf16[64,512]{1,0:T(8,128)(2,1)S(1)}, bf16[64,512]{1,0:T(8,128)(2,1)S(1)}, u32[]{:S(2)}, u32[]{:S(2)}) %collective-permute-start.11) | collective-permute-done | bytes 65568 | tf_op jit(solution)/shard_map/ppermute | solution.py:33
  45.8 0.0 collective-permute-done.9.refs_4_
  45.8 0.0 collective-permute-done.8.refs_2_
  45.8 0.0 copy-done.4
  45.8 0.0 copy-done.7
  45.8 2.2 %finish.1 = (bf16[4,64,2048]{2,1,0:T(8,128)(2,1)}, bf16[4,64,512]{2,1,0:T(8,128)(2,1)}) custom-call(bf16[64,64]{1,0:T(8,128)(2,1)S(1)} %copy-done.7, bf16[4,64,2048]{2,1,0:T(8,128)(2,1)S(1)} %copy-done, f32[4,64,2048]{2,1,0:T(8,128)S(1)} %get-tuple-element.26.mixed_ref, f32[64,128]{1,0:T(8,128)S(1)} %get-tuple-element.27.lse_ref, f32[256,512]{1,0:T(8,128)S(1)} %copy-done.4, ...), custom_call_target="tpu_custom_call" | custom-call | flops 1073741824 | bytes 5242880 | tf_op jit(solution)/shard_map/finish/pallas_call | solution.py:436
Async XLA Ops:
  3.3 19.6 %collective-permute-start.2 = (bf16[1040,128]{1,0:T(8,128)(2,1)}, bf16[1040,128]{1,0:T(8,128)(2,1)S(1)}, u32[]{:S(2)}, u32[]{:S(2)}) collective-permute-start(bf16[1040,128]{1,0:T(8,128)(2,1)} %get-tuple-element.35), channel_id=1, source_target_pairs={{0,12},{4,8},{8,4},{12,0},{1,13},{5,9},{9,5},{13,1},{2,14},{6,10},... | collective-permute-start | bytes 798728 | tf_op jit(solution)/shard_map/ppermute | solution.py:33
  8.4 22.9 %collective-permute-start.3 = (bf16[1040,128]{1,0:T(8,128)(2,1)}, bf16[1040,128]{1,0:T(8,128)(2,1)S(1)}, u32[]{:S(2)}, u32[]{:S(2)}) collective-permute-start(bf16[1040,128]{1,0:T(8,128)(2,1)} %get-tuple-element.36), channel_id=1, source_target_pairs={{0,8},{4,12},{8,0},{12,4},{1,9},{5,13},{9,1},{13,5},{2,10},{6,14},... | collective-permute-start | bytes 798728 | tf_op jit(solution)/shard_map/ppermute | solution.py:33
  8.4 22.9 %collective-permute-start.4 = (bf16[1040,128]{1,0:T(8,128)(2,1)}, bf16[1040,128]{1,0:T(8,128)(2,1)S(1)}, u32[]{:S(2)}, u32[]{:S(2)}) collective-permute-start(bf16[1040,128]{1,0:T(8,128)(2,1)} %get-tuple-element.37), channel_id=1, source_target_pairs={{0,4},{4,0},{8,12},{12,8},{1,5},{5,1},{9,13},{13,9},{2,6},{6,2},{1... | collective-permute-start | bytes 798728 | tf_op jit(solution)/shard_map/ppermute | solution.py:33
  9.1 7.9 %copy-start = (bf16[4,64,2048]{2,1,0:T(8,128)(2,1)S(1)}, bf16[4,64,2048]{2,1,0:T(8,128)(2,1)}, u32[]{:S(2)}) copy-start(bf16[4,64,2048]{2,1,0:T(8,128)(2,1)} %query_ref.3) | copy-start | bytes 3145732
  9.1 7.9 %copy-start.1 = (bf16[64,2,128,128]{3,2,1,0:T(8,128)(2,1)S(1)}, bf16[64,2,128,128]{3,2,1,0:T(8,128)(2,1)}, u32[]{:S(2)}) copy-start(bf16[64,2,128,128]{3,2,1,0:T(8,128)(2,1)} %key_ref.1) | copy-start | bytes 12582916
  9.1 7.9 %copy-start.2 = (bf16[64,2,128,128]{3,2,1,0:T(8,128)(2,1)S(1)}, bf16[64,2,128,128]{3,2,1,0:T(8,128)(2,1)}, u32[]{:S(2)}) copy-start(bf16[64,2,128,128]{3,2,1,0:T(8,128)(2,1)} %value_ref.1) | copy-start | bytes 12582916
  9.1 7.9 %copy-start.8 = (s32[64]{0:T(128)S(1)}, s32[64]{0:T(128)}, u32[]{:S(2)}) copy-start(s32[64]{0:T(128)} %lengths_ref.1) | copy-start | bytes 772
  14.8 21.7 %collective-permute-start = (bf16[256,512]{1,0:T(8,128)(2,1)S(1)}, bf16[256,512]{1,0:T(8,128)(2,1)S(1)}, u32[]{:S(2)}, u32[]{:S(2)}) collective-permute-start(bf16[256,512]{1,0:T(8,128)(2,1)S(1)} %get-tuple-element.30), channel_id=1, source_target_pairs={{0,2},{1,3},{2,0},{3,1},{4,6},{5,7},{6,4},{7,5},{8,10},{9,11},{10,... | collective-permute-start | bytes 786440 | tf_op jit(solution)/shard_map/ppermute | solution.py:33
  16.5 14.8 %copy-start.3 = (bf16[32,16,2048]{2,1,0:T(8,128)(2,1)S(1)}, bf16[32,16,2048]{2,1,0:T(8,128)(2,1)}, u32[]{:S(2)}) copy-start(bf16[32,16,2048]{2,1,0:T(8,128)(2,1)} %param.15) | copy-start | bytes 6291460
  16.5 14.8 %copy-start.6 = (bf16[1040,128]{1,0:T(8,128)(2,1)S(1)}, bf16[1040,128]{1,0:T(8,128)(2,1)}, u32[]{:S(2)}) copy-start(bf16[1040,128]{1,0:T(8,128)(2,1)} %get-tuple-element.34.refs_0_) | copy-start | bytes 798724
  16.5 19.6 %copy-start.5 = (bf16[32,16,512]{2,1,0:T(8,128)(2,1)S(1)}, bf16[32,16,512]{2,1,0:T(8,128)(2,1)}, u32[]{:S(2)}) copy-start(bf16[32,16,512]{2,1,0:T(8,128)(2,1)} %param.16) | copy-start | bytes 1572868
  16.5 20.0 %copy-start.9 = (f32[256,512]{1,0:T(8,128)S(1)}, f32[256,512]{1,0:T(8,128)}, u32[]{:S(2)}) copy-start(f32[256,512]{1,0:T(8,128)} %get-tuple-element.43) | copy-start | bytes 1572868
  16.5 20.0 %collective-permute-start.1 = (bf16[256,512]{1,0:T(8,128)(2,1)S(1)}, bf16[256,512]{1,0:T(8,128)(2,1)S(1)}, u32[]{:S(2)}, u32[]{:S(2)}) collective-permute-start(bf16[256,512]{1,0:T(8,128)(2,1)S(1)} %get-tuple-element.32), channel_id=1, source_target_pairs={{0,2},{1,3},{2,0},{3,1},{4,6},{5,7},{6,4},{7,5},{8,10},{9,11},{10,... | collective-permute-start | bytes 786440 | tf_op jit(solution)/shard_map/ppermute | solution.py:33
  22.9 22.9 %copy-start.4 = (f32[256,512]{1,0:T(8,128)S(1)}, f32[256,512]{1,0:T(8,128)}, u32[]{:S(2)}) copy-start(f32[256,512]{1,0:T(8,128)} %get-tuple-element.41.refs_0_) | copy-start | bytes 1572868
  22.9 22.9 %copy-start.7 = (bf16[64,64]{1,0:T(8,128)(2,1)S(1)}, bf16[64,64]{1,0:T(8,128)(2,1)}, u32[]{:S(2)}) copy-start(bf16[64,64]{1,0:T(8,128)(2,1)} %get-tuple-element.25.back_ref) | copy-start | bytes 24580
  32.1 3.3 %collective-permute-start.5 = (f32[16,256]{1,0:T(8,128)S(1)}, f32[16,256]{1,0:T(8,128)S(1)}, u32[]{:S(2)}, u32[]{:S(2)}) collective-permute-start(f32[16,256]{1,0:T(8,128)S(1)} %get-tuple-element.39.refs_0_), channel_id=1, source_target_pairs={{0,3},{1,2},{2,1},{3,0},{4,7},{5,6},{6,5},{7,4},{8,11},{9,10},{10,... | collective-permute-start | bytes 49160 | tf_op jit(solution)/shard_map/ppermute | solution.py:33
  32.4 3.7 %collective-permute-start.6 = (f32[16,256]{1,0:T(8,128)S(1)}, f32[16,256]{1,0:T(8,128)S(1)}, u32[]{:S(2)}, u32[]{:S(2)}) collective-permute-start(f32[16,256]{1,0:T(8,128)S(1)} %get-tuple-element.39.refs_0_), channel_id=1, source_target_pairs={{0,2},{1,3},{2,0},{3,1},{4,6},{5,7},{6,4},{7,5},{8,10},{9,11},{10,... | collective-permute-start | bytes 49160 | tf_op jit(solution)/shard_map/ppermute | solution.py:33
  33.7 2.4 %collective-permute-start.7 = (f32[16,256]{1,0:T(8,128)S(1)}, f32[16,256]{1,0:T(8,128)S(1)}, u32[]{:S(2)}, u32[]{:S(2)}) collective-permute-start(f32[16,256]{1,0:T(8,128)S(1)} %get-tuple-element.39.refs_0_), channel_id=1, source_target_pairs={{0,1},{1,0},{2,3},{3,2},{4,5},{5,4},{6,7},{7,6},{8,9},{9,8},{10,11... | collective-permute-start | bytes 49160 | tf_op jit(solution)/shard_map/ppermute | solution.py:33
  36.6 9.2 %collective-permute-start.8 = (bf16[256,512]{1,0:T(8,128)(2,1)S(1)}, bf16[256,512]{1,0:T(8,128)(2,1)S(1)}, u32[]{:S(2)}, u32[]{:S(2)}) collective-permute-start(bf16[256,512]{1,0:T(8,128)(2,1)S(1)} %add_convert_fusion), channel_id=1, source_target_pairs={{0,1},{1,0},{2,3},{3,2},{4,5},{5,4},{6,7},{7,6},{8,9},{9,8},{10,11... | collective-permute-start | bytes 786440 | tf_op jit(solution)/shard_map/ppermute | solution.py:33
  36.9 6.8 %collective-permute-start.10 = (bf16[64,512]{1,0:T(8,128)(2,1)S(1)}, bf16[64,512]{1,0:T(8,128)(2,1)S(1)}, u32[]{:S(2)}, u32[]{:S(2)}) collective-permute-start(bf16[64,512]{1,0:T(8,128)(2,1)S(1)} %get-tuple-element.46), channel_id=1, source_target_pairs={{0,12},{4,8},{8,4},{12,0},{1,13},{5,9},{9,5},{13,1},{2,14},{6,10},... | collective-permute-start | bytes 196616 | tf_op jit(solution)/shard_map/ppermute | solution.py:33
  39.3 6.5 %collective-permute-start.11 = (bf16[64,512]{1,0:T(8,128)(2,1)S(1)}, bf16[64,512]{1,0:T(8,128)(2,1)S(1)}, u32[]{:S(2)}, u32[]{:S(2)}) collective-permute-start(bf16[64,512]{1,0:T(8,128)(2,1)S(1)} %get-tuple-element.47), channel_id=1, source_target_pairs={{0,8},{4,12},{8,0},{12,4},{1,9},{5,13},{9,1},{13,5},{2,10},{6,14},... | collective-permute-start | bytes 196616 | tf_op jit(solution)/shard_map/ppermute | solution.py:33
  39.3 6.5 %collective-permute-start.9 = (bf16[64,512]{1,0:T(8,128)(2,1)S(1)}, bf16[64,512]{1,0:T(8,128)(2,1)S(1)}, u32[]{:S(2)}, u32[]{:S(2)}) collective-permute-start(bf16[64,512]{1,0:T(8,128)(2,1)S(1)} %get-tuple-element.45), channel_id=1, source_target_pairs={{0,4},{4,0},{8,12},{12,8},{1,5},{5,1},{9,13},{13,9},{2,6},{6,2},{1... | collective-permute-start | bytes 196616 | tf_op jit(solution)/shard_map/ppermute | solution.py:33

commit v8 on v7

--- a/solution.py
+++ b/solution.py
@@ -220,7 +220,7 @@
 def past(lengths, queries, keys, values):
     steps, seqs, width = queries.shape
     _, heads, positions, size = keys.shape
-    chunk = 8
+    chunk = 16
     cache_spec = pl.BlockSpec((chunk, heads, positions, size), lambda i, n: (i, 0, 0, 0))
     return pl.pallas_call(
         past_kernel,

time: 48.1 us -> 48.1 us (level)
  Pallas kernels: 17.5 us -> 16.4 us
  waiting for transfers between devices: 15.1 us -> 16.2 us
    pallas_call x1, Pallas kernels: 5.88 us -> 4.76 us  [past(): pl.pallas_call(past_kernel, grid_spec=pltpu.PrefetchScalarGridSpec(num_sc...]
    ppermute x12, waiting for transfers between devices: 15.1 us -> 16.2 us  [swap(): return lambda value: lax.ppermute(value, axis, pairs)]
  transfers between devices with their start and end apart: 12 -> 12, of which waited for: 5 -> 5; matrix products, arithmetic and copies ran while one was open for 0% -> 0% of each run, Pallas kernels for 26% -> 24%
where the time goes in v8:
time: 48.1 us; the launch traced here: 48 us
  Pallas kernels  16.4 us (34%)
  waiting for transfers between devices  16.2 us (34%)
  starting transfers between devices  14.5 us (30%)
  between operations  0.76 us (2%)
    ppermute x12, waiting for transfers between devices, swap(): return lambda value: lax.ppermute(value, axis, pairs)  16.2 us
    ppermute x12, starting transfers between devices, swap(): return lambda value: lax.ppermute(value, axis, pairs)  14.5 us
    pallas_call x1, Pallas kernels, base(): pl.pallas_call(functools.partial(base_kernel, size), out_shape=[jax.Shape...  5.73 us
    pallas_call x1, Pallas kernels, past(): pl.pallas_call(past_kernel, grid_spec=pltpu.PrefetchScalarGridSpec(num_sc...  4.76 us
    pallas_call x1, Pallas kernels, route(): pl.pallas_call(functools.partial(route_kernel, order, cap, entries), out_...  2.69 us
    pallas_call x1, Pallas kernels, finish(): pl.pallas_call(functools.partial(finish_kernel, turns, len(summands), cap...  2.16 us
  transfers between devices with their start and end apart: 12, of which 5 were waited for; matrix products, arithmetic and copies ran while one was open for 0% of the time, Pallas kernels for 24%

profile of v8, /device:TPU:0, one launch (start us, length us, event | category | flops | bytes accessed | tf_op | source)
XLA Modules:
  0.0 48.0 jit_solution(8875021250165099069)
XLA Ops:
  0.6 2.7 %route.1 = (bf16[1040,128]{1,0:T(8,128)(2,1)}, bf16[1040,128]{1,0:T(8,128)(2,1)}, bf16[1040,128]{1,0:T(8,128)(2,1)}, bf16[1040,128]{1,0:T(8,128)(2,1)}, bf16[64,64]{1,0:T(8,128)(2,1)}) custom-call(s32[1,64]{1,0:T(1,128)} %bitcast.8, s32[1,128]{1,0:T(1,128)} %bitcast.9, bf16[4,64,2048]{2,1,0:T(8,128)(2,1)} %hidden_hbm.1), custom_call_target="tpu_custom_call" | custom-call | flops 67108864 | bytes 2097152 | tf_op jit(solution)/shard_map/route/pallas_call | solution.py:102
  3.3 5.1 %collective-permute-start.2 = (bf16[1040,128]{1,0:T(8,128)(2,1)}, bf16[1040,128]{1,0:T(8,128)(2,1)S(1)}, u32[]{:S(2)}, u32[]{:S(2)}) collective-permute-start(bf16[1040,128]{1,0:T(8,128)(2,1)} %get-tuple-element.35), channel_id=1, source_target_pairs={{0,12},{4,8},{8,4},{12,0},{1,13},{5,9},{9,5},{13,1},{2,14},{6,10},... | collective-permute-start | bytes 798728 | tf_op jit(solution)/shard_map/ppermute | solution.py:33
  8.4 0.0 collective-permute-start.3
  8.4 0.6 %collective-permute-start.4 = (bf16[1040,128]{1,0:T(8,128)(2,1)}, bf16[1040,128]{1,0:T(8,128)(2,1)S(1)}, u32[]{:S(2)}, u32[]{:S(2)}) collective-permute-start(bf16[1040,128]{1,0:T(8,128)(2,1)} %get-tuple-element.37), channel_id=1, source_target_pairs={{0,4},{4,0},{8,12},{12,8},{1,5},{5,1},{9,13},{13,9},{2,6},{6,2},{1... | collective-permute-start | bytes 798728 | tf_op jit(solution)/shard_map/ppermute | solution.py:33
  9.1 0.0 copy-start
  9.1 0.0 copy-start.1
  9.1 0.0 copy-start.2
  9.1 0.0 copy-start.8
  9.1 5.7 %base.1 = (f32[256,512]{1,0:T(8,128)}, f32[256,512]{1,0:T(8,128)}, bf16[256,512]{1,0:T(8,128)(2,1)S(1)}, bf16[256,512]{1,0:T(8,128)(2,1)S(1)}) custom-call(bf16[256,2048]{1,0:T(8,128)(2,1)} %bitcast.7, bf16[2048,2048]{1,0:T(8,128)(2,1)} %projection_hbm.1), custom_call_target="tpu_custom_call" | custom-call | bytes 4096 | tf_op jit(solution)/shard_map/base/pallas_call | solution.py:148
  14.8 1.7 %collective-permute-start = (bf16[256,512]{1,0:T(8,128)(2,1)S(1)}, bf16[256,512]{1,0:T(8,128)(2,1)S(1)}, u32[]{:S(2)}, u32[]{:S(2)}) collective-permute-start(bf16[256,512]{1,0:T(8,128)(2,1)S(1)} %get-tuple-element.30), channel_id=1, source_target_pairs={{0,2},{1,3},{2,0},{3,1},{4,6},{5,7},{6,4},{7,5},{8,10},{9,11},{10,... | collective-permute-start | bytes 786440 | tf_op jit(solution)/shard_map/ppermute | solution.py:33
  16.5 0.0 copy-start.3
  16.5 0.0 copy-start.6
  16.5 0.0 copy-start.5
  16.5 0.0 copy-start.9
  16.5 0.4 collective-permute-start.1
  17.0 0.0 copy-done
  17.0 0.0 copy-done.1
  17.0 0.0 copy-done.2
  17.0 0.0 copy-done.8
  17.0 4.8 %past.1 = (f32[4,64,2048]{2,1,0:T(8,128)S(1)}, f32[64,128]{1,0:T(8,128)S(1)}) custom-call(s32[64]{0:T(128)S(1)} %copy-done.8, bf16[4,64,2048]{2,1,0:T(8,128)(2,1)S(1)} %copy-done, bf16[64,2,128,128]{3,2,1,0:T(8,128)(2,1)S(1)} %copy-done.1, bf16[64,2,128,128]{3,2,1,0:T(8,128)(2,1)S(1)} %copy-done.2), custom_call_target="tpu_custom_call" | custom-call | bytes 4096 | tf_op jit(solution)/shard_map/past/pallas_call | solution.py:225
  21.8 0.0 copy-start.4
  21.8 0.0 copy-start.7
  21.8 0.0 collective-permute-done.2.refs_1_
  21.8 9.5 %collective-permute-done.3.refs_2_ = bf16[1040,128]{1,0:T(8,128)(2,1)S(1)} collective-permute-done((bf16[1040,128]{1,0:T(8,128)(2,1)}, bf16[1040,128]{1,0:T(8,128)(2,1)S(1)}, u32[]{:S(2)}, u32[]{:S(2)}) %collective-permute-start.3) | collective-permute-done | bytes 266272 | tf_op jit(solution)/shard_map/ppermute | solution.py:33
  31.3 0.0 collective-permute-done.4.refs_3_
  31.3 0.0 copy-done.3
  31.3 0.0 copy-done.6
  31.3 0.8 %shrink.1 = (f32[16,256]{1,0:T(8,128)S(1)}, s32[1,256]{1,0:T(1,128)S(1)}) custom-call(bf16[512,2048]{1,0:T(8,128)(2,1)S(1)} %bitcast.5, bf16[1040,128]{1,0:T(8,128)(2,1)S(1)} %copy-done.6, bf16[1040,128]{1,0:T(8,128)(2,1)S(1)} %collective-permute-done.2.refs_1_, bf16[1040,128]{1,0:T(8,128)(2,1)S(1)} %collective-permute-done.3.refs_2_, ...), custom_call_target="tpu_custom_call" | custom-call | flops 536870912 | bytes 3145728 | tf_op jit(solution)/shard_map/shrink/pallas_call | solution.py:275
  32.1 0.3 collective-permute-start.5
  32.4 1.3 %collective-permute-start.6 = (f32[16,256]{1,0:T(8,128)S(1)}, f32[16,256]{1,0:T(8,128)S(1)}, u32[]{:S(2)}, u32[]{:S(2)}) collective-permute-start(f32[16,256]{1,0:T(8,128)S(1)} %get-tuple-element.39.refs_0_), channel_id=1, source_target_pairs={{0,2},{1,3},{2,0},{3,1},{4,6},{5,7},{6,4},{7,5},{8,10},{9,11},{10,... | collective-permute-start | bytes 49160 | tf_op jit(solution)/shard_map/ppermute | solution.py:33
  33.7 0.3 collective-permute-start.7
  34.0 1.4 %collective-permute-done.5.refs_1_ = f32[16,256]{1,0:T(8,128)S(1)} collective-permute-done((f32[16,256]{1,0:T(8,128)S(1)}, f32[16,256]{1,0:T(8,128)S(1)}, u32[]{:S(2)}, u32[]{:S(2)}) %collective-permute-start.5) | collective-permute-done | bytes 16416 | tf_op jit(solution)/shard_map/ppermute | solution.py:33
  35.4 0.7 %collective-permute-done.6.refs_2_ = f32[16,256]{1,0:T(8,128)S(1)} collective-permute-done((f32[16,256]{1,0:T(8,128)S(1)}, f32[16,256]{1,0:T(8,128)S(1)}, u32[]{:S(2)}, u32[]{:S(2)}) %collective-permute-start.6) | collective-permute-done | bytes 16416 | tf_op jit(solution)/shard_map/ppermute | solution.py:33
  36.1 0.0 collective-permute-done.7.refs_3_
  36.2 0.0 copy-done.5
  36.2 0.3 expand.1
  36.5 0.0 collective-permute-done.refs_1_
  36.5 0.0 collective-permute-done.1
  36.5 0.0 copy-done.9
  36.5 0.1 add_convert_fusion
  36.6 0.3 collective-permute-start.8
  36.9 2.5 %collective-permute-start.10 = (bf16[64,512]{1,0:T(8,128)(2,1)S(1)}, bf16[64,512]{1,0:T(8,128)(2,1)S(1)}, u32[]{:S(2)}, u32[]{:S(2)}) collective-permute-start(bf16[64,512]{1,0:T(8,128)(2,1)S(1)} %get-tuple-element.46), channel_id=1, source_target_pairs={{0,12},{4,8},{8,4},{12,0},{1,13},{5,9},{9,5},{13,1},{2,14},{6,10},... | collective-permute-start | bytes 196616 | tf_op jit(solution)/shard_map/ppermute | solution.py:33
  39.3 0.0 collective-permute-start.11
  39.3 1.9 %collective-permute-start.9 = (bf16[64,512]{1,0:T(8,128)(2,1)S(1)}, bf16[64,512]{1,0:T(8,128)(2,1)S(1)}, u32[]{:S(2)}, u32[]{:S(2)}) collective-permute-start(bf16[64,512]{1,0:T(8,128)(2,1)S(1)} %get-tuple-element.45), channel_id=1, source_target_pairs={{0,4},{4,0},{8,12},{12,8},{1,5},{5,1},{9,13},{13,9},{2,6},{6,2},{1... | collective-permute-start | bytes 196616 | tf_op jit(solution)/shard_map/ppermute | solution.py:33
  41.3 2.4 %collective-permute-done.10.refs_5_ = bf16[64,512]{1,0:T(8,128)(2,1)S(1)} collective-permute-done((bf16[64,512]{1,0:T(8,128)(2,1)S(1)}, bf16[64,512]{1,0:T(8,128)(2,1)S(1)}, u32[]{:S(2)}, u32[]{:S(2)}) %collective-permute-start.10) | collective-permute-done | bytes 65568 | tf_op jit(solution)/shard_map/ppermute | solution.py:33
  43.7 2.1 %collective-permute-done.11.refs_6_ = bf16[64,512]{1,0:T(8,128)(2,1)S(1)} collective-permute-done((bf16[64,512]{1,0:T(8,128)(2,1)S(1)}, bf16[64,512]{1,0:T(8,128)(2,1)S(1)}, u32[]{:S(2)}, u32[]{:S(2)}) %collective-permute-start.11) | collective-permute-done | bytes 65568 | tf_op jit(solution)/shard_map/ppermute | solution.py:33
  45.8 0.0 collective-permute-done.9.refs_4_
  45.8 0.0 collective-permute-done.8.refs_2_
  45.8 0.0 copy-done.4
  45.8 0.0 copy-done.7
  45.8 2.2 %finish.1 = (bf16[4,64,2048]{2,1,0:T(8,128)(2,1)}, bf16[4,64,512]{2,1,0:T(8,128)(2,1)}) custom-call(bf16[64,64]{1,0:T(8,128)(2,1)S(1)} %copy-done.7, bf16[4,64,2048]{2,1,0:T(8,128)(2,1)S(1)} %copy-done, f32[4,64,2048]{2,1,0:T(8,128)S(1)} %get-tuple-element.26.mixed_ref, f32[64,128]{1,0:T(8,128)S(1)} %get-tuple-element.27.lse_ref, f32[256,512]{1,0:T(8,128)S(1)} %copy-done.4, ...), custom_call_target="tpu_custom_call" | custom-call | flops 1073741824 | bytes 5242880 | tf_op jit(solution)/shard_map/finish/pallas_call | solution.py:436
Async XLA Ops:
  3.3 18.5 %collective-permute-start.2 = (bf16[1040,128]{1,0:T(8,128)(2,1)}, bf16[1040,128]{1,0:T(8,128)(2,1)S(1)}, u32[]{:S(2)}, u32[]{:S(2)}) collective-permute-start(bf16[1040,128]{1,0:T(8,128)(2,1)} %get-tuple-element.35), channel_id=1, source_target_pairs={{0,12},{4,8},{8,4},{12,0},{1,13},{5,9},{9,5},{13,1},{2,14},{6,10},... | collective-permute-start | bytes 798728 | tf_op jit(solution)/shard_map/ppermute | solution.py:33
  8.4 22.9 %collective-permute-start.3 = (bf16[1040,128]{1,0:T(8,128)(2,1)}, bf16[1040,128]{1,0:T(8,128)(2,1)S(1)}, u32[]{:S(2)}, u32[]{:S(2)}) collective-permute-start(bf16[1040,128]{1,0:T(8,128)(2,1)} %get-tuple-element.36), channel_id=1, source_target_pairs={{0,8},{4,12},{8,0},{12,4},{1,9},{5,13},{9,1},{13,5},{2,10},{6,14},... | collective-permute-start | bytes 798728 | tf_op jit(solution)/shard_map/ppermute | solution.py:33
  8.4 22.9 %collective-permute-start.4 = (bf16[1040,128]{1,0:T(8,128)(2,1)}, bf16[1040,128]{1,0:T(8,128)(2,1)S(1)}, u32[]{:S(2)}, u32[]{:S(2)}) collective-permute-start(bf16[1040,128]{1,0:T(8,128)(2,1)} %get-tuple-element.37), channel_id=1, source_target_pairs={{0,4},{4,0},{8,12},{12,8},{1,5},{5,1},{9,13},{13,9},{2,6},{6,2},{1... | collective-permute-start | bytes 798728 | tf_op jit(solution)/shard_map/ppermute | solution.py:33
  9.1 7.9 %copy-start = (bf16[4,64,2048]{2,1,0:T(8,128)(2,1)S(1)}, bf16[4,64,2048]{2,1,0:T(8,128)(2,1)}, u32[]{:S(2)}) copy-start(bf16[4,64,2048]{2,1,0:T(8,128)(2,1)} %query_ref.3) | copy-start | bytes 3145732
  9.1 7.9 %copy-start.1 = (bf16[64,2,128,128]{3,2,1,0:T(8,128)(2,1)S(1)}, bf16[64,2,128,128]{3,2,1,0:T(8,128)(2,1)}, u32[]{:S(2)}) copy-start(bf16[64,2,128,128]{3,2,1,0:T(8,128)(2,1)} %key_ref.1) | copy-start | bytes 12582916
  9.1 7.9 %copy-start.2 = (bf16[64,2,128,128]{3,2,1,0:T(8,128)(2,1)S(1)}, bf16[64,2,128,128]{3,2,1,0:T(8,128)(2,1)}, u32[]{:S(2)}) copy-start(bf16[64,2,128,128]{3,2,1,0:T(8,128)(2,1)} %value_ref.1) | copy-start | bytes 12582916
  9.1 7.9 %copy-start.8 = (s32[64]{0:T(128)S(1)}, s32[64]{0:T(128)}, u32[]{:S(2)}) copy-start(s32[64]{0:T(128)} %lengths_ref.1) | copy-start | bytes 772
  14.8 21.7 %collective-permute-start = (bf16[256,512]{1,0:T(8,128)(2,1)S(1)}, bf16[256,512]{1,0:T(8,128)(2,1)S(1)}, u32[]{:S(2)}, u32[]{:S(2)}) collective-permute-start(bf16[256,512]{1,0:T(8,128)(2,1)S(1)} %get-tuple-element.30), channel_id=1, source_target_pairs={{0,2},{1,3},{2,0},{3,1},{4,6},{5,7},{6,4},{7,5},{8,10},{9,11},{10,... | collective-permute-start | bytes 786440 | tf_op jit(solution)/shard_map/ppermute | solution.py:33
  16.5 14.8 %copy-start.3 = (bf16[32,16,2048]{2,1,0:T(8,128)(2,1)S(1)}, bf16[32,16,2048]{2,1,0:T(8,128)(2,1)}, u32[]{:S(2)}) copy-start(bf16[32,16,2048]{2,1,0:T(8,128)(2,1)} %param.15) | copy-start | bytes 6291460
  16.5 14.8 %copy-start.6 = (bf16[1040,128]{1,0:T(8,128)(2,1)S(1)}, bf16[1040,128]{1,0:T(8,128)(2,1)}, u32[]{:S(2)}) copy-start(bf16[1040,128]{1,0:T(8,128)(2,1)} %get-tuple-element.34.refs_0_) | copy-start | bytes 798724
  16.5 19.6 %copy-start.5 = (bf16[32,16,512]{2,1,0:T(8,128)(2,1)S(1)}, bf16[32,16,512]{2,1,0:T(8,128)(2,1)}, u32[]{:S(2)}) copy-start(bf16[32,16,512]{2,1,0:T(8,128)(2,1)} %param.16) | copy-start | bytes 1572868
  16.5 20.0 %copy-start.9 = (f32[256,512]{1,0:T(8,128)S(1)}, f32[256,512]{1,0:T(8,128)}, u32[]{:S(2)}) copy-start(f32[256,512]{1,0:T(8,128)} %get-tuple-element.43) | copy-start | bytes 1572868
  16.5 20.0 %collective-permute-start.1 = (bf16[256,512]{1,0:T(8,128)(2,1)S(1)}, bf16[256,512]{1,0:T(8,128)(2,1)S(1)}, u32[]{:S(2)}, u32[]{:S(2)}) collective-permute-start(bf16[256,512]{1,0:T(8,128)(2,1)S(1)} %get-tuple-element.32), channel_id=1, source_target_pairs={{0,2},{1,3},{2,0},{3,1},{4,6},{5,7},{6,4},{7,5},{8,10},{9,11},{10,... | collective-permute-start | bytes 786440 | tf_op jit(solution)/shard_map/ppermute | solution.py:33
  21.8 24.0 %copy-start.4 = (f32[256,512]{1,0:T(8,128)S(1)}, f32[256,512]{1,0:T(8,128)}, u32[]{:S(2)}) copy-start(f32[256,512]{1,0:T(8,128)} %get-tuple-element.41.refs_0_) | copy-start | bytes 1572868
  21.8 24.0 %copy-start.7 = (bf16[64,64]{1,0:T(8,128)(2,1)S(1)}, bf16[64,64]{1,0:T(8,128)(2,1)}, u32[]{:S(2)}) copy-start(bf16[64,64]{1,0:T(8,128)(2,1)} %get-tuple-element.25.back_ref) | copy-start | bytes 24580
  32.1 3.3 %collective-permute-start.5 = (f32[16,256]{1,0:T(8,128)S(1)}, f32[16,256]{1,0:T(8,128)S(1)}, u32[]{:S(2)}, u32[]{:S(2)}) collective-permute-start(f32[16,256]{1,0:T(8,128)S(1)} %get-tuple-element.39.refs_0_), channel_id=1, source_target_pairs={{0,3},{1,2},{2,1},{3,0},{4,7},{5,6},{6,5},{7,4},{8,11},{9,10},{10,... | collective-permute-start | bytes 49160 | tf_op jit(solution)/shard_map/ppermute | solution.py:33
  32.4 3.7 %collective-permute-start.6 = (f32[16,256]{1,0:T(8,128)S(1)}, f32[16,256]{1,0:T(8,128)S(1)}, u32[]{:S(2)}, u32[]{:S(2)}) collective-permute-start(f32[16,256]{1,0:T(8,128)S(1)} %get-tuple-element.39.refs_0_), channel_id=1, source_target_pairs={{0,2},{1,3},{2,0},{3,1},{4,6},{5,7},{6,4},{7,5},{8,10},{9,11},{10,... | collective-permute-start | bytes 49160 | tf_op jit(solution)/shard_map/ppermute | solution.py:33
  33.7 2.4 %collective-permute-start.7 = (f32[16,256]{1,0:T(8,128)S(1)}, f32[16,256]{1,0:T(8,128)S(1)}, u32[]{:S(2)}, u32[]{:S(2)}) collective-permute-start(f32[16,256]{1,0:T(8,128)S(1)} %get-tuple-element.39.refs_0_), channel_id=1, source_target_pairs={{0,1},{1,0},{2,3},{3,2},{4,5},{5,4},{6,7},{7,6},{8,9},{9,8},{10,11... | collective-permute-start | bytes 49160 | tf_op jit(solution)/shard_map/ppermute | solution.py:33
  36.6 9.2 %collective-permute-start.8 = (bf16[256,512]{1,0:T(8,128)(2,1)S(1)}, bf16[256,512]{1,0:T(8,128)(2,1)S(1)}, u32[]{:S(2)}, u32[]{:S(2)}) collective-permute-start(bf16[256,512]{1,0:T(8,128)(2,1)S(1)} %add_convert_fusion), channel_id=1, source_target_pairs={{0,1},{1,0},{2,3},{3,2},{4,5},{5,4},{6,7},{7,6},{8,9},{9,8},{10,11... | collective-permute-start | bytes 786440 | tf_op jit(solution)/shard_map/ppermute | solution.py:33
  36.9 6.8 %collective-permute-start.10 = (bf16[64,512]{1,0:T(8,128)(2,1)S(1)}, bf16[64,512]{1,0:T(8,128)(2,1)S(1)}, u32[]{:S(2)}, u32[]{:S(2)}) collective-permute-start(bf16[64,512]{1,0:T(8,128)(2,1)S(1)} %get-tuple-element.46), channel_id=1, source_target_pairs={{0,12},{4,8},{8,4},{12,0},{1,13},{5,9},{9,5},{13,1},{2,14},{6,10},... | collective-permute-start | bytes 196616 | tf_op jit(solution)/shard_map/ppermute | solution.py:33
  39.3 6.5 %collective-permute-start.11 = (bf16[64,512]{1,0:T(8,128)(2,1)S(1)}, bf16[64,512]{1,0:T(8,128)(2,1)S(1)}, u32[]{:S(2)}, u32[]{:S(2)}) collective-permute-start(bf16[64,512]{1,0:T(8,128)(2,1)S(1)} %get-tuple-element.47), channel_id=1, source_target_pairs={{0,8},{4,12},{8,0},{12,4},{1,9},{5,13},{9,1},{13,5},{2,10},{6,14},... | collective-permute-start | bytes 196616 | tf_op jit(solution)/shard_map/ppermute | solution.py:33
  39.3 6.5 %collective-permute-start.9 = (bf16[64,512]{1,0:T(8,128)(2,1)S(1)}, bf16[64,512]{1,0:T(8,128)(2,1)S(1)}, u32[]{:S(2)}, u32[]{:S(2)}) collective-permute-start(bf16[64,512]{1,0:T(8,128)(2,1)S(1)} %get-tuple-element.45), channel_id=1, source_target_pairs={{0,4},{4,0},{8,12},{12,8},{1,5},{5,1},{9,13},{13,9},{2,6},{6,2},{1... | collective-permute-start | bytes 196616 | tf_op jit(solution)/shard_map/ppermute | solution.py:33

commit v9 on v8

--- a/solution.py
+++ b/solution.py
@@ -252,7 +252,11 @@
 
 
 def shrink_kernel(count, steps, cap, entries, rank, weight_ref, *refs):
-    blocks, out_ref, slot_ref = refs[:count], refs[count], refs[count + 1]
+    blocks, early, (out_ref, slot_ref) = refs[:count], refs[count:-2], refs[-2:]
+    before = early[0].shape[1] if early else 0
+    if early:
+        out_ref[:, :before] = early[0][...]
+        slot_ref[:, :before] = early[1][...]
     tiles = weight_ref.shape[1] // LANES
     rows = []
     for block in blocks:
@@ -262,16 +266,16 @@
     rows = jnp.concatenate(rows, axis=0)
     slots = [b[steps * tiles * cap :, :][:1, : steps * cap].astype(F32) for b in blocks]
     slots = jnp.concatenate(slots, axis=1).astype(jnp.int32)
-    slot_ref[...] = slots
+    slot_ref[:, before:] = slots
     every = lax.dot_general(weight_ref[...], rows, NT, preferred_element_type=F32)
     kept = jnp.where(slot_mask(entries, rank, slots), every, 0.0)
-    out_ref[...] = jnp.sum(kept.reshape(entries, rank, kept.shape[1]), axis=0)
-
-
-def shrink(weight, blocks, steps, cap):
+    out_ref[:, before:] = jnp.sum(kept.reshape(entries, rank, kept.shape[1]), axis=0)
+
+
+def shrink(weight, blocks, steps, cap, early=()):
     entries, rank, features = weight.shape
     count = len(blocks)
-    rows = count * steps * cap
+    rows = count * steps * cap + (early[0].shape[1] if early else 0)
     return pl.pallas_call(
         functools.partial(shrink_kernel, count, steps, cap, entries, rank),
         out_shape=[
@@ -283,7 +287,7 @@
             2 * entries * rank * features * rows, 2 * features * (entries * rank + rows)
         ),
         name="shrink",
-    )(weight.reshape(entries * rank, features), *blocks)
+    )(weight.reshape(entries * rank, features), *blocks, *early)
 
 
 def expand_kernel(groups, size, entries, rank, weight_ref, slot_ref, *refs):
@@ -476,7 +480,7 @@
     heads = cached_key_rows.shape[1]
 
     order = [0] + sorted(range(1, groups), reverse=True)
-    turns = [0, groups - 1] + list(range(1, groups - 1))
+    turns = [0] + list(reversed(range(1, groups)))
     *blocks, back = route(requests, adapter_store_row, hidden, order, cap, entries)
     over_dp = [swap("dp", groups, k) for k in order[1:]]
     over_tp = [swap("tp", size, k) for k in reversed(range(1, size))]
@@ -491,7 +495,9 @@
     mixed, lse = past(lengths, queries, cached_key_rows, cached_value_rows)
 
     block, _ = lax.optimization_barrier((blocks[0], lse))
-    shrunk, slots = shrink(adapter_shrink_weight, [block] + got, steps, cap)
+    half = groups // 2
+    early = shrink(adapter_shrink_weight, [block] + got[: half - 1], steps, cap)
+    shrunk, slots = shrink(adapter_shrink_weight, got[half - 1 :], steps, cap, early)
     partial = [shrunk] + [move(shrunk) for move in over_tp]
     deltas = expand(adapter_expand_weight, partial, slots, groups)
     returned = [deltas[0]] + [move(delta) for move, delta in zip(over_dp, deltas[1:])]

time: 48.1 us -> 48.2 us (level)
  starting transfers between devices: 14.5 us -> 13.5 us
  Pallas kernels: 16.4 us -> 17.2 us
    ppermute x12, starting transfers between devices: 14.5 us -> 13.5 us  [swap(): return lambda value: lax.ppermute(value, axis, pairs)]
    pallas_call x1 -> x2, Pallas kernels: 0.76 us -> 1.42 us  [shrink(): pl.pallas_call(functools.partial(shrink_kernel, count, steps, cap, entrie...]
  transfers between devices with their start and end apart: 12 -> 12, of which waited for: 5 -> 5; matrix products, arithmetic and copies ran while one was open for 0% -> 0% of each run, Pallas kernels for 24% -> 26%
where the time goes in v9:
time: 48.2 us; the launch traced here: 48 us
  Pallas kernels  17.2 us (36%)
  waiting for transfers between devices  16.4 us (34%)
  starting transfers between devices  13.5 us (28%)
  between operations  0.78 us (2%)
    ppermute x12, waiting for transfers between devices, swap(): return lambda value: lax.ppermute(value, axis, pairs)  16.4 us
    ppermute x12, starting transfers between devices, swap(): return lambda value: lax.ppermute(value, axis, pairs)  13.5 us
    pallas_call x1, Pallas kernels, base(): pl.pallas_call(functools.partial(base_kernel, size), out_shape=[jax.Shape...  5.74 us
    pallas_call x1, Pallas kernels, past(): pl.pallas_call(past_kernel, grid_spec=pltpu.PrefetchScalarGridSpec(num_sc...  4.76 us
    pallas_call x1, Pallas kernels, route(): pl.pallas_call(functools.partial(route_kernel, order, cap, entries), out_...  2.75 us
    pallas_call x1, Pallas kernels, finish(): pl.pallas_call(functools.partial(finish_kernel, turns, len(summands), cap...  2.14 us
    pallas_call x2, Pallas kernels, shrink(): pl.pallas_call(functools.partial(shrink_kernel, count, steps, cap, entrie...  1.42 us
  transfers between devices with their start and end apart: 12, of which 5 were waited for; matrix products, arithmetic and copies ran while one was open for 0% of the time, Pallas kernels for 26%

profile of v9, /device:TPU:0, one launch (start us, length us, event | category | flops | bytes accessed | tf_op | source)
XLA Modules:
  0.0 48.0 jit_solution(11481105965504946214)
XLA Ops:
  0.6 2.8 %route.1 = (bf16[1040,128]{1,0:T(8,128)(2,1)}, bf16[1040,128]{1,0:T(8,128)(2,1)}, bf16[1040,128]{1,0:T(8,128)(2,1)}, bf16[1040,128]{1,0:T(8,128)(2,1)}, bf16[64,64]{1,0:T(8,128)(2,1)}) custom-call(s32[1,64]{1,0:T(1,128)} %bitcast.9, s32[1,128]{1,0:T(1,128)} %bitcast.10, bf16[4,64,2048]{2,1,0:T(8,128)(2,1)} %hidden_hbm.1), custom_call_target="tpu_custom_call" | custom-call | flops 67108864 | bytes 2097152 | tf_op jit(solution)/shard_map/route/pallas_call | solution.py:102
  3.4 5.1 %collective-permute-start.4 = (bf16[1040,128]{1,0:T(8,128)(2,1)}, bf16[1040,128]{1,0:T(8,128)(2,1)S(1)}, u32[]{:S(2)}, u32[]{:S(2)}) collective-permute-start(bf16[1040,128]{1,0:T(8,128)(2,1)} %get-tuple-element.39), channel_id=1, source_target_pairs={{0,12},{4,8},{8,4},{12,0},{1,13},{5,9},{9,5},{13,1},{2,14},{6,10},... | collective-permute-start | bytes 798728 | tf_op jit(solution)/shard_map/ppermute | solution.py:33
  8.5 0.0 collective-permute-start.2
  8.5 0.6 %collective-permute-start.3 = (bf16[1040,128]{1,0:T(8,128)(2,1)}, bf16[1040,128]{1,0:T(8,128)(2,1)S(1)}, u32[]{:S(2)}, u32[]{:S(2)}) collective-permute-start(bf16[1040,128]{1,0:T(8,128)(2,1)} %get-tuple-element.36), channel_id=1, source_target_pairs={{0,4},{4,0},{8,12},{12,8},{1,5},{5,1},{9,13},{13,9},{2,6},{6,2},{1... | collective-permute-start | bytes 798728 | tf_op jit(solution)/shard_map/ppermute | solution.py:33
  9.1 0.0 copy-start.1
  9.1 0.0 copy-start.2
  9.1 0.0 copy-start.3
  9.1 0.0 copy-start.8
  9.1 5.7 %base.1 = (f32[256,512]{1,0:T(8,128)}, f32[256,512]{1,0:T(8,128)}, bf16[256,512]{1,0:T(8,128)(2,1)S(1)}, bf16[256,512]{1,0:T(8,128)(2,1)S(1)}) custom-call(bf16[256,2048]{1,0:T(8,128)(2,1)} %bitcast.8, bf16[2048,2048]{1,0:T(8,128)(2,1)} %projection_hbm.1), custom_call_target="tpu_custom_call" | custom-call | bytes 4096 | tf_op jit(solution)/shard_map/base/pallas_call | solution.py:148
  14.9 1.7 %collective-permute-start = (bf16[256,512]{1,0:T(8,128)(2,1)S(1)}, bf16[256,512]{1,0:T(8,128)(2,1)S(1)}, u32[]{:S(2)}, u32[]{:S(2)}) collective-permute-start(bf16[256,512]{1,0:T(8,128)(2,1)S(1)} %get-tuple-element.32), channel_id=1, source_target_pairs={{0,2},{1,3},{2,0},{3,1},{4,6},{5,7},{6,4},{7,5},{8,10},{9,11},{10,... | collective-permute-start | bytes 786440 | tf_op jit(solution)/shard_map/ppermute | solution.py:33
  16.6 0.0 copy-start
  16.6 0.0 copy-start.6
  16.6 0.4 collective-permute-start.1
  17.0 0.0 copy-done.1
  17.0 0.0 copy-done.2
  17.0 0.0 copy-done.3
  17.0 0.0 copy-done.8
  17.0 4.8 %past.1 = (f32[4,64,2048]{2,1,0:T(8,128)S(1)}, f32[64,128]{1,0:T(8,128)S(1)}) custom-call(s32[64]{0:T(128)S(1)} %copy-done.8, bf16[4,64,2048]{2,1,0:T(8,128)(2,1)S(1)} %copy-done.1, bf16[64,2,128,128]{3,2,1,0:T(8,128)(2,1)S(1)} %copy-done.2, bf16[64,2,128,128]{3,2,1,0:T(8,128)(2,1)S(1)} %copy-done.3), custom_call_target="tpu_custom_call" | custom-call | bytes 4096 | tf_op jit(solution)/shard_map/past/pallas_call | solution.py:225
  21.8 0.0 copy-start.5
  21.8 0.0 copy-start.9
  21.8 0.0 copy-start.4
  21.8 0.0 copy-start.7
  21.8 0.0 collective-permute-done.4.refs_1_
  21.8 0.0 copy-done
  21.8 0.0 copy-done.6
  21.9 0.7 %shrink.2 = (f32[16,128]{1,0:T(8,128)S(1)}, s32[1,128]{1,0:T(1,128)S(1)}) custom-call(bf16[512,2048]{1,0:T(8,128)(2,1)S(1)} %bitcast.5, bf16[1040,128]{1,0:T(8,128)(2,1)S(1)} %copy-done.6, bf16[1040,128]{1,0:T(8,128)(2,1)S(1)} %collective-permute-done.4.refs_1_), custom_call_target="tpu_custom_call" | custom-call | flops 268435456 | bytes 2621440 | tf_op jit(solution)/shard_map/shrink/pallas_call | solution.py:279
  22.6 8.8 %collective-permute-done.2.refs_0_ = bf16[1040,128]{1,0:T(8,128)(2,1)S(1)} collective-permute-done((bf16[1040,128]{1,0:T(8,128)(2,1)}, bf16[1040,128]{1,0:T(8,128)(2,1)S(1)}, u32[]{:S(2)}, u32[]{:S(2)}) %collective-permute-start.2) | collective-permute-done | bytes 266272 | tf_op jit(solution)/shard_map/ppermute | solution.py:33
  31.4 0.0 collective-permute-done.3.refs_1_
  31.4 0.7 %shrink.3 = (f32[16,256]{1,0:T(8,128)S(1)}, s32[1,256]{1,0:T(1,128)S(1)}) custom-call(bf16[512,2048]{1,0:T(8,128)(2,1)S(1)} %bitcast.6, bf16[1040,128]{1,0:T(8,128)(2,1)S(1)} %collective-permute-done.2.refs_0_, bf16[1040,128]{1,0:T(8,128)(2,1)S(1)} %collective-permute-done.3.refs_1_, f32[16,128]{1,0:T(8,128)S(1)} %get-tuple-element.40.refs_2_, ...), custom_call_target="tpu_custom_call" | custom-call | flops 536870912 | bytes 3145728 | tf_op jit(solution)/shard_map/shrink/pallas_call | solution.py:279
  32.1 0.3 collective-permute-start.5
  32.4 1.3 %collective-permute-start.6 = (f32[16,256]{1,0:T(8,128)S(1)}, f32[16,256]{1,0:T(8,128)S(1)}, u32[]{:S(2)}, u32[]{:S(2)}) collective-permute-start(f32[16,256]{1,0:T(8,128)S(1)} %get-tuple-element.43.refs_0_), channel_id=1, source_target_pairs={{0,2},{1,3},{2,0},{3,1},{4,6},{5,7},{6,4},{7,5},{8,10},{9,11},{10,... | collective-permute-start | bytes 49160 | tf_op jit(solution)/shard_map/ppermute | solution.py:33
  33.7 0.3 collective-permute-start.7
  34.0 1.4 %collective-permute-done.5.refs_1_ = f32[16,256]{1,0:T(8,128)S(1)} collective-permute-done((f32[16,256]{1,0:T(8,128)S(1)}, f32[16,256]{1,0:T(8,128)S(1)}, u32[]{:S(2)}, u32[]{:S(2)}) %collective-permute-start.5) | collective-permute-done | bytes 16416 | tf_op jit(solution)/shard_map/ppermute | solution.py:33
  35.4 0.7 %collective-permute-done.6.refs_2_ = f32[16,256]{1,0:T(8,128)S(1)} collective-permute-done((f32[16,256]{1,0:T(8,128)S(1)}, f32[16,256]{1,0:T(8,128)S(1)}, u32[]{:S(2)}, u32[]{:S(2)}) %collective-permute-start.6) | collective-permute-done | bytes 16416 | tf_op jit(solution)/shard_map/ppermute | solution.py:33
  36.2 0.0 collective-permute-done.7.refs_3_
  36.2 0.0 copy-done.5
  36.2 0.3 expand.1
  36.5 0.0 collective-permute-done.refs_1_
  36.5 0.0 collective-permute-done.1
  36.5 0.0 copy-done.9
  36.5 0.1 add_convert_fusion
  36.6 0.3 collective-permute-start.8
  36.9 0.0 collective-permute-start.10
  36.9 2.5 %collective-permute-start.11 = (bf16[64,512]{1,0:T(8,128)(2,1)S(1)}, bf16[64,512]{1,0:T(8,128)(2,1)S(1)}, u32[]{:S(2)}, u32[]{:S(2)}) collective-permute-start(bf16[64,512]{1,0:T(8,128)(2,1)S(1)} %get-tuple-element.51), channel_id=1, source_target_pairs={{0,12},{4,8},{8,4},{12,0},{1,13},{5,9},{9,5},{13,1},{2,14},{6,10},... | collective-permute-start | bytes 196616 | tf_op jit(solution)/shard_map/ppermute | solution.py:33
  39.3 1.0 %collective-permute-start.9 = (bf16[64,512]{1,0:T(8,128)(2,1)S(1)}, bf16[64,512]{1,0:T(8,128)(2,1)S(1)}, u32[]{:S(2)}, u32[]{:S(2)}) collective-permute-start(bf16[64,512]{1,0:T(8,128)(2,1)S(1)} %get-tuple-element.49), channel_id=1, source_target_pairs={{0,4},{4,0},{8,12},{12,8},{1,5},{5,1},{9,13},{13,9},{2,6},{6,2},{1... | collective-permute-start | bytes 196616 | tf_op jit(solution)/shard_map/ppermute | solution.py:33
  40.4 4.3 %collective-permute-done.10.refs_5_ = bf16[64,512]{1,0:T(8,128)(2,1)S(1)} collective-permute-done((bf16[64,512]{1,0:T(8,128)(2,1)S(1)}, bf16[64,512]{1,0:T(8,128)(2,1)S(1)}, u32[]{:S(2)}, u32[]{:S(2)}) %collective-permute-start.10) | collective-permute-done | bytes 65568 | tf_op jit(solution)/shard_map/ppermute | solution.py:33
  44.7 0.0 collective-permute-done.11.refs_6_
  44.7 1.2 %collective-permute-done.9.refs_4_ = bf16[64,512]{1,0:T(8,128)(2,1)S(1)} collective-permute-done((bf16[64,512]{1,0:T(8,128)(2,1)S(1)}, bf16[64,512]{1,0:T(8,128)(2,1)S(1)}, u32[]{:S(2)}, u32[]{:S(2)}) %collective-permute-start.9) | collective-permute-done | bytes 65568 | tf_op jit(solution)/shard_map/ppermute | solution.py:33
  45.8 0.0 collective-permute-done.8.refs_2_
  45.8 0.0 copy-done.4
  45.9 0.0 copy-done.7
  45.9 2.1 %finish.1 = (bf16[4,64,2048]{2,1,0:T(8,128)(2,1)}, bf16[4,64,512]{2,1,0:T(8,128)(2,1)}) custom-call(bf16[64,64]{1,0:T(8,128)(2,1)S(1)} %copy-done.7, bf16[4,64,2048]{2,1,0:T(8,128)(2,1)S(1)} %copy-done.1, f32[4,64,2048]{2,1,0:T(8,128)S(1)} %get-tuple-element.28.mixed_ref, f32[64,128]{1,0:T(8,128)S(1)} %get-tuple-element.29.lse_ref, ...), custom_call_target="tpu_custom_call" | custom-call | flops 1073741824 | bytes 5242880 | tf_op jit(solution)/shard_map/finish/pallas_call | solution.py:440
Async XLA Ops:
  3.4 18.4 %collective-permute-start.4 = (bf16[1040,128]{1,0:T(8,128)(2,1)}, bf16[1040,128]{1,0:T(8,128)(2,1)S(1)}, u32[]{:S(2)}, u32[]{:S(2)}) collective-permute-start(bf16[1040,128]{1,0:T(8,128)(2,1)} %get-tuple-element.39), channel_id=1, source_target_pairs={{0,12},{4,8},{8,4},{12,0},{1,13},{5,9},{9,5},{13,1},{2,14},{6,10},... | collective-permute-start | bytes 798728 | tf_op jit(solution)/shard_map/ppermute | solution.py:33
  8.5 22.9 %collective-permute-start.2 = (bf16[1040,128]{1,0:T(8,128)(2,1)}, bf16[1040,128]{1,0:T(8,128)(2,1)S(1)}, u32[]{:S(2)}, u32[]{:S(2)}) collective-permute-start(bf16[1040,128]{1,0:T(8,128)(2,1)} %get-tuple-element.35), channel_id=1, source_target_pairs={{0,8},{4,12},{8,0},{12,4},{1,9},{5,13},{9,1},{13,5},{2,10},{6,14},... | collective-permute-start | bytes 798728 | tf_op jit(solution)/shard_map/ppermute | solution.py:33
  8.5 22.9 %collective-permute-start.3 = (bf16[1040,128]{1,0:T(8,128)(2,1)}, bf16[1040,128]{1,0:T(8,128)(2,1)S(1)}, u32[]{:S(2)}, u32[]{:S(2)}) collective-permute-start(bf16[1040,128]{1,0:T(8,128)(2,1)} %get-tuple-element.36), channel_id=1, source_target_pairs={{0,4},{4,0},{8,12},{12,8},{1,5},{5,1},{9,13},{13,9},{2,6},{6,2},{1... | collective-permute-start | bytes 798728 | tf_op jit(solution)/shard_map/ppermute | solution.py:33
  9.1 7.9 %copy-start.1 = (bf16[4,64,2048]{2,1,0:T(8,128)(2,1)S(1)}, bf16[4,64,2048]{2,1,0:T(8,128)(2,1)}, u32[]{:S(2)}) copy-start(bf16[4,64,2048]{2,1,0:T(8,128)(2,1)} %query_ref.3) | copy-start | bytes 3145732
  9.1 7.9 %copy-start.2 = (bf16[64,2,128,128]{3,2,1,0:T(8,128)(2,1)S(1)}, bf16[64,2,128,128]{3,2,1,0:T(8,128)(2,1)}, u32[]{:S(2)}) copy-start(bf16[64,2,128,128]{3,2,1,0:T(8,128)(2,1)} %key_ref.1) | copy-start | bytes 12582916
  9.1 7.9 %copy-start.3 = (bf16[64,2,128,128]{3,2,1,0:T(8,128)(2,1)S(1)}, bf16[64,2,128,128]{3,2,1,0:T(8,128)(2,1)}, u32[]{:S(2)}) copy-start(bf16[64,2,128,128]{3,2,1,0:T(8,128)(2,1)} %value_ref.1) | copy-start | bytes 12582916
  9.1 7.9 %copy-start.8 = (s32[64]{0:T(128)S(1)}, s32[64]{0:T(128)}, u32[]{:S(2)}) copy-start(s32[64]{0:T(128)} %lengths_ref.1) | copy-start | bytes 772
  14.9 21.6 %collective-permute-start = (bf16[256,512]{1,0:T(8,128)(2,1)S(1)}, bf16[256,512]{1,0:T(8,128)(2,1)S(1)}, u32[]{:S(2)}, u32[]{:S(2)}) collective-permute-start(bf16[256,512]{1,0:T(8,128)(2,1)S(1)} %get-tuple-element.32), channel_id=1, source_target_pairs={{0,2},{1,3},{2,0},{3,1},{4,6},{5,7},{6,4},{7,5},{8,10},{9,11},{10,... | collective-permute-start | bytes 786440 | tf_op jit(solution)/shard_map/ppermute | solution.py:33
  16.6 5.2 %copy-start = (bf16[32,16,2048]{2,1,0:T(8,128)(2,1)S(1)}, bf16[32,16,2048]{2,1,0:T(8,128)(2,1)}, u32[]{:S(2)}) copy-start(bf16[32,16,2048]{2,1,0:T(8,128)(2,1)} %param.15) | copy-start | bytes 6291460
  16.6 5.2 %copy-start.6 = (bf16[1040,128]{1,0:T(8,128)(2,1)S(1)}, bf16[1040,128]{1,0:T(8,128)(2,1)}, u32[]{:S(2)}) copy-start(bf16[1040,128]{1,0:T(8,128)(2,1)} %get-tuple-element.38.refs_0_) | copy-start | bytes 798724
  16.6 19.9 %collective-permute-start.1 = (bf16[256,512]{1,0:T(8,128)(2,1)S(1)}, bf16[256,512]{1,0:T(8,128)(2,1)S(1)}, u32[]{:S(2)}, u32[]{:S(2)}) collective-permute-start(bf16[256,512]{1,0:T(8,128)(2,1)S(1)} %get-tuple-element.34), channel_id=1, source_target_pairs={{0,2},{1,3},{2,0},{3,1},{4,6},{5,7},{6,4},{7,5},{8,10},{9,11},{10,... | collective-permute-start | bytes 786440 | tf_op jit(solution)/shard_map/ppermute | solution.py:33
  21.8 14.4 %copy-start.5 = (bf16[32,16,512]{2,1,0:T(8,128)(2,1)S(1)}, bf16[32,16,512]{2,1,0:T(8,128)(2,1)}, u32[]{:S(2)}) copy-start(bf16[32,16,512]{2,1,0:T(8,128)(2,1)} %param.16) | copy-start | bytes 1572868
  21.8 14.7 %copy-start.9 = (f32[256,512]{1,0:T(8,128)S(1)}, f32[256,512]{1,0:T(8,128)}, u32[]{:S(2)}) copy-start(f32[256,512]{1,0:T(8,128)} %get-tuple-element.47) | copy-start | bytes 1572868
  21.8 24.1 %copy-start.4 = (f32[256,512]{1,0:T(8,128)S(1)}, f32[256,512]{1,0:T(8,128)}, u32[]{:S(2)}) copy-start(f32[256,512]{1,0:T(8,128)} %get-tuple-element.45.refs_0_) | copy-start | bytes 1572868
  21.8 24.0 %copy-start.7 = (bf16[64,64]{1,0:T(8,128)(2,1)S(1)}, bf16[64,64]{1,0:T(8,128)(2,1)}, u32[]{:S(2)}) copy-start(bf16[64,64]{1,0:T(8,128)(2,1)} %get-tuple-element.27.back_ref) | copy-start | bytes 24580
  32.1 3.3 %collective-permute-start.5 = (f32[16,256]{1,0:T(8,128)S(1)}, f32[16,256]{1,0:T(8,128)S(1)}, u32[]{:S(2)}, u32[]{:S(2)}) collective-permute-start(f32[16,256]{1,0:T(8,128)S(1)} %get-tuple-element.43.refs_0_), channel_id=1, source_target_pairs={{0,3},{1,2},{2,1},{3,0},{4,7},{5,6},{6,5},{7,4},{8,11},{9,10},{10,... | collective-permute-start | bytes 49160 | tf_op jit(solution)/shard_map/ppermute | solution.py:33
  32.4 3.7 %collective-permute-start.6 = (f32[16,256]{1,0:T(8,128)S(1)}, f32[16,256]{1,0:T(8,128)S(1)}, u32[]{:S(2)}, u32[]{:S(2)}) collective-permute-start(f32[16,256]{1,0:T(8,128)S(1)} %get-tuple-element.43.refs_0_), channel_id=1, source_target_pairs={{0,2},{1,3},{2,0},{3,1},{4,6},{5,7},{6,4},{7,5},{8,10},{9,11},{10,... | collective-permute-start | bytes 49160 | tf_op jit(solution)/shard_map/ppermute | solution.py:33
  33.7 2.4 %collective-permute-start.7 = (f32[16,256]{1,0:T(8,128)S(1)}, f32[16,256]{1,0:T(8,128)S(1)}, u32[]{:S(2)}, u32[]{:S(2)}) collective-permute-start(f32[16,256]{1,0:T(8,128)S(1)} %get-tuple-element.43.refs_0_), channel_id=1, source_target_pairs={{0,1},{1,0},{2,3},{3,2},{4,5},{5,4},{6,7},{7,6},{8,9},{9,8},{10,11... | collective-permute-start | bytes 49160 | tf_op jit(solution)/shard_map/ppermute | solution.py:33
  36.6 9.2 %collective-permute-start.8 = (bf16[256,512]{1,0:T(8,128)(2,1)S(1)}, bf16[256,512]{1,0:T(8,128)(2,1)S(1)}, u32[]{:S(2)}, u32[]{:S(2)}) collective-permute-start(bf16[256,512]{1,0:T(8,128)(2,1)S(1)} %add_convert_fusion), channel_id=1, source_target_pairs={{0,1},{1,0},{2,3},{3,2},{4,5},{5,4},{6,7},{7,6},{8,9},{9,8},{10,11... | collective-permute-start | bytes 786440 | tf_op jit(solution)/shard_map/ppermute | solution.py:33
  36.9 7.8 %collective-permute-start.10 = (bf16[64,512]{1,0:T(8,128)(2,1)S(1)}, bf16[64,512]{1,0:T(8,128)(2,1)S(1)}, u32[]{:S(2)}, u32[]{:S(2)}) collective-permute-start(bf16[64,512]{1,0:T(8,128)(2,1)S(1)} %get-tuple-element.50), channel_id=1, source_target_pairs={{0,8},{4,12},{8,0},{12,4},{1,9},{5,13},{9,1},{13,5},{2,10},{6,14},... | collective-permute-start | bytes 196616 | tf_op jit(solution)/shard_map/ppermute | solution.py:33
  36.9 7.8 %collective-permute-start.11 = (bf16[64,512]{1,0:T(8,128)(2,1)S(1)}, bf16[64,512]{1,0:T(8,128)(2,1)S(1)}, u32[]{:S(2)}, u32[]{:S(2)}) collective-permute-start(bf16[64,512]{1,0:T(8,128)(2,1)S(1)} %get-tuple-element.51), channel_id=1, source_target_pairs={{0,12},{4,8},{8,4},{12,0},{1,13},{5,9},{9,5},{13,1},{2,14},{6,10},... | collective-permute-start | bytes 196616 | tf_op jit(solution)/shard_map/ppermute | solution.py:33
  39.3 6.5 %collective-permute-start.9 = (bf16[64,512]{1,0:T(8,128)(2,1)S(1)}, bf16[64,512]{1,0:T(8,128)(2,1)S(1)}, u32[]{:S(2)}, u32[]{:S(2)}) collective-permute-start(bf16[64,512]{1,0:T(8,128)(2,1)S(1)} %get-tuple-element.49), channel_id=1, source_target_pairs={{0,4},{4,0},{8,12},{12,8},{1,5},{5,1},{9,13},{13,9},{2,6},{6,2},{1... | collective-permute-start | bytes 196616 | tf_op jit(solution)/shard_map/ppermute | solution.py:33
